TPU v7x, 32 devices: a whole 2x2x4 slice. The times are simulated.
32 devices in a mesh: fsdp: 4 (over y, x), ctx: 8 (over z, core).
Axes of the slice: x: 2, y: 2, z: 4, core: 2. Of those that a mesh axis runs over, the one named last changes fastest.
Arguments:
- tokens: bfloat16 [4, 1024, 768], P('fsdp', 'ctx'), may hold values from -6 to 6
- cotangent: bfloat16 [4, 1024, 768], P('fsdp', 'ctx'), may hold values from -6 to 6
- encoder: bfloat16 [4, 512, 768], P('fsdp', 'ctx'), may hold values from -6 to 6
- expert_ids: int32 [4, 1024, 1], P('fsdp', 'ctx'), may hold values from 0 to 7
- block_order: int32 [16], replicated, may hold values from 0 to 15, as said below
- bucket_table: int32 [1024], replicated, may hold values from 0 to 31, as said below
- first_gain: bfloat16 [768], P('fsdp'), may hold values from 0.099609375 to 1.8984375
- second_gain: bfloat16 [768], P('fsdp'), may hold values from 0.099609375 to 1.8984375
- third_gain: bfloat16 [768], P('fsdp'), may hold values from 0.099609375 to 1.8984375
- position_bias: bfloat16 [32, 12], P('fsdp'), may hold values from -6 to 6
- query_weight: bfloat16 [768, 768], P('fsdp'), may hold values from -0.21875 to 0.21875
- key_weight: bfloat16 [768, 768], P('fsdp'), may hold values from -0.21875 to 0.21875
- value_weight: bfloat16 [768, 768], P('fsdp'), may hold values from -0.21875 to 0.21875
- out_weight: bfloat16 [768, 768], P('fsdp'), may hold values from -1.75 to 1.75
- cross_query: bfloat16 [768, 768], P('fsdp'), may hold values from -0.21875 to 0.21875
- cross_key: bfloat16 [768, 768], P('fsdp'), may hold values from -0.21875 to 0.21875
- cross_value: bfloat16 [768, 768], P('fsdp'), may hold values from -0.21875 to 0.21875
- cross_out: bfloat16 [768, 768], P('fsdp'), may hold values from -1.75 to 1.75
- router_weight: bfloat16 [768, 8], P('fsdp'), may hold values from -0.15625 to 0.15625
- expert_in: bfloat16 [8, 768, 3072], P('ctx', None, 'fsdp'), may hold values from -0.21875 to 0.21875
- expert_out: bfloat16 [8, 3072, 768], P('ctx', 'fsdp'), may hold values from -1.25 to 1.25
Outputs:
- mixed_out: bfloat16 [4, 1024, 768], P('fsdp', 'ctx')
- tokens_grad: float32 [4, 1024, 768], P('fsdp', 'ctx')
- grad_first_gain: float32 [768], P('fsdp')
- grad_second_gain: float32 [768], P('fsdp')
- grad_third_gain: float32 [768], P('fsdp')
- grad_position_bias: float32 [32, 12], P('fsdp')
- grad_query_weight: float32 [768, 768], P('fsdp')
- grad_key_weight: float32 [768, 768], P('fsdp')
- grad_value_weight: float32 [768, 768], P('fsdp')
- grad_out_weight: float32 [768, 768], P('fsdp')
- grad_cross_query: float32 [768, 768], P('fsdp')
- grad_cross_key: float32 [768, 768], P('fsdp')
- grad_cross_value: float32 [768, 768], P('fsdp')
- grad_cross_out: float32 [768, 768], P('fsdp')
- grad_router_weight: float32 [768, 8], P('fsdp')
- grad_expert_in: float32 [8, 768, 3072], P('ctx', None, 'fsdp')
- grad_expert_out: float32 [8, 3072, 768], P('ctx', 'fsdp')
Inputs may be any that keep to these rules, and one draw needn't show every extreme that they name: `block_order`: entries 2c and 2c + 1 are k and 15 - k for some k; every value appears once. `bucket_table`: entry d is d for d < 16 and never falls as d grows; every distance from 128 on has bucket 32 - 1.
All inputs are finite; a program needn't handle non-finite values.
Results may differ from a plain program's by a relative error of at most 0.024.
Values may be sent and summed in bfloat16 or wider, within the bound.
No kernel may reach another device: no remote copies, remote signals or barrier semaphores. Data moves between devices by JAX's collectives and lax.ppermute only.
A program may use at most 256 MiB of HBM per device.

v0:
```python
import math
from functools import partial

import jax
import jax.numpy as jnp
from jax import lax
from jax.experimental import pallas as pl
from jax.experimental.pallas import tpu as pltpu
from jax.sharding import PartitionSpec as P

HEADS = 12
HEAD_DIM = 64
BUCKETS = 32
GROUP = 4
OWN_HEADS = HEADS // GROUP
EPSILON = 1e-06
MASKED = -1e30
LOW = jnp.bfloat16
WIDE = jnp.float32
VMEM_LIMIT = 56 * 1024 * 1024
NT = (((1,), (1,)), ((), ()))
TN = (((0,), (0,)), ((), ()))


def swap_fsdp(rows, k):
    size = lax.axis_size("fsdp")
    return lax.ppermute(rows, "fsdp", [(i, i ^ k) for i in range(size)])


def swap_core(rows):
    size = lax.axis_size("ctx")
    return lax.ppermute(rows, "ctx", [(i, i ^ 1) for i in range(size)])


def swap_group(rows, k):
    size = lax.axis_size("ctx")
    return lax.ppermute(rows, "ctx", [(i, i ^ (2 * k)) for i in range(size)])


def shift_rest(rows, r):
    size = lax.axis_size("ctx")
    step = 2 * GROUP * r
    return lax.ppermute(rows, "ctx", [(i, (i + step) % size) for i in range(size)])


def rest_count():
    return lax.axis_size("ctx") // (2 * GROUP)


def block_at(blocks, index):
    return lax.dynamic_index_in_dim(blocks, index, 0, keepdims=False)


def in_order(parts, index):
    parts = list(parts)
    bit = 1
    while bit < len(parts):
        flag = (index & bit) != 0
        parts = [jnp.where(flag, parts[i ^ bit], parts[i]) for i in range(len(parts))]
        bit *= 2
    return parts


def tie(*values):
    return lax.optimization_barrier(values)


def after(value, *earlier):
    return tie(value, *earlier)[0]


def gather_group(rows):
    return [rows] + [swap_group(rows, k) for k in range(1, GROUP)]


def gather_fsdp(rows):
    return [rows] + [swap_fsdp(rows, k) for k in range(1, lax.axis_size("fsdp"))]


def sum_rest(values):
    size = lax.axis_size("ctx")
    if rest_count() == 1:
        return values
    near = 2 * GROUP
    groups = [list(range(i, size, near)) for i in range(near)]
    return lax.psum(values, "ctx", axis_index_groups=groups)


def takes(us):
    return pl.CostEstimate(flops=int(us * 1e9), bytes_accessed=int(us * 3.5e6), transcendentals=0)


def vmem(count):
    return [pl.BlockSpec(memory_space=pltpu.VMEM)] * count


def smem():
    return pl.BlockSpec(memory_space=pltpu.SMEM)


def pack_kernel(index_ref, small_ref, *refs):
    group, core = index_ref[0], index_ref[1]
    ins, (qkv_ref, early_ref, late_ref) = refs[:-3], refs[-3:]
    rows = early_ref.shape[1]
    own = qkv_ref.shape[1] // 3
    shard = 2 * rows
    for choice in range(GROUP):

        @pl.when(group == choice)
        def take():
            for which in range(3):
                qkv_ref[:shard, which * own : (which + 1) * own] = ins[which][
                    :, choice * own : (choice + 1) * own
                ]

    qkv_ref[shard:] = jnp.zeros((small_ref.shape[0], 3 * own), LOW)
    qkv_ref[shard:, :shard] = small_ref[...]
    here = pl.ds(pl.multiple_of(core * rows, 16), rows)
    early = early_ref.shape[0]
    for i in range(early):
        early_ref[i] = ins[3 + i][here]
    for i in range(late_ref.shape[0]):
        late_ref[i] = ins[3 + early + i][here]


def pack_weights(small, weights, early, group, core):
    shard, width = weights[0].shape
    own = width // GROUP
    late = len(weights) - 3 - early
    return pl.pallas_call(
        pack_kernel,
        out_shape=[
            jax.ShapeDtypeStruct((shard + small.shape[0], 3 * own), LOW),
            jax.ShapeDtypeStruct((early, shard // 2, width), LOW),
            jax.ShapeDtypeStruct((late, shard // 2, width), LOW),
        ],
        in_specs=[smem()] + vmem(1 + len(weights)),
        out_specs=vmem(3),
        compiler_params=pltpu.CompilerParams(vmem_limit_bytes=VMEM_LIMIT),
        cost_estimate=takes(3),
        name="pack_weights",
    )(jnp.stack([group, core]).astype(jnp.int32), small, *weights)


def place_qkv_kernel(index_ref, *refs):
    pieces, (out, small) = refs[:-2], refs[-2:]
    rows = out.shape[1]
    for k in range(len(pieces)):
        out[index_ref[k]] = pieces[k][:rows]
        small[index_ref[k]] = pieces[k][rows:, :rows]


def place_qkv(pieces, extra, f_index):
    count = len(pieces)
    rows, width = pieces[0].shape
    rows = rows - extra
    whole, small = pl.pallas_call(
        place_qkv_kernel,
        out_shape=[
            jax.ShapeDtypeStruct((count, rows, width), LOW),
            jax.ShapeDtypeStruct((count, extra, rows), LOW),
        ],
        in_specs=[smem()] + vmem(count),
        out_specs=vmem(2),
        compiler_params=pltpu.CompilerParams(vmem_limit_bytes=VMEM_LIMIT),
        cost_estimate=takes(2.3),
        name="place_qkv",
    )(jnp.stack([f_index ^ k for k in range(count)]).astype(jnp.int32), *pieces)
    return whole.reshape(count * rows, width), small


def stack_kernel(turned, index_ref, *refs):
    count = len(refs) - 1
    out = refs[-1]
    for item in range(out.shape[0]):
        for k in range(count):
            spot = index_ref[count + k] if item < turned else index_ref[k]
            out[item, spot] = refs[k][item]


def stack_pieces(pieces, turned, f_index, g_index):
    count = len(pieces)
    spots = [f_index ^ k for k in range(count)]
    indices = jnp.stack(spots + [g_index ^ spot for spot in spots]).astype(jnp.int32)
    number, rows, width = pieces[0].shape
    return pl.pallas_call(
        partial(stack_kernel, turned),
        out_shape=jax.ShapeDtypeStruct((number, count, rows, width), LOW),
        in_specs=[smem()] + vmem(count),
        out_specs=vmem(1)[0],
        compiler_params=pltpu.CompilerParams(vmem_limit_bytes=VMEM_LIMIT),
        cost_estimate=takes(2.7),
        name="stack_pieces",
    )(indices, *pieces)


def weave_kernel(index_ref, mine_ref, theirs_ref, *outs):
    core = index_ref[0]
    for item, out in enumerate(outs):
        for block in range(out.shape[0]):
            out[block, core] = mine_ref[item, block]
            out[block, 1 - core] = theirs_ref[item, block]


def weave_halves(mine, theirs, core):
    number, count, rows, width = mine.shape
    whole = pl.pallas_call(
        weave_kernel,
        out_shape=[jax.ShapeDtypeStruct((count, 2, rows, width), LOW)] * number,
        in_specs=[smem()] + vmem(2),
        out_specs=vmem(number),
        compiler_params=pltpu.CompilerParams(vmem_limit_bytes=VMEM_LIMIT),
        cost_estimate=takes(4),
        name="weave_halves",
    )(core.reshape(1).astype(jnp.int32), mine, theirs)
    return [one.reshape(count * 2 * rows, width) for one in whole]


def expert_kernel(*refs):
    count = (len(refs) - 3) // 2
    pieces, in_ref, out_ref = refs[:count], refs[count], refs[count + 1]
    answers, middle = refs[count + 2 : 2 * count + 2], refs[-1]
    rows, width = pieces[0].shape[0], pieces[0].shape[1] // 2
    hidden = in_ref.shape[1]
    scale = math.sqrt(2 / math.pi)
    for k in range(count):
        inner = dot(pieces[k][:, :width], in_ref[...])
        square = inner * inner
        bent = jnp.tanh(scale * (inner + 0.044715 * (inner * square)))
        activated = (0.5 * inner * (1.0 + bent)).astype(LOW)
        slope = 0.5 * (1.0 + bent) + 0.5 * inner * (1.0 - bent * bent) * (
            scale * (1.0 + 3 * 0.044715 * square)
        )
        inner_low = (dot_nt(pieces[k][:, width:], out_ref[...]) * slope).astype(LOW)
        answers[k][:, :width] = dot(activated, out_ref[...]).astype(LOW)
        answers[k][:, width:] = dot_nt(inner_low, in_ref[...]).astype(LOW)
        here = slice(k * rows, (k + 1) * rows)
        middle[here, :hidden] = activated
        middle[here, hidden:] = inner_low


def run_experts(pieces, expert_in, expert_out):
    count = len(pieces)
    width, hidden = expert_in.shape
    rows = pieces[0].shape[0]
    results = pl.pallas_call(
        expert_kernel,
        out_shape=[jax.ShapeDtypeStruct((rows, 2 * width), LOW)] * count
        + [jax.ShapeDtypeStruct((count * rows, 2 * hidden), LOW)],
        in_specs=vmem(count + 2),
        out_specs=vmem(count + 1),
        compiler_params=pltpu.CompilerParams(vmem_limit_bytes=VMEM_LIMIT),
        cost_estimate=takes(8.2),
        name="experts",
    )(*pieces, expert_in, expert_out)
    return list(results[:count]), results[count]


def expert_grads_kernel(*refs):
    pieces, (middle, in_ref, out_ref) = refs[:-3], refs[-3:]
    width, hidden = in_ref.shape
    rows = jnp.concatenate([piece[...] for piece in pieces])
    in_ref[...] = dot_tn(rows[:, :width], middle[:, hidden:])
    out_ref[...] = dot_tn(middle[:, :hidden], rows[:, width:])


def expert_grads(pieces, middle):
    width = pieces[0].shape[1] // 2
    hidden = middle.shape[1] // 2
    return pl.pallas_call(
        expert_grads_kernel,
        out_shape=[
            jax.ShapeDtypeStruct((width, hidden), WIDE),
            jax.ShapeDtypeStruct((hidden, width), WIDE),
        ],
        in_specs=vmem(1 + len(pieces)),
        out_specs=vmem(2),
        compiler_params=pltpu.CompilerParams(vmem_limit_bytes=VMEM_LIMIT),
        cost_estimate=takes(5.7),
        name="expert_grads",
    )(*pieces, middle)


def home_kernel(rests, *refs):
    pieces, outs = refs[: len(refs) - GROUP], refs[len(refs) - GROUP :]
    block = outs[0].shape[0] // rests
    for k, out in enumerate(outs):
        for r in range(rests):
            here = slice((r * GROUP + k) * block, (r * GROUP + k + 1) * block)
            out[r * block : (r + 1) * block] = sum_low(
                pieces[0][here], [piece[here] for piece in pieces[1:]]
            )


def sum_home(pieces, rests):
    rows, width = pieces[0].shape
    return pl.pallas_call(
        partial(home_kernel, rests),
        out_shape=[jax.ShapeDtypeStruct((rows // GROUP, width), LOW)] * GROUP,
        in_specs=vmem(len(pieces)),
        out_specs=vmem(GROUP),
        compiler_params=pltpu.CompilerParams(vmem_limit_bytes=VMEM_LIMIT),
        cost_estimate=takes(2.4),
        name="sum_home",
    )(*pieces)


def grads_kernel(turns, extra_rows, index_ref, *refs):
    f_index, core, turn = index_ref[0], index_ref[1], index_ref[2]
    ins, spread_ref, keep, send = refs[: 2 * len(turns)], refs[-3], refs[-2], refs[-1]
    size, _, half = keep.shape
    shard = ins[0].shape[1] // size
    for item, turned in enumerate(turns):
        rows_ref, grad_ref = ins[2 * item], ins[2 * item + 1]
        for out, side in ((keep, core), (send, 1 - core)):
            grad = grad_ref[:, pl.ds(pl.multiple_of(side * half, 128), half)]
            product = dot_tn(rows_ref[...], grad).astype(LOW)
            for block in range(size):
                spot = block ^ f_index ^ (turn if turned else 0)
                out[spot, item * shard : (item + 1) * shard] = product[
                    block * shard : (block + 1) * shard
                ]
    first = len(turns) * shard
    for block in range(size):
        spot = block ^ f_index
        piece = spread_ref[:, block * shard : (block + 1) * shard].astype(LOW)
        keep[spot, first:] = jnp.zeros((extra_rows, half), LOW)
        send[spot, first:] = jnp.zeros((extra_rows, half), LOW)
        keep[spot, first : first + spread_ref.shape[0], :shard] = piece


def weight_grads(turns, pairs, spread, extra_rows, f_index, core, turn, size):
    width = pairs[0][0].shape[1]
    rows = len(turns) * (width // size) + extra_rows
    shape = jax.ShapeDtypeStruct((size, rows, width // 2), LOW)
    flat = [array for pair in pairs for array in pair] + [spread]
    return pl.pallas_call(
        partial(grads_kernel, turns, extra_rows),
        out_shape=[shape, shape],
        in_specs=[smem()] + vmem(len(flat)),
        out_specs=vmem(2),
        compiler_params=pltpu.CompilerParams(vmem_limit_bytes=VMEM_LIMIT),
        cost_estimate=takes(7.5),
        name="weight_grads",
    )(jnp.stack([f_index, core, turn]).astype(jnp.int32), *flat)


def add_low(left, right):
    return (left.astype(WIDE) + right.astype(WIDE)).astype(LOW)


def sum_low(first, others):
    total = first.astype(WIDE)
    for other in others:
        total = total + other.astype(WIDE)
    return total.astype(LOW)


def add_kernel(keep_ref, received_ref, *outs):
    for k, out in enumerate(outs):
        out[...] = add_low(keep_ref[k], received_ref[k])


def add_pieces(keep, received):
    size = keep.shape[0]
    return pl.pallas_call(
        add_kernel,
        out_shape=[jax.ShapeDtypeStruct(keep.shape[1:], LOW)] * size,
        in_specs=vmem(2),
        out_specs=vmem(size),
        compiler_params=pltpu.CompilerParams(vmem_limit_bytes=VMEM_LIMIT),
        cost_estimate=takes(4),
        name="add_pieces",
    )(keep, received)


def quarter_kernel(index_ref, *refs):
    pieces, outs = refs[: len(refs) - GROUP], refs[len(refs) - GROUP :]
    rows = outs[0].shape[0]
    for k, out in enumerate(outs):
        here = pl.ds(pl.multiple_of(index_ref[k] * rows, 16), rows)
        out[...] = sum_low(pieces[0][here], [piece[here] for piece in pieces[1:]])


def sum_quarters(pieces, group):
    rows, width = pieces[0].shape
    return pl.pallas_call(
        quarter_kernel,
        out_shape=[jax.ShapeDtypeStruct((rows // GROUP, width), LOW)] * GROUP,
        in_specs=[smem()] + vmem(len(pieces)),
        out_specs=vmem(GROUP),
        compiler_params=pltpu.CompilerParams(vmem_limit_bytes=VMEM_LIMIT),
        cost_estimate=takes(3),
        name="sum_quarters",
    )(jnp.stack([group ^ k for k in range(GROUP)]).astype(jnp.int32), *pieces)


def collect_kernel(index_ref, *refs):
    pieces, out = refs[:-1], refs[-1]
    for k in range(len(pieces)):
        out[index_ref[k]] = pieces[k][...]


def collect(pieces, spots):
    rows = pieces[0]
    return pl.pallas_call(
        collect_kernel,
        out_shape=jax.ShapeDtypeStruct((GROUP,) + rows.shape, rows.dtype),
        in_specs=[smem()] + vmem(GROUP),
        out_specs=vmem(1)[0],
        cost_estimate=takes(2),
        name="collect",
    )(jnp.stack(spots).astype(jnp.int32), *pieces)


def row_sums(values):
    ones = jnp.ones((8, values.shape[1]), WIDE)
    sums = lax.dot_general(
        ones, values, NT, precision=lax.Precision.HIGHEST, preferred_element_type=WIDE
    )
    return sums[:1]


def finish_kernel(index_ref, mine_ref, theirs_ref, weight_ref, gain_ref, *outs):
    core = index_ref[0]
    half = mine_ref.shape[1]
    shard = outs[0].shape[0]
    wholes, (router_ref, third_ref, second_ref) = outs[:-3], outs[-3:]
    for number, out in enumerate(wholes):
        here = slice(number * shard, (number + 1) * shard)
        out[:, pl.ds(pl.multiple_of(core * half, 128), half)] = mine_ref[here].astype(WIDE)
        out[:, pl.ds(pl.multiple_of((1 - core) * half, 128), half)] = theirs_ref[here].astype(WIDE)
    second_ref[...] = row_sums(weight_ref[...].astype(WIDE) * wholes[1][...]) / gain_ref[
        ...
    ].astype(WIDE)
    here = slice(len(wholes) * shard, None)
    spread = mine_ref[here].astype(WIDE) + theirs_ref[here].astype(WIDE)
    experts = router_ref.shape[0]
    router_ref[...] = spread[:experts, :shard]
    third_ref[...] = spread[experts : experts + 1, :shard]


def finish_weights(mine, theirs, weight, gain, core, experts):
    shard, width = weight.shape
    shapes = [(shard, width)] * 5 + [(experts, shard)] + [(1, shard)] * 2
    results = pl.pallas_call(
        finish_kernel,
        out_shape=[jax.ShapeDtypeStruct(shape, WIDE) for shape in shapes],
        in_specs=[smem()] + vmem(4),
        out_specs=vmem(len(shapes)),
        compiler_params=pltpu.CompilerParams(vmem_limit_bytes=VMEM_LIMIT),
        cost_estimate=takes(3),
        name="finish_weights",
    )(core.reshape(1).astype(jnp.int32), mine, theirs, weight, gain[None])
    return list(results[:5]) + [results[5].T] + [one[0] for one in results[6:]]


def qkv_grads_kernel(index_ref, rows_ref, grad_ref, table_ref, keep, send):
    f_index, core = index_ref[0], index_ref[1]
    size = keep.shape[0]
    extra = 16
    rows = keep.shape[1] - extra
    product = dot_tn(rows_ref[...], grad_ref[...])
    buckets = table_ref.shape[0] // size
    for block in range(size):
        spot = block ^ f_index
        top = product[2 * block * rows : (2 * block + 1) * rows].astype(LOW)
        bottom = product[(2 * block + 1) * rows : (2 * block + 2) * rows].astype(LOW)
        keep[spot, :rows] = jnp.where(core == 0, top, bottom)
        send[spot, :rows] = jnp.where(core == 0, bottom, top)
        keep[spot, rows:] = jnp.zeros((extra, keep.shape[2]), LOW)
        send[spot, rows:] = jnp.zeros((extra, keep.shape[2]), LOW)
        keep[spot, rows : rows + buckets, : table_ref.shape[1]] = table_ref[
            block * buckets : (block + 1) * buckets
        ].astype(LOW)


def qkv_finish_kernel(index_ref, mine_ref, theirs_ref, *refs):
    core = index_ref[0]
    weights, gain_ref, outs, bias_ref, gain_out = refs[:3], refs[3], refs[4:7], refs[7], refs[8]
    own = mine_ref.shape[2] // 3
    rows = outs[0].shape[0] // 2
    product = None
    for which in range(3):
        for source, side in ((mine_ref, core), (theirs_ref, 1 - core)):
            whole = jnp.concatenate(
                [
                    source[g, :rows, which * own : (which + 1) * own].astype(WIDE)
                    for g in range(GROUP)
                ],
                axis=1,
            )
            outs[which][pl.ds(pl.multiple_of(side * rows, 8), rows)] = whole
        one = weights[which][...].astype(WIDE) * outs[which][...]
        product = one if product is None else product + one
    gain_out[...] = row_sums(product) / gain_ref[...].astype(WIDE)
    buckets = bias_ref.shape[0]
    for g in range(GROUP):
        table = mine_ref[g, rows:, :128].astype(WIDE) + theirs_ref[g, rows:, :128].astype(WIDE)
        bias_ref[:, g * OWN_HEADS : (g + 1) * OWN_HEADS] = table[:buckets, :OWN_HEADS]


def qkv_weight_grads(rows, grads, table, f_index, core, size):
    width = rows.shape[1]
    half_shard = width // size // 2
    extra = 16
    shape = jax.ShapeDtypeStruct((size, half_shard + extra, grads.shape[1]), LOW)
    return pl.pallas_call(
        qkv_grads_kernel,
        out_shape=[shape, shape],
        in_specs=[smem()] + vmem(3),
        out_specs=vmem(2),
        compiler_params=pltpu.CompilerParams(vmem_limit_bytes=VMEM_LIMIT),
        cost_estimate=takes(3.1),
        name="qkv_grads",
    )(jnp.stack([f_index, core]).astype(jnp.int32), rows, grads, table)


def finish_qkv(mine, theirs, weights, gain, core, bias_shape):
    shard, width = weights[0].shape
    shapes = [(shard, width)] * 3 + [bias_shape, (1, shard)]
    results = pl.pallas_call(
        qkv_finish_kernel,
        out_shape=[jax.ShapeDtypeStruct(shape, WIDE) for shape in shapes],
        in_specs=[smem()] + vmem(6),
        out_specs=vmem(len(shapes)),
        compiler_params=pltpu.CompilerParams(vmem_limit_bytes=VMEM_LIMIT),
        cost_estimate=takes(2.6),
        name="qkv_finish",
    )(core.reshape(1).astype(jnp.int32), mine, theirs, *weights, gain[None])
    return list(results[:4]) + [results[4][0]]


def head_lanes(head, width):
    first = head // 2 * 128
    return first, min(first + 128, width)


def only_head(rows, head):
    if rows.shape[-1] == HEAD_DIM:
        return rows
    lane = lax.broadcasted_iota(jnp.int32, rows.shape, rows.ndim - 1)
    return jnp.where(lane // HEAD_DIM == head % 2, rows, jnp.zeros_like(rows))


def bias_block(kind_ref, tile_ref, head, step, first_block, width):
    rows = []
    for half in range(2):
        columns = []
        for pair in range(width // 128):
            left = kind_ref[2 * step + half, first_block + 2 * pair]
            right = kind_ref[2 * step + half, first_block + 2 * pair + 1]
            columns.append(tile_ref[0, head, left] + tile_ref[1, head, right])
        rows.append(jnp.concatenate(columns, axis=1))
    return jnp.concatenate(rows, axis=0)


def chunk_scores(query_head, key_ref, lanes, first, width, head, step, kind_ref, tile_ref):
    keys = key_ref[pl.ds(first, width), lanes[0] : lanes[1]]
    scores = lax.dot_general(query_head, keys, NT, preferred_element_type=WIDE)
    if kind_ref is not None:
        scores = scores + bias_block(kind_ref, tile_ref, head, step, first // HEAD_DIM, width)
    return scores


def forward_body(step, kind_ref, tile_ref, query_ref, key_ref, value_ref, out_ref, log_ref):
    width = query_ref.shape[-1]
    key_count = key_ref.shape[0]
    chunk = math.gcd(key_count, 1024)
    rows = query_ref.shape[0]
    lane = lax.broadcasted_iota(jnp.int32, (rows, 128), 1)
    logs = jnp.zeros((rows, 128), WIDE)
    tile_out = None
    for head in range(width // HEAD_DIM):
        lanes = head_lanes(head, width)
        query_head = only_head(query_ref[:, lanes[0] : lanes[1]], head) * jnp.asarray(0.125, LOW)

        def one_chunk(index, running):
            top, total, mixed = running
            first = index * chunk
            scores = chunk_scores(
                query_head, key_ref, lanes, first, chunk, head, step, kind_ref, tile_ref
            )
            new_top = jnp.maximum(top, jnp.max(scores, axis=1, keepdims=True))
            weights = jnp.exp(scores - new_top)
            shrink = jnp.exp(top - new_top)
            total = total * shrink + jnp.sum(weights, axis=1, keepdims=True)
            values = value_ref[pl.ds(first, chunk), lanes[0] : lanes[1]]
            mixed = mixed * shrink + jnp.dot(
                weights.astype(LOW), values, preferred_element_type=WIDE
            )
            return new_top, total, mixed

        running = (
            jnp.full((rows, 1), -1e29, WIDE),
            jnp.zeros((rows, 1), WIDE),
            jnp.zeros((rows, lanes[1] - lanes[0]), WIDE),
        )
        if key_count == chunk:
            running = one_chunk(0, running)
        else:
            running = lax.fori_loop(0, key_count // chunk, one_chunk, running)
        top, total, mixed = running
        mixed = only_head(mixed / total, head)
        logs = jnp.where(lane == head, top + jnp.log(total), logs)
        tile_out = mixed if head % 2 == 0 else tile_out + mixed
        if head % 2 == 1 or head == width // HEAD_DIM - 1:
            out_ref[:, lanes[0] : lanes[1]] = tile_out.astype(LOW)
    log_ref[...] = logs


def backward_body(
    step, kind_ref, tile_ref, query_ref, up_ref, log_ref, key_ref, value_ref, dq_ref, dk_ref, dv_ref, sums
):
    width = query_ref.shape[-1]
    key_count = key_ref.shape[0]
    chunk = math.gcd(key_count, 1024)
    rows = query_ref.shape[0]
    tile_out = None
    for head in range(width // HEAD_DIM):
        lanes = head_lanes(head, width)
        query_head = only_head(query_ref[:, lanes[0] : lanes[1]], head) * jnp.asarray(0.125, LOW)
        up_head = only_head(up_ref[:, lanes[0] : lanes[1]], head)
        log_head = log_ref[:, head : head + 1]

        def probs_of(first):
            scores = chunk_scores(
                query_head, key_ref, lanes, first, chunk, head, step, kind_ref, tile_ref
            )
            probs = jnp.exp(scores - log_head)
            values = value_ref[pl.ds(first, chunk), lanes[0] : lanes[1]]
            prob_grad = lax.dot_general(up_head, values, NT, preferred_element_type=WIDE)
            return probs, prob_grad

        def finish(first, probs, prob_grad, delta):
            score_grad = probs * (prob_grad - delta)
            if sums is not None:
                for half in range(2):
                    for pair in range(chunk // 128):
                        block = first // HEAD_DIM + 2 * pair
                        left = kind_ref[2 * step + half, block]
                        right = kind_ref[2 * step + half, block + 1]
                        piece = score_grad[
                            half * HEAD_DIM : (half + 1) * HEAD_DIM, pair * 128 : (pair + 1) * 128
                        ]
                        sums[0, head, left] += piece
                        sums[1, head, right] += piece
            score_low = score_grad.astype(LOW)
            here = pl.ds(first, chunk)
            dk_ref[here, lanes[0] : lanes[1]] += lax.dot_general(
                score_low, query_head, TN, preferred_element_type=WIDE
            )
            dv_ref[here, lanes[0] : lanes[1]] += lax.dot_general(
                probs.astype(LOW), up_head, TN, preferred_element_type=WIDE
            )
            keys = key_ref[here, lanes[0] : lanes[1]]
            return jnp.dot(score_low, keys, preferred_element_type=WIDE)

        if key_count == chunk:
            probs, prob_grad = probs_of(0)
            delta = jnp.sum(probs * prob_grad, axis=1, keepdims=True)
            query_grad = finish(0, probs, prob_grad, delta)
        else:

            def add_delta(index, delta):
                probs, prob_grad = probs_of(index * chunk)
                return delta + jnp.sum(probs * prob_grad, axis=1, keepdims=True)

            delta = lax.fori_loop(0, key_count // chunk, add_delta, jnp.zeros((rows, 1), WIDE))

            def add_grad(index, total):
                probs, prob_grad = probs_of(index * chunk)
                return total + finish(index * chunk, probs, prob_grad, delta)

            query_grad = lax.fori_loop(
                0, key_count // chunk, add_grad, jnp.zeros((rows, lanes[1] - lanes[0]), WIDE)
            )
        query_grad = only_head(query_grad * 0.125, head)
        tile_out = query_grad if head % 2 == 0 else tile_out + query_grad
        if head % 2 == 1 or head == width // HEAD_DIM - 1:
            dq_ref[:, lanes[0] : lanes[1]] = tile_out.astype(LOW)


def load_keys(own_ref, rest_ref, key_ref, value_ref):
    own, width = own_ref.shape[0], key_ref.shape[1]
    key_ref[:own] = own_ref[:, :width]
    key_ref[own:] = rest_ref[:, :width]
    value_ref[:own] = own_ref[:, width:]
    value_ref[own:] = rest_ref[:, width:]


def self_forward_kernel(kind_ref, tile_ref, query_ref, own_ref, rest_ref, *refs):
    outs, log_ref, out_ref, key_ref, value_ref = refs[:-4], refs[-4], refs[-3], refs[-2], refs[-1]

    @pl.when(pl.program_id(0) == 0)
    def start():
        load_keys(own_ref, rest_ref, key_ref, value_ref)

    forward_body(
        pl.program_id(0), kind_ref, tile_ref, query_ref, key_ref, value_ref, out_ref, log_ref
    )
    for k in range(len(outs)):

        @pl.when(pl.program_id(0) == k)
        def store():
            outs[k][...] = out_ref[...]


def self_backward_kernel(first, last, kind_ref, tile_ref, query_ref, up_ref, log_ref, own_ref, rest_ref, *refs):
    if first > 0:
        dk_start, dv_start, sums_start = refs[:3]
        refs = refs[3:]
    dq_ref, outs, (key_ref, value_ref, dk_ref, dv_ref) = refs[0], refs[1:4], refs[4:]
    sums = outs[2]

    @pl.when(pl.program_id(0) == 0)
    def start():
        load_keys(own_ref, rest_ref, key_ref, value_ref)
        if first > 0:
            dk_ref[...] = dk_start[...]
            dv_ref[...] = dv_start[...]
            sums[...] = sums_start[...]
        else:
            dk_ref[...] = jnp.zeros_like(dk_ref)
            dv_ref[...] = jnp.zeros_like(dv_ref)
            sums[...] = jnp.zeros_like(sums)

    backward_body(
        first + pl.program_id(0),
        kind_ref,
        tile_ref,
        query_ref,
        up_ref,
        log_ref,
        key_ref,
        value_ref,
        dq_ref,
        dk_ref,
        dv_ref,
        sums,
    )

    @pl.when(pl.program_id(0) == pl.num_programs(0) - 1)
    def end():
        if last:
            own, width = own_ref.shape[0], key_ref.shape[1]
            for out, here in ((outs[0], slice(0, own)), (outs[1], slice(own, None))):
                out[:, :width] = dk_ref[here].astype(LOW)
                out[:, width:] = dv_ref[here].astype(LOW)
        else:
            outs[0][...] = dk_ref[...]
            outs[1][...] = dv_ref[...]


def cross_forward_kernel(query_ref, key_ref, value_ref, out_ref, log_ref):
    forward_body(0, None, None, query_ref, key_ref, value_ref, out_ref, log_ref)


def cross_backward_kernel(
    query_ref, up_ref, log_ref, key_ref, value_ref, dq_ref, dk_out, dv_out, dk_ref, dv_ref
):
    dk_ref[...] = jnp.zeros_like(dk_ref)
    dv_ref[...] = jnp.zeros_like(dv_ref)
    backward_body(
        0, None, None, query_ref, up_ref, log_ref, key_ref, value_ref, dq_ref, dk_ref, dv_ref, None
    )
    dk_out[...] = dk_ref[...].astype(LOW)
    dv_out[...] = dv_ref[...].astype(LOW)


def whole_block(shape):
    return pl.BlockSpec(shape, lambda *index: (0,) * len(shape))


def row_block(rows, width):
    return pl.BlockSpec((rows, width), lambda i, *rest: (i, 0))


def lane_block(rows):
    return pl.BlockSpec((rows, 128), lambda i, *rest: (0, i))


def self_forward(kinds, tiles, queries, own, rest):
    count, width = queries.shape
    rows = 2 * HEAD_DIM
    keys = own.shape[0] + rest.shape[0]
    return pl.pallas_call(
        self_forward_kernel,
        grid_spec=pltpu.PrefetchScalarGridSpec(
            num_scalar_prefetch=1,
            grid=(count // rows,),
            in_specs=[
                whole_block(tiles.shape),
                row_block(rows, width),
                whole_block(own.shape),
                whole_block(rest.shape),
            ],
            out_specs=[whole_block((rows, width))] * (count // rows) + [row_block(rows, 128)],
            scratch_shapes=[
                pltpu.VMEM((rows, width), LOW),
                pltpu.VMEM((keys, width), LOW),
                pltpu.VMEM((keys, width), LOW),
            ],
        ),
        out_shape=[jax.ShapeDtypeStruct((rows, width), LOW)] * (count // rows)
        + [jax.ShapeDtypeStruct((count, 128), WIDE)],
        compiler_params=pltpu.CompilerParams(vmem_limit_bytes=VMEM_LIMIT),
        cost_estimate=takes(8.5),
        name="self_forward",
    )(kinds, tiles, queries, own, rest)


def self_backward(first, last, kinds, tiles, queries, up_rows, logs, own, rest, start=()):
    count, width = queries.shape
    rows = 2 * HEAD_DIM
    done = last == count // rows
    keys = own.shape[0] + rest.shape[0]
    if done:
        shapes = [jax.ShapeDtypeStruct(own.shape, LOW), jax.ShapeDtypeStruct(rest.shape, LOW)]
    else:
        shapes = [jax.ShapeDtypeStruct((keys, width), WIDE)] * 2
    shapes.append(jax.ShapeDtypeStruct(tiles.shape, WIDE))

    def rows_at(lanes):
        return pl.BlockSpec((rows, lanes), lambda i, *refs: (first + i, 0))

    return pl.pallas_call(
        partial(self_backward_kernel, first, done),
        grid_spec=pltpu.PrefetchScalarGridSpec(
            num_scalar_prefetch=1,
            grid=(last - first,),
            in_specs=[
                whole_block(tiles.shape),
                rows_at(width),
                rows_at(width),
                rows_at(128),
                whole_block(own.shape),
                whole_block(rest.shape),
            ]
            + [whole_block(array.shape) for array in start],
            out_specs=[row_block(rows, width)] + [whole_block(shape.shape) for shape in shapes],
            scratch_shapes=[pltpu.VMEM((keys, width), LOW)] * 2
            + [pltpu.VMEM((keys, width), WIDE)] * 2,
        ),
        out_shape=[jax.ShapeDtypeStruct(((last - first) * rows, width), LOW)] + shapes,
        compiler_params=pltpu.CompilerParams(vmem_limit_bytes=VMEM_LIMIT),
        cost_estimate=takes(9),
        name="self_backward",
    )(kinds, tiles, queries, up_rows, logs, own, rest, *start)


def cross_forward(queries, keys, values):
    count, width = queries.shape
    key_count = keys.shape[0]
    return pl.pallas_call(
        cross_forward_kernel,
        grid=(width // 128,),
        in_specs=[lane_block(count), lane_block(key_count), lane_block(key_count)],
        out_specs=[lane_block(count), lane_block(count)],
        out_shape=[
            jax.ShapeDtypeStruct((count, width), LOW),
            jax.ShapeDtypeStruct((count, width), WIDE),
        ],
        compiler_params=pltpu.CompilerParams(vmem_limit_bytes=VMEM_LIMIT),
        cost_estimate=takes(6.6),
        name="cross_forward",
    )(queries, keys, values)


def cross_backward(queries, up_rows, logs, keys, values):
    count, width = queries.shape
    key_count = keys.shape[0]
    return pl.pallas_call(
        cross_backward_kernel,
        grid=(width // 128,),
        in_specs=[lane_block(count)] * 3 + [lane_block(key_count)] * 2,
        out_specs=[lane_block(count), lane_block(key_count), lane_block(key_count)],
        scratch_shapes=[pltpu.VMEM((key_count, 128), WIDE), pltpu.VMEM((key_count, 128), WIDE)],
        out_shape=[
            jax.ShapeDtypeStruct((count, width), LOW),
            jax.ShapeDtypeStruct(keys.shape, LOW),
            jax.ShapeDtypeStruct(keys.shape, LOW),
        ],
        compiler_params=pltpu.CompilerParams(vmem_limit_bytes=VMEM_LIMIT),
        cost_estimate=takes(8.2),
        name="cross_backward",
    )(queries, up_rows, logs, keys, values)


def tiles_kernel(bound_ref, bias_ref, out_ref):
    shape = (HEAD_DIM, 2 * HEAD_DIM)
    lane = lax.broadcasted_iota(jnp.int32, shape, 1)
    row = lax.broadcasted_iota(jnp.int32, shape, 0)
    left = lane < HEAD_DIM
    offset = row - lane % HEAD_DIM
    for head in range(OWN_HEADS):
        far = jnp.full(shape, bias_ref[BUCKETS - 1, head], WIDE)
        tiles = [jnp.full(shape, MASKED, WIDE)]
        for apart in range(3):
            tile = tiles[0]
            for bucket in range(BUCKETS):
                reached = offset + apart * HEAD_DIM >= bound_ref[bucket]
                tile = jnp.where(reached, bias_ref[bucket, head], tile)
            tiles.append(tile)
        for kind, tile in enumerate(tiles + [far]):
            out_ref[0, head, kind] = jnp.where(left, tile, 0.0)
            out_ref[1, head, kind] = jnp.where(left, 0.0, tile)


def bias_tiles(lower_bounds, own_bias):
    shape = (2, OWN_HEADS, 5, HEAD_DIM, 2 * HEAD_DIM)
    return pl.pallas_call(
        tiles_kernel,
        out_shape=jax.ShapeDtypeStruct(shape, WIDE),
        in_specs=[pl.BlockSpec(memory_space=pltpu.SMEM)] * 2,
        out_specs=pl.BlockSpec(memory_space=pltpu.VMEM),
        cost_estimate=takes(2.7),
        name="bias_tiles",
    )(lower_bounds, own_bias)


def bucket_sums(sums, lower_bounds):
    tiles = sums[0, :, 1:, :, :HEAD_DIM] + sums[1, :, 1:, :, HEAD_DIM:]
    shape = (3, HEAD_DIM, HEAD_DIM, BUCKETS)
    distance = (
        lax.broadcasted_iota(jnp.int32, shape, 0) * HEAD_DIM
        + lax.broadcasted_iota(jnp.int32, shape, 1)
        - lax.broadcasted_iota(jnp.int32, shape, 2)
    )
    upper_bounds = jnp.concatenate([lower_bounds[1:], jnp.full((1,), 1 << 30, jnp.int32)])
    hot = ((distance >= lower_bounds) & (distance < upper_bounds)).astype(LOW)
    near = tiles[:, :3].reshape(OWN_HEADS, -1)
    high = near.astype(LOW)
    low = (near - high.astype(WIDE)).astype(LOW)
    both = jnp.dot(
        jnp.concatenate([high, low]), hot.reshape(-1, BUCKETS), preferred_element_type=WIDE
    )
    table = both[:OWN_HEADS] + both[OWN_HEADS:]
    far = jnp.sum(tiles[:, 3], axis=(1, 2))
    return table + jnp.where(jnp.arange(BUCKETS) == BUCKETS - 1, far[:, None], 0.0)


def rms_of(values):
    return lax.rsqrt(jnp.mean(values * values, axis=-1, keepdims=True) + EPSILON)


def norm_grad(values, inv_rms, gain, upstream):
    scaled = gain * upstream
    inner = jnp.mean(scaled * values, axis=-1, keepdims=True)
    return inv_rms * scaled - values * (inv_rms * inv_rms * inv_rms * inner)


def dot(left, right):
    return jnp.dot(left, right, preferred_element_type=WIDE)


def dot_nt(left, right):
    return lax.dot_general(left, right, NT, preferred_element_type=WIDE)


def dot_tn(left, right):
    return lax.dot_general(left, right, TN, preferred_element_type=WIDE)


def on_device(
    tokens,
    cotangent,
    encoder,
    expert_ids,
    block_order,
    bucket_table,
    first_gain,
    second_gain,
    third_gain,
    position_bias,
    query_weight,
    key_weight,
    value_weight,
    out_weight,
    cross_query,
    cross_key,
    cross_value,
    cross_out,
    router_weight,
    expert_in,
    expert_out,
):
    ctx_size = lax.axis_size("ctx")
    fsdp_size = lax.axis_size("fsdp")
    rests = rest_count()
    f_index = lax.axis_index("fsdp")
    ctx_index = lax.axis_index("ctx")
    core = ctx_index % 2
    group = (ctx_index // 2) % GROUP
    rest = ctx_index // (2 * GROUP)
    seq_count, span, width = tokens.shape
    shard = width // fsdp_size
    own_width = width // GROUP
    half_shard = shard // 2
    half_width = width // 2
    experts = expert_in.shape[0] * ctx_size
    capacity = (5 * seq_count * span + 4 * experts - 1) // (4 * experts)
    hidden_low = tokens.reshape(span, width)
    upstream = cotangent.reshape(span, width).astype(WIDE)

    small = jnp.concatenate(
        [
            first_gain[None],
            second_gain[None],
            third_gain[None],
            router_weight.T,
            jnp.pad(position_bias.reshape(1, -1), ((0, 0), (0, shard - position_bias.size))),
        ]
    )
    small = jnp.pad(small, ((0, -small.shape[0] % 16), (0, 0)))
    extra = small.shape[0]
    qkv_payload, early, late = pack_weights(
        small,
        (
            query_weight,
            key_weight,
            value_weight,
            out_weight,
            cross_key,
            cross_value,
            cross_query,
            cross_out,
        ),
        3,
        group,
        core,
    )
    first_hops = tie(*gather_group(hidden_low), *gather_fsdp(qkv_payload), early, late)
    own_rows = jnp.concatenate(first_hops[:GROUP])
    own_qkv, small_full = place_qkv(first_hops[GROUP : GROUP + fsdp_size], extra, f_index)
    early, late = first_hops[GROUP + fsdp_size :]
    early_x, early_y = swap_fsdp(early, 1), swap_fsdp(early, 2)
    expert_ids = after(expert_ids, qkv_payload)
    block_order, bucket_table, _ = tie(block_order, bucket_table, qkv_payload)

    gain_one = small_full[:, 0].reshape(width).astype(WIDE)
    gain_two = small_full[:, 1].reshape(width).astype(WIDE)
    gain_three = small_full[:, 2].reshape(width).astype(WIDE)
    router_full = small_full[:, 3 : 3 + experts].transpose(1, 0, 2).reshape(experts, width)
    bias_full = small_full[:, 3 + experts, : position_bias.size].reshape(BUCKETS, HEADS)

    slots = jnp.arange(GROUP, dtype=jnp.int32)
    key_devices = (
        ((rest - jnp.arange(rests, dtype=jnp.int32)) % rests)[:, None, None] * (2 * GROUP)
        + (group ^ slots)[None, None, :] * 2
        + (core ^ jnp.arange(2, dtype=jnp.int32))[None, :, None]
    ).reshape(-1)
    key_blocks = (key_devices[:, None] * 2 + jnp.arange(2, dtype=jnp.int32)[None]).reshape(-1)
    block_count = block_order.shape[0]
    hits = key_blocks[:, None] == jnp.arange(block_count, dtype=jnp.int32)[None]
    key_places = jnp.sum(jnp.where(hits, block_order[None], 0), axis=1)
    query_places = key_places[: 2 * GROUP]
    kinds = jnp.clip(query_places[:, None] - key_places[None], -1, 3) + 1
    lower_bounds = jnp.sum(
        (bucket_table[:, None] < jnp.arange(BUCKETS, dtype=jnp.int32)[None]).astype(jnp.int32),
        axis=0,
    )
    own_bias = lax.dynamic_slice_in_dim(
        bias_full.astype(WIDE), group * OWN_HEADS, OWN_HEADS, 1
    )
    tiles = bias_tiles(lower_bounds, own_bias)

    routes = expert_ids.reshape(-1)
    chosen = routes[:, None] == jnp.arange(experts, dtype=jnp.int32)[None]
    order = jnp.arange(span)
    lower = (order[:, None] > order[None]).astype(LOW)
    earlier = dot(lower, chosen.astype(LOW))
    slot_rank = jnp.sum(jnp.where(chosen, earlier, 0.0), axis=1).astype(jnp.int32)
    block_rows = -(-2 * capacity // 8) * 8
    slot_rows = rests * GROUP * block_rows
    target = (
        (((routes // (2 * GROUP) - rest) % rests) * GROUP + (((routes // 2) % GROUP) ^ group))
        * block_rows
        + core * capacity
        + slot_rank
    )
    code = jnp.where(slot_rank < capacity, (routes % 2) * slot_rows + target, -1)
    own_code = jnp.broadcast_to(code.astype(WIDE)[:, None], (span, 128))
    other_code = swap_core(own_code)
    codes = jnp.concatenate([own_code[:, :1], other_code[:, :1]]).astype(jnp.int32)
    placing = (
        codes == core * slot_rows + jnp.arange(slot_rows, dtype=jnp.int32)[None]
    ).astype(LOW)
    chosen = chosen.astype(WIDE)

    wide_rows = own_rows.astype(WIDE)
    normed_own = (wide_rows * rms_of(wide_rows) * gain_one).astype(LOW)
    own_count = GROUP * span
    queries = dot(normed_own, own_qkv[:, :own_width]).astype(LOW)
    pairs_own = dot(normed_own, own_qkv[:, own_width:]).astype(LOW)
    pairs_rest = swap_core(pairs_own)
    encoder_pieces = gather_group(after(encoder, early).reshape(-1, width))
    pairs_own, pairs_rest, early_x, early_y, *encoder_pieces = tie(
        pairs_own, pairs_rest, early_x, early_y, *encoder_pieces
    )
    early_xy = swap_fsdp(early_x, 2)
    late_x, late_y = swap_fsdp(late, 1), swap_fsdp(late, 2)
    if rests > 1:
        near = jnp.concatenate([pairs_own, pairs_rest])
        pairs_rest = jnp.concatenate(
            [pairs_rest] + [shift_rest(near, r) for r in range(1, rests)]
        )
    *attended_own, self_logs = self_forward(kinds, tiles, queries, pairs_own, pairs_rest)
    *attended_own, early_xy, late_x = tie(*attended_own, early_xy, late_x)
    attended = [attended_own[0]] + [swap_group(attended_own[k], k) for k in range(1, GROUP)]
    late_xy = swap_fsdp(late_x, 2)
    early_mine = stack_pieces((early, early_x, early_y, early_xy), 1, f_index, group)
    early_theirs = swap_core(early_mine)
    encoder_own = jnp.concatenate(encoder_pieces)
    encoder_other = swap_core(encoder_own)
    *attended, early_theirs, encoder_other, late_y = tie(
        *attended, early_theirs, encoder_other, late_y
    )
    out_full, cross_k_full, cross_v_full = weave_halves(early_mine, early_theirs, core)
    encoder_all = jnp.concatenate([encoder_own, encoder_other])
    if rests > 1:
        encoder_all = jnp.concatenate(
            [encoder_all] + [shift_rest(encoder_all, r) for r in range(1, rests)]
        )
    attended = jnp.concatenate(attended, axis=1)
    hidden = hidden_low.astype(WIDE)
    first_sum = hidden + dot(attended, out_full)
    inv_two = rms_of(first_sum)
    normed_two = (first_sum * inv_two * gain_two).astype(LOW)
    normed_two, late_xy = tie(normed_two, late_xy)
    late_mine = stack_pieces((late, late_x, late_y, late_xy), 0, f_index, group)
    late_theirs = swap_core(late_mine)

    cross_keys = dot(after(encoder_all, late_mine), cross_k_full).astype(LOW)
    cross_values = dot(encoder_all, cross_v_full).astype(LOW)
    cross_q_full, cross_o_full = weave_halves(late_mine, late_theirs, core)
    cross_rows = dot(normed_two, cross_q_full).astype(LOW)
    cross_mixed, cross_logs = cross_forward(cross_rows, cross_keys, cross_values)
    second_sum = first_sum + dot(cross_mixed, cross_o_full)
    inv_three = rms_of(second_sum)
    normed_three = (second_sum * inv_three * gain_three).astype(LOW)

    logits = dot_nt(normed_three, router_full)
    router_probs = jax.nn.softmax(logits, axis=-1)
    gate_value = jnp.sum(router_probs * chosen, axis=-1, keepdims=True)
    scaled_up = (gate_value * upstream).astype(LOW)

    sides = jnp.concatenate([normed_three, scaled_up], axis=1)
    sides = jnp.concatenate([sides, swap_core(sides)])
    sent = dot_tn(placing, sides).astype(LOW).reshape(rests, GROUP * block_rows, 2 * width)
    near = jnp.concatenate(
        [sent[0]] + [shift_rest(sent[r], r) for r in range(1, rests)]
    ).reshape(rests, GROUP, block_rows, 2 * width)
    arrived = jnp.concatenate(
        [near[:, 0]] + [swap_group(near[:, k], k) for k in range(1, GROUP)], axis=1
    ).reshape(slot_rows, 2 * width)
    arrivals = tie(*gather_fsdp(arrived))
    answers, middle = run_experts(arrivals, expert_in[0], expert_out[0])
    answers = tie(answers[0], *[swap_fsdp(answers[k], k) for k in range(1, fsdp_size)])
    answers = sum_home(answers, rests)
    near = [answers[0]] + [swap_group(answers[k], k) for k in range(1, GROUP)]
    near = jnp.concatenate(
        [piece.reshape(rests, block_rows, 2 * width) for piece in near], axis=1
    )
    home = jnp.concatenate([near[0]] + [shift_rest(near[r], -r) for r in range(1, rests)])
    both = dot(placing, home).astype(LOW)
    both = both[:span].astype(WIDE) + swap_core(both[span:]).astype(WIDE)
    moe_rows, dispatch_grad = both[:, :width], both[:, width:]
    grad_expert_in, grad_expert_out = expert_grads(arrivals, middle)
    grad_expert_in, grad_expert_out = grad_expert_in[None], grad_expert_out[None]

    mixed_out = (second_sum + gate_value * moe_rows).astype(LOW).reshape(tokens.shape)
    gate_grad = jnp.sum(upstream * moe_rows, axis=-1, keepdims=True)
    logit_low = (gate_grad * gate_value * (chosen - router_probs)).astype(LOW)
    three_grad = dispatch_grad + dot(logit_low, router_full)
    second_grad = upstream + norm_grad(second_sum, inv_three, gain_three, three_grad)
    gain_three_part = jnp.sum(three_grad * second_sum * inv_three, axis=0, keepdims=True)
    router_part = dot_tn(logit_low, normed_three)
    spread = jnp.concatenate([router_part, gain_three_part])
    spread = jnp.pad(spread, ((0, -spread.shape[0] % 16), (0, 0)))

    branch_two = second_grad.astype(LOW)
    cross_up = dot_nt(branch_two, cross_o_full).astype(LOW)
    cross_q_low, cross_k_part, cross_v_part = cross_backward(
        cross_rows, cross_up, cross_logs, cross_keys, cross_values
    )
    two_grad = dot_nt(cross_q_low, cross_q_full)
    first_grad = second_grad + norm_grad(first_sum, inv_two, gain_two, two_grad)

    branch_one = first_grad.astype(LOW)
    self_up = dot_nt(branch_one, out_full).astype(LOW)
    branch_one, self_up = tie(branch_one, self_up)
    up_pieces = [self_up[:, :own_width]] + [
        swap_group(self_up[:, k * own_width : (k + 1) * own_width], k) for k in range(1, GROUP)
    ]
    extra_rows = -(-spread.shape[0] // 64) * 64
    keep, send = weight_grads(
        (False, False, False, False, True),
        (
            (cross_mixed, branch_two),
            (normed_two, cross_q_low),
            (encoder_all, cross_k_part),
            (encoder_all, cross_v_part),
            (attended, branch_one),
        ),
        spread,
        extra_rows,
        f_index,
        core,
        group,
        fsdp_size,
    )
    *up_pieces, received = tie(*up_pieces, swap_core(send))
    up_own = jnp.concatenate(up_pieces)
    parts = [add_low(keep[k], received[k]) for k in range(fsdp_size)]
    up_own, *parts[1:] = tie(up_own, *parts[1:])
    parts = [parts[0]] + [swap_fsdp(parts[k], k) for k in range(1, fsdp_size)]
    query_low, pair_own, pair_rest, bias_parts = self_backward(
        0, own_count // span, kinds, tiles, queries, up_own, self_logs, pairs_own, pairs_rest
    )
    query_low, pair_own, pair_rest, bias_parts, parts[1], parts[2] = tie(
        query_low, pair_own, pair_rest, bias_parts, parts[1], parts[2]
    )
    if rests > 1:
        near = jnp.concatenate([pair_own, pair_rest[:own_count]]).astype(WIDE)
        for r in range(1, rests):
            first = (2 * r - 1) * own_count
            piece = pair_rest[first : first + 2 * own_count]
            near = near + shift_rest(piece, -r).astype(WIDE)
        pair_own, pair_rest = near[:own_count].astype(LOW), near[own_count:].astype(LOW)
    pair_low = add_low(pair_own, swap_core(pair_rest))
    qkv_low = jnp.concatenate([query_low, pair_low], axis=1)
    one_part = dot_nt(qkv_low, own_qkv).astype(LOW)
    one_parts = one_part.reshape(GROUP, span, width)
    one_parts = [one_parts[0]] + [swap_group(one_parts[k], k) for k in range(1, GROUP)]

    table = jnp.pad(bucket_sums(bias_parts, lower_bounds).T, ((0, 0), (0, 128 - OWN_HEADS)))
    qkv_keep, qkv_send = qkv_weight_grads(normed_own, qkv_low, table, f_index, core, fsdp_size)
    qkv_send, parts[3:] = tie(swap_core(qkv_send), parts[3:])
    qkv_parts = add_pieces(qkv_keep, qkv_send)
    qkv_parts = [qkv_parts[0]] + [swap_fsdp(qkv_parts[k], k) for k in range(1, fsdp_size)]
    qkv_shard = sum_rest(sum_low(qkv_parts[0], qkv_parts[1:])).astype(LOW)
    *one_parts, parts[0] = tie(*one_parts, parts[0])
    one_grad = sum(one.astype(WIDE) for one in one_parts)
    tokens_grad = first_grad + norm_grad(hidden, rms_of(hidden), gain_one, one_grad)
    tokens_grad = tokens_grad.reshape(tokens.shape)
    quarters = sum_quarters(parts, group)
    quarters = [quarters[0]] + [swap_group(quarters[k], k) for k in range(1, GROUP)]
    dense_shard = sum_rest(sum_low(quarters[0], quarters[1:])).astype(LOW)
    spots = [group ^ k for k in range(GROUP)]
    qkv_mine = collect(gather_group(qkv_shard), spots)
    query_total, key_total, value_total, bias_total, grad_gain_one = finish_qkv(
        qkv_mine,
        swap_core(qkv_mine),
        (query_weight, key_weight, value_weight),
        first_gain,
        core,
        position_bias.shape,
    )
    dense_mine = collect(gather_group(dense_shard), spots).reshape(-1, half_width)
    (
        cross_o_total,
        cross_q_total,
        cross_k_total,
        cross_v_total,
        out_total,
        grad_router,
        grad_gain_three,
        grad_gain_two,
    ) = finish_weights(dense_mine, swap_core(dense_mine), cross_query, second_gain, core, experts)

    return (
        mixed_out,
        tokens_grad,
        grad_gain_one,
        grad_gain_two,
        grad_gain_three,
        bias_total,
        query_total,
        key_total,
        value_total,
        out_total,
        cross_q_total,
        cross_k_total,
        cross_v_total,
        cross_o_total,
        grad_router,
        grad_expert_in,
        grad_expert_out,
    )


def solution(mesh):
    rows = P("fsdp", "ctx", None)
    vector = P("fsdp")
    matrix = P("fsdp", None)
    expert_specs = (P("ctx", None, "fsdp"), P("ctx", "fsdp", None))
    return jax.shard_map(
        on_device,
        mesh=mesh,
        in_specs=(rows,) * 4 + (P(),) * 2 + (vector,) * 3 + (matrix,) * 10 + expert_specs,
        out_specs=(rows,) * 2 + (vector,) * 3 + (matrix,) * 10 + expert_specs,
        check_vma=False,
    )
```

profile of v0, /device:TPU:13, one launch (start us, length us, event | category | flops | bytes accessed | tf_op | source)
XLA Modules:
  0.0 368.8 jit_solution(1075604182243272431)
XLA Ops:
  0.9 2.3 collective-permute-start.1
  8.0 2.8 pack_weights.1
  16.7 7.3 %collective-permute-done.2 = bf16[128,768]{1,0:T(8,128)(2,1)S(1)} collective-permute-done((bf16[128,768]{1,0:T(8,128)(2,1)S(1)}, bf16[128,768]{1,0:T(8,128)(2,1)S(1)}, u32[]{:S(2)}, u32[]{:S(2)}) %collective-permute-start.2) | collective-permute-done | bytes 196640 | tf_op jit(solution)/shard_map/ppermute | solution.py:37
  24.9 2.3 place_qkv.1
  32.2 3.8 %collective-permute-start.6 = (bf16[512,384]{1,0:T(8,128)(2,1)S(1)}, bf16[512,384]{1,0:T(8,128)(2,1)S(1)}, u32[]{:S(2)}, u32[]{:S(2)}) collective-permute-start(bf16[512,384]{1,0:T(8,128)(2,1)S(1)} %convolution_convert_fusion.5.own_ref), channel_id=1, source_target_pairs={{0,1},{1,0},{2,3},{3,2},{4,5},{5,4},{6,7},{7,6},{8,9},{9,8},{10,11... | collective-permute-start | bytes 1179656 | tf_op jit(solution)/shard_map/ppermute | solution.py:32
  38.2 2.3 collective-permute-done.9
  40.7 2.8 bias_tiles.1.tile_ref
  43.8 4.1 %collective-permute-done.11 = bf16[64,768]{1,0:T(8,128)(2,1)S(1)} collective-permute-done((bf16[64,768]{1,0:T(8,128)(2,1)S(1)}, bf16[64,768]{1,0:T(8,128)(2,1)S(1)}, u32[]{:S(2)}, u32[]{:S(2)}) %collective-permute-start.11) | collective-permute-done | bytes 98336 | tf_op jit(solution)/shard_map/ppermute | solution.py:37
  49.3 8.6 %self_forward.1 = (bf16[128,192]{1,0:T(8,128)(2,1)}, bf16[128,192]{1,0:T(8,128)(2,1)}, bf16[128,192]{1,0:T(8,128)(2,1)}, bf16[128,192]{1,0:T(8,128)(2,1)}, f32[512,128]{1,0:T(8,128)}) custom-call(s32[8,16]{1,0:T(8,128)} %clamp_add_fusion.kind_ref, f32[2,3,5,64,128]{4,3,2,1,0:T(8,128)} %bias_tiles.1.tile_ref, ...), custom_call_target="tpu_custom_call" | custom-call | flops 8499999744 | bytes 29750000 | tf_op jit(solution)/shard_map/self_forward/pallas_call | solution.py:787
  59.5 2.8 stack_pieces.2.mine_ref
  62.3 1.8 collective-permute-start.17
  66.1 1.8 collective-permute-start.15
  67.9 4.8 %collective-permute-done.19.refs_2_ = bf16[2,96,768]{2,1,0:T(8,128)(2,1)S(1)} collective-permute-done((bf16[2,96,768]{2,1,0:T(8,128)(2,1)S(1)}, bf16[2,96,768]{2,1,0:T(8,128)(2,1)S(1)}, u32[]{:S(2)}, u32[]{:S(2)}) %collective-permute-start.19) | collective-permute-done | bytes 294944 | tf_op jit(solution)/shard_map/ppermute | solution.py:27
  76.9 4.0 %weave_halves.2 = (bf16[4,2,96,768]{3,2,1,0:T(8,128)(2,1)}, bf16[4,2,96,768]{3,2,1,0:T(8,128)(2,1)}, bf16[4,2,96,768]{3,2,1,0:T(8,128)(2,1)}) custom-call(s32[1]{0:T(128)} %bitcast.2.index_ref, bf16[3,4,96,768]{3,2,1,0:T(8,128)(2,1)} %stack_pieces.2.mine_ref, bf16[3,4,96,768]{3,2,1,0:T(8,128)(2,1)} %collective-permute-done.17.theirs_ref), custom_call_target="tpu_custom_call" | custom-call | flops 4000000000 | bytes 14000000 | tf_op jit(solution)/shard_map/weave_halves/pallas_call | solution.py:207
  81.1 1.8 multiply_reduce_fusion.4
  84.3 2.3 stack_pieces.3.mine_ref
  89.2 1.8 convolution_convert_fusion.2.value_ref
  91.0 1.7 convolution_convert_fusion.3.key_ref
  93.6 3.1 weave_halves.3
  96.8 2.3 convolution_convert_fusion.9.query_ref
  99.1 6.6 %cross_forward.1 = (bf16[128,768]{1,0:T(8,128)(2,1)}, f32[128,768]{1,0:T(8,128)}) custom-call(bf16[128,768]{1,0:T(8,128)(2,1)} %convolution_convert_fusion.9.query_ref, bf16[512,768]{1,0:T(8,128)(2,1)} %convolution_convert_fusion.3.key_ref, bf16[512,768]{1,0:T(8,128)(2,1)} %convolution_convert_fusion.2.value_ref), custom_call_target="tpu_custom_call" | custom-call | flops 6600000000 | bytes 23100000 | tf_op jit(solution)/shard_map/cross_forward/pallas_call | solution.py:855
  107.7 1.7 collective-permute-done.23
  112.5 7.5 %collective-permute-done.26 = bf16[1,40,1536]{2,1,0:T(8,128)(2,1)S(1)} collective-permute-done((bf16[1,40,1536]{2,1,0:T(8,128)(2,1)S(1)}, bf16[1,40,1536]{2,1,0:T(8,128)(2,1)S(1)}, u32[]{:S(2)}, u32[]{:S(2)}) %collective-permute-start.26) | collective-permute-done | bytes 122912 | tf_op jit(solution)/shard_map/ppermute | solution.py:37
  120.0 1.6 collective-permute-done.25
  124.4 9.7 %collective-permute-done.27.refs_1_ = bf16[160,1536]{1,0:T(8,128)(2,1)S(1)} collective-permute-done((bf16[160,1536]{1,0:T(8,128)(2,1)S(1)}, bf16[160,1536]{1,0:T(8,128)(2,1)S(1)}, u32[]{:S(2)}, u32[]{:S(2)}) %collective-permute-start.27) | collective-permute-done | bytes 491552 | tf_op jit(solution)/shard_map/ppermute | solution.py:27
  134.1 11.4 %collective-permute-done.29.refs_3_ = bf16[160,1536]{1,0:T(8,128)(2,1)S(1)} collective-permute-done((bf16[160,1536]{1,0:T(8,128)(2,1)S(1)}, bf16[160,1536]{1,0:T(8,128)(2,1)S(1)}, u32[]{:S(2)}, u32[]{:S(2)}) %collective-permute-start.29) | collective-permute-done | bytes 491552 | tf_op jit(solution)/shard_map/ppermute | solution.py:27
  146.3 8.2 %experts.1 = (bf16[160,1536]{1,0:T(8,128)(2,1)}, bf16[160,1536]{1,0:T(8,128)(2,1)}, bf16[160,1536]{1,0:T(8,128)(2,1)}, bf16[160,1536]{1,0:T(8,128)(2,1)}, bf16[640,1536]{1,0:T(8,128)(2,1)}) custom-call(bf16[160,1536]{1,0:T(8,128)(2,1)} %copy-done.10, bf16[160,1536]{1,0:T(8,128)(2,1)} %copy-done.31, bf16[160,1536]{1,0:T(8,128)(2,1)} %copy-done.32, ...), custom_call_target="tpu_custom_call" | custom-call | flops 8200000000 | bytes 28700000 | tf_op jit(solution)/shard_map/experts/pallas_call | solution.py:246
  154.5 1.6 collective-permute-start.31
  157.2 8.9 %collective-permute-done.30.refs_1_ = bf16[160,1536]{1,0:T(8,128)(2,1)S(1)} collective-permute-done((bf16[160,1536]{1,0:T(8,128)(2,1)}, bf16[160,1536]{1,0:T(8,128)(2,1)S(1)}, u32[]{:S(2)}, u32[]{:S(2)}) %collective-permute-start.30) | collective-permute-done | bytes 491552 | tf_op jit(solution)/shard_map/ppermute | solution.py:27
  166.1 10.4 %collective-permute-done.32.refs_3_ = bf16[160,1536]{1,0:T(8,128)(2,1)S(1)} collective-permute-done((bf16[160,1536]{1,0:T(8,128)(2,1)}, bf16[160,1536]{1,0:T(8,128)(2,1)S(1)}, u32[]{:S(2)}, u32[]{:S(2)}) %collective-permute-start.32) | collective-permute-done | bytes 491552 | tf_op jit(solution)/shard_map/ppermute | solution.py:27
  177.3 2.4 sum_home.1
  179.6 3.3 collective-permute-start.34
  183.9 7.6 %collective-permute-done.34 = bf16[40,1536]{1,0:T(8,128)(2,1)S(1)} collective-permute-done((bf16[40,1536]{1,0:T(8,128)(2,1)}, bf16[40,1536]{1,0:T(8,128)(2,1)S(1)}, u32[]{:S(2)}, u32[]{:S(2)}) %collective-permute-start.34) | collective-permute-done | bytes 122912 | tf_op jit(solution)/shard_map/ppermute | solution.py:37
  192.9 2.3 collective-permute-start.36
  199.3 8.1 %cross_backward.1 = (bf16[128,768]{1,0:T(8,128)(2,1)}, bf16[512,768]{1,0:T(8,128)(2,1)}, bf16[512,768]{1,0:T(8,128)(2,1)}) custom-call(bf16[128,768]{1,0:T(8,128)(2,1)} %convolution_convert_fusion.9.query_ref, bf16[128,768]{1,0:T(8,128)(2,1)} %convolution_convert_fusion.8.up_ref, f32[128,768]{1,0:T(8,128)} %get-tuple-element.216.log_ref, ...), custom_call_target="tpu_custom_call" | custom-call | flops 8200000000 | bytes 28700000 | tf_op jit(solution)/shard_map/cross_backward/pallas_call | solution.py:873
  207.5 1.6 multiply_reduce_fusion.1
  211.6 7.6 %weight_grads.1 = (bf16[4,1024,384]{2,1,0:T(8,128)(2,1)}, bf16[4,1024,384]{2,1,0:T(8,128)(2,1)}) custom-call(s32[3]{0:T(128)} %pad_add_fusion.2.index_ref, bf16[128,768]{1,0:T(8,128)(2,1)} %get-tuple-element.197.refs_0_, bf16[128,768]{1,0:T(8,128)(2,1)} %copy-done.8, bf16[128,768]{1,0:T(8,128)(2,1)} %copy-done.7, ...), custom_call_target="tpu_custom_call" | custom-call | flops 7500000256 | bytes 26250000 | tf_op jit(solution)/shard_map/weight_grads/pallas_call | solution.py:337
  224.1 2.0 collective-permute-done.38
  226.1 3.7 %collective-permute-done.39 = bf16[128,192]{1,0:T(8,128)(2,1)S(1)} collective-permute-done((bf16[128,192]{1,0:T(8,128)(2,1)S(1)}, bf16[128,192]{1,0:T(8,128)(2,1)S(1)}, u32[]{:S(2)}, u32[]{:S(2)}) %collective-permute-start.39) | collective-permute-done | bytes 49184 | tf_op jit(solution)/shard_map/ppermute | solution.py:37
  229.8 4.4 %fusion.8 = (bf16[1024,384]{1,0:T(8,128)(2,1)}, bf16[1024,384]{1,0:T(8,128)(2,1)S(1)}, bf16[1024,384]{1,0:T(8,128)(2,1)S(1)}, bf16[1024,384]{1,0:T(8,128)(2,1)S(1)}) fusion(bf16[4,1024,384]{2,1,0:T(8,128)(2,1)} %collective-permute-done.40, bf16[4,1024,384]{2,1,0:T(8,128)(2,1)} %get-tuple-element.227), kind=kLoop, calls=%fused_computation.29 | loop fusion | flops 6291456 | bytes 9437184 | tf_op jit(solution)/shard_map/convert_element_type | solution.py:349
  237.6 12.6 %self_backward.1 = (bf16[512,192]{1,0:T(8,128)(2,1)}, bf16[512,384]{1,0:T(8,128)(2,1)}, bf16[512,384]{1,0:T(8,128)(2,1)}, f32[2,3,5,64,128]{4,3,2,1,0:T(8,128)}) custom-call(s32[8,16]{1,0:T(8,128)} %clamp_add_fusion.kind_ref, f32[2,3,5,64,128]{4,3,2,1,0:T(8,128)} %bias_tiles.1.tile_ref, bf16[512,192]{1,0:T(8,128)(2,1)} %convolution_convert_fusion.6.query_ref, ...), custom_call_target="tpu_custom_call" | custom-call | flops 8999999488 | bytes 31500000 | tf_op jit(solution)/shard_map/self_backward/pallas_call | solution.py:827
  250.2 3.0 collective-permute-done.41.refs_1_
  253.9 3.4 collective-permute-start.43
  261.5 3.2 qkv_grads.1
  266.0 15.3 %collective-permute-start.44 = (bf16[128,768]{1,0:T(8,128)(2,1)S(1)}, bf16[128,768]{1,0:T(8,128)(2,1)S(1)}, u32[]{:S(2)}, u32[]{:S(2)}) collective-permute-start(bf16[128,768]{1,0:T(8,128)(2,1)S(1)} %get-tuple-element.294), channel_id=1, source_target_pairs={{0,2},{1,3},{2,0},{3,1},{4,6},{5,7},{6,4},{7,5},{8,10},{9,11},{10,... | collective-permute-start | bytes 589832 | tf_op jit(solution)/shard_map/ppermute | solution.py:37
  281.2 2.5 collective-permute-start.45
  284.4 5.1 %collective-permute-done.44 = bf16[128,768]{1,0:T(8,128)(2,1)S(1)} collective-permute-done((bf16[128,768]{1,0:T(8,128)(2,1)S(1)}, bf16[128,768]{1,0:T(8,128)(2,1)S(1)}, u32[]{:S(2)}, u32[]{:S(2)}) %collective-permute-start.44) | collective-permute-done | bytes 196640 | tf_op jit(solution)/shard_map/ppermute | solution.py:37
  289.5 6.5 %collective-permute-done.45 = bf16[128,768]{1,0:T(8,128)(2,1)S(1)} collective-permute-done((bf16[128,768]{1,0:T(8,128)(2,1)S(1)}, bf16[128,768]{1,0:T(8,128)(2,1)S(1)}, u32[]{:S(2)}, u32[]{:S(2)}) %collective-permute-start.45) | collective-permute-done | bytes 196640 | tf_op jit(solution)/shard_map/ppermute | solution.py:37
  296.0 4.4 %collective-permute-done.46 = bf16[128,768]{1,0:T(8,128)(2,1)S(1)} collective-permute-done((bf16[128,768]{1,0:T(8,128)(2,1)S(1)}, bf16[128,768]{1,0:T(8,128)(2,1)S(1)}, u32[]{:S(2)}, u32[]{:S(2)}) %collective-permute-start.46) | collective-permute-done | bytes 196640 | tf_op jit(solution)/shard_map/ppermute | solution.py:37
  301.2 2.1 add_pieces.1
  303.3 2.4 collective-permute-start.51
  306.0 2.9 sum_quarters.1
  309.0 2.0 collective-permute-start.58
  313.0 3.0 collective-permute-start.53
  316.0 6.4 %collective-permute-done.58 = bf16[256,384]{1,0:T(8,128)(2,1)S(1)} collective-permute-done((bf16[256,384]{1,0:T(8,128)(2,1)}, bf16[256,384]{1,0:T(8,128)(2,1)S(1)}, u32[]{:S(2)}, u32[]{:S(2)}) %collective-permute-start.58) | collective-permute-done | bytes 196640 | tf_op jit(solution)/shard_map/ppermute | solution.py:37
  323.1 3.4 collective-permute-done.57
  327.5 4.1 %collective-permute-start.59 = (bf16[256,384]{1,0:T(8,128)(2,1)S(1)}, bf16[256,384]{1,0:T(8,128)(2,1)S(1)}, u32[]{:S(2)}, u32[]{:S(2)}) collective-permute-start(bf16[256,384]{1,0:T(8,128)(2,1)S(1)} %add_convert_fusion.5.refs_0_), channel_id=1, source_target_pairs={{0,2},{1,3},{2,0},{3,1},{4,6},{5,7},{6,4},{7,5},{8,10},{9,11},{10,... | collective-permute-start | bytes 589832 | tf_op jit(solution)/shard_map/ppermute | solution.py:37
  332.9 5.7 %expert_grads.1 = (f32[768,768]{1,0:T(8,128)}, f32[768,768]{1,0:T(8,128)}) custom-call(bf16[160,1536]{1,0:T(8,128)(2,1)} %copy-done.10, bf16[160,1536]{1,0:T(8,128)(2,1)} %copy-done.31, bf16[160,1536]{1,0:T(8,128)(2,1)} %copy-done.32, bf16[160,1536]{1,0:T(8,128)(2,1)} %copy-done.33, bf16[640,1536]{1,0:T(8,128)(2,1)} %get-tuple-element.274.refs_4_), custom_call_target="tpu_custom_call" | custom-call | flops 5699999744 | bytes 19950000 | tf_op jit(solution)/shard_map/expert_grads/pallas_call | solution.py:270
  338.7 8.6 %collective-permute-done.54.refs_3_ = bf16[112,576]{1,0:T(8,128)(2,1)S(1)} collective-permute-done((bf16[112,576]{1,0:T(8,128)(2,1)S(1)}, bf16[112,576]{1,0:T(8,128)(2,1)S(1)}, u32[]{:S(2)}, u32[]{:S(2)}) %collective-permute-start.54) | collective-permute-done | bytes 129056 | tf_op jit(solution)/shard_map/ppermute | solution.py:37
  348.0 2.0 collect.2.mine_ref
  351.5 4.2 %collective-permute-done.61.refs_3_ = bf16[256,384]{1,0:T(8,128)(2,1)S(1)} collective-permute-done((bf16[256,384]{1,0:T(8,128)(2,1)S(1)}, bf16[256,384]{1,0:T(8,128)(2,1)S(1)}, u32[]{:S(2)}, u32[]{:S(2)}) %collective-permute-start.61) | collective-permute-done | bytes 196640 | tf_op jit(solution)/shard_map/ppermute | solution.py:37
  356.4 2.2 collect.3
  361.6 2.9 qkv_finish.1
  365.4 3.4 finish_weights.1
  (324 shorter events, 81.0 us)
Async XLA Ops:
  0.7 15.3 %collective-permute-start = (bf16[128,768]{1,0:T(8,128)(2,1)}, bf16[128,768]{1,0:T(8,128)(2,1)S(1)}, u32[]{:S(2)}, u32[]{:S(2)}) collective-permute-start(bf16[128,768]{1,0:T(8,128)(2,1)} %bitcast.113), channel_id=1, source_target_pairs={{0,2},{1,3},{2,0},{3,1},{4,6},{5,7},{6,4},{7,5},{8,10},{9,11},{10,... | collective-permute-start | bytes 589832 | tf_op jit(solution)/shard_map/ppermute | solution.py:37
  0.9 15.9 %collective-permute-start.1 = (bf16[128,768]{1,0:T(8,128)(2,1)}, bf16[128,768]{1,0:T(8,128)(2,1)S(1)}, u32[]{:S(2)}, u32[]{:S(2)}) collective-permute-start(bf16[128,768]{1,0:T(8,128)(2,1)} %bitcast.114), channel_id=1, source_target_pairs={{0,4},{1,5},{2,6},{3,7},{4,0},{5,1},{6,2},{7,3},{8,12},{9,13},{10,... | collective-permute-start | bytes 589832 | tf_op jit(solution)/shard_map/ppermute | solution.py:37
  10.8 13.2 %collective-permute-start.3 = (bf16[208,576]{1,0:T(8,128)(2,1)}, bf16[208,576]{1,0:T(8,128)(2,1)S(1)}, u32[]{:S(2)}, u32[]{:S(2)}) collective-permute-start(bf16[208,576]{1,0:T(8,128)(2,1)} %get-tuple-element.152.refs_0_), channel_id=1, source_target_pairs={{0,8},{8,0},{16,24},{24,16},{1,9},{9,1},{17,25},{25,17},{2,10},{10... | collective-permute-start | bytes 718856 | tf_op jit(solution)/shard_map/ppermute | solution.py:27
  12.1 12.0 %collective-permute-start.4 = (bf16[208,576]{1,0:T(8,128)(2,1)}, bf16[208,576]{1,0:T(8,128)(2,1)S(1)}, u32[]{:S(2)}, u32[]{:S(2)}) collective-permute-start(bf16[208,576]{1,0:T(8,128)(2,1)} %get-tuple-element.152.refs_0_), channel_id=1, source_target_pairs={{0,16},{8,24},{16,0},{24,8},{1,17},{9,25},{17,1},{25,9},{2,18},{10... | collective-permute-start | bytes 718856 | tf_op jit(solution)/shard_map/ppermute | solution.py:27
  12.3 11.7 %collective-permute-start.5 = (bf16[208,576]{1,0:T(8,128)(2,1)}, bf16[208,576]{1,0:T(8,128)(2,1)S(1)}, u32[]{:S(2)}, u32[]{:S(2)}) collective-permute-start(bf16[208,576]{1,0:T(8,128)(2,1)} %get-tuple-element.152.refs_0_), channel_id=1, source_target_pairs={{0,24},{8,16},{16,8},{24,0},{1,25},{9,17},{17,9},{25,1},{2,26},{10... | collective-permute-start | bytes 718856 | tf_op jit(solution)/shard_map/ppermute | solution.py:27
  15.9 8.1 %collective-permute-start.2 = (bf16[128,768]{1,0:T(8,128)(2,1)S(1)}, bf16[128,768]{1,0:T(8,128)(2,1)S(1)}, u32[]{:S(2)}, u32[]{:S(2)}) collective-permute-start(bf16[128,768]{1,0:T(8,128)(2,1)S(1)} %bitcast.115), channel_id=1, source_target_pairs={{0,6},{1,7},{2,4},{3,5},{4,2},{5,3},{6,0},{7,1},{8,14},{9,15},{10,... | collective-permute-start | bytes 589832 | tf_op jit(solution)/shard_map/ppermute | solution.py:37
  30.5 17.4 %collective-permute-start.7 = (bf16[3,96,768]{2,1,0:T(8,128)(2,1)S(1)}, bf16[3,96,768]{2,1,0:T(8,128)(2,1)S(1)}, u32[]{:S(2)}, u32[]{:S(2)}) collective-permute-start(bf16[3,96,768]{2,1,0:T(8,128)(2,1)S(1)} %copy-done.37), channel_id=1, source_target_pairs={{0,8},{8,0},{16,24},{24,16},{1,9},{9,1},{17,25},{25,17},{2,10},{10... | collective-permute-start | bytes 1327112 | tf_op jit(solution)/shard_map/ppermute | solution.py:27
  31.8 16.1 %collective-permute-start.8 = (bf16[3,96,768]{2,1,0:T(8,128)(2,1)S(1)}, bf16[3,96,768]{2,1,0:T(8,128)(2,1)S(1)}, u32[]{:S(2)}, u32[]{:S(2)}) collective-permute-start(bf16[3,96,768]{2,1,0:T(8,128)(2,1)S(1)} %copy-done.37), channel_id=1, source_target_pairs={{0,16},{8,24},{16,0},{24,8},{1,17},{9,25},{17,1},{25,9},{2,18},{10... | collective-permute-start | bytes 1327112 | tf_op jit(solution)/shard_map/ppermute | solution.py:27
  32.2 15.7 %collective-permute-start.6 = (bf16[512,384]{1,0:T(8,128)(2,1)S(1)}, bf16[512,384]{1,0:T(8,128)(2,1)S(1)}, u32[]{:S(2)}, u32[]{:S(2)}) collective-permute-start(bf16[512,384]{1,0:T(8,128)(2,1)S(1)} %convolution_convert_fusion.5.own_ref), channel_id=1, source_target_pairs={{0,1},{1,0},{2,3},{3,2},{4,5},{5,4},{6,7},{7,6},{8,9},{9,8},{10,11... | collective-permute-start | bytes 1179656 | tf_op jit(solution)/shard_map/ppermute | solution.py:32
  36.1 4.5 %collective-permute-start.9 = (bf16[64,768]{1,0:T(8,128)(2,1)S(1)}, bf16[64,768]{1,0:T(8,128)(2,1)S(1)}, u32[]{:S(2)}, u32[]{:S(2)}) collective-permute-start(bf16[64,768]{1,0:T(8,128)(2,1)S(1)} %bitcast.125), channel_id=1, source_target_pairs={{0,2},{1,3},{2,0},{3,1},{4,6},{5,7},{6,4},{7,5},{8,10},{9,11},{10,... | collective-permute-start | bytes 294920 | tf_op jit(solution)/shard_map/ppermute | solution.py:37
  36.3 7.2 %collective-permute-start.10 = (bf16[64,768]{1,0:T(8,128)(2,1)S(1)}, bf16[64,768]{1,0:T(8,128)(2,1)S(1)}, u32[]{:S(2)}, u32[]{:S(2)}) collective-permute-start(bf16[64,768]{1,0:T(8,128)(2,1)S(1)} %bitcast.126), channel_id=1, source_target_pairs={{0,4},{1,5},{2,6},{3,7},{4,0},{5,1},{6,2},{7,3},{8,12},{9,13},{10,... | collective-permute-start | bytes 294920 | tf_op jit(solution)/shard_map/ppermute | solution.py:37
  40.6 7.4 %collective-permute-start.11 = (bf16[64,768]{1,0:T(8,128)(2,1)S(1)}, bf16[64,768]{1,0:T(8,128)(2,1)S(1)}, u32[]{:S(2)}, u32[]{:S(2)}) collective-permute-start(bf16[64,768]{1,0:T(8,128)(2,1)S(1)} %bitcast.127), channel_id=1, source_target_pairs={{0,6},{1,7},{2,4},{3,5},{4,2},{5,3},{6,0},{7,1},{8,14},{9,15},{10,... | collective-permute-start | bytes 294920 | tf_op jit(solution)/shard_map/ppermute | solution.py:37
  43.5 14.4 %collective-permute-start.13 = (bf16[2,96,768]{2,1,0:T(8,128)(2,1)S(1)}, bf16[2,96,768]{2,1,0:T(8,128)(2,1)S(1)}, u32[]{:S(2)}, u32[]{:S(2)}) collective-permute-start(bf16[2,96,768]{2,1,0:T(8,128)(2,1)S(1)} %copy-done.43), channel_id=1, source_target_pairs={{0,8},{8,0},{16,24},{24,16},{1,9},{9,1},{17,25},{25,17},{2,10},{10... | collective-permute-start | bytes 884744 | tf_op jit(solution)/shard_map/ppermute | solution.py:27
  48.0 10.8 %collective-permute-start.12 = (bf16[3,96,768]{2,1,0:T(8,128)(2,1)S(1)}, bf16[3,96,768]{2,1,0:T(8,128)(2,1)S(1)}, u32[]{:S(2)}, u32[]{:S(2)}) collective-permute-start(bf16[3,96,768]{2,1,0:T(8,128)(2,1)S(1)} %collective-permute-done.7.refs_1_), channel_id=1, source_target_pairs={{0,16},{8,24},{16,0},{24,8},{1,17},{9,25},{17,1},{25,9},{2,18},{10... | collective-permute-start | bytes 1327112 | tf_op jit(solution)/shard_map/ppermute | solution.py:27
  62.3 14.6 %collective-permute-start.17 = (bf16[3,4,96,768]{3,2,1,0:T(8,128)(2,1)}, bf16[3,4,96,768]{3,2,1,0:T(8,128)(2,1)}, u32[]{:S(2)}, u32[]{:S(2)}) collective-permute-start(bf16[3,4,96,768]{3,2,1,0:T(8,128)(2,1)} %stack_pieces.2.mine_ref), channel_id=1, source_target_pairs={{0,1},{1,0},{2,3},{3,2},{4,5},{5,4},{6,7},{7,6},{8,9},{9,8},{10,11... | collective-permute-start | bytes 5308424 | tf_op jit(solution)/shard_map/ppermute | solution.py:32
  64.2 8.6 %collective-permute-start.19 = (bf16[2,96,768]{2,1,0:T(8,128)(2,1)S(1)}, bf16[2,96,768]{2,1,0:T(8,128)(2,1)S(1)}, u32[]{:S(2)}, u32[]{:S(2)}) collective-permute-start(bf16[2,96,768]{2,1,0:T(8,128)(2,1)S(1)} %copy-done.43), channel_id=1, source_target_pairs={{0,16},{8,24},{16,0},{24,8},{1,17},{9,25},{17,1},{25,9},{2,18},{10... | collective-permute-start | bytes 884744 | tf_op jit(solution)/shard_map/ppermute | solution.py:27
  65.4 8.1 %collective-permute-start.18 = (bf16[256,768]{1,0:T(8,128)(2,1)S(1)}, bf16[256,768]{1,0:T(8,128)(2,1)S(1)}, u32[]{:S(2)}, u32[]{:S(2)}) collective-permute-start(bf16[256,768]{1,0:T(8,128)(2,1)S(1)} %pad_maximum_fusion.2), channel_id=1, source_target_pairs={{0,1},{1,0},{2,3},{3,2},{4,5},{5,4},{6,7},{7,6},{8,9},{9,8},{10,11... | collective-permute-start | bytes 1179656 | tf_op jit(solution)/shard_map/ppermute | solution.py:32
  66.0 8.7 %collective-permute-start.14 = (bf16[128,192]{1,0:T(8,128)(2,1)S(1)}, bf16[128,192]{1,0:T(8,128)(2,1)S(1)}, u32[]{:S(2)}, u32[]{:S(2)}) collective-permute-start(bf16[128,192]{1,0:T(8,128)(2,1)S(1)} %copy-done.58), channel_id=1, source_target_pairs={{0,2},{1,3},{2,0},{3,1},{4,6},{5,7},{6,4},{7,5},{8,10},{9,11},{10,... | collective-permute-start | bytes 147464 | tf_op jit(solution)/shard_map/ppermute | solution.py:37
  66.1 9.9 %collective-permute-start.15 = (bf16[128,192]{1,0:T(8,128)(2,1)S(1)}, bf16[128,192]{1,0:T(8,128)(2,1)S(1)}, u32[]{:S(2)}, u32[]{:S(2)}) collective-permute-start(bf16[128,192]{1,0:T(8,128)(2,1)S(1)} %copy-done.57), channel_id=1, source_target_pairs={{0,4},{1,5},{2,6},{3,7},{4,0},{5,1},{6,2},{7,3},{8,12},{9,13},{10,... | collective-permute-start | bytes 147464 | tf_op jit(solution)/shard_map/ppermute | solution.py:37
  72.8 4.2 %collective-permute-start.16 = (bf16[128,192]{1,0:T(8,128)(2,1)S(1)}, bf16[128,192]{1,0:T(8,128)(2,1)S(1)}, u32[]{:S(2)}, u32[]{:S(2)}) collective-permute-start(bf16[128,192]{1,0:T(8,128)(2,1)S(1)} %copy-done.56), channel_id=1, source_target_pairs={{0,6},{1,7},{2,4},{3,5},{4,2},{5,3},{6,0},{7,1},{8,14},{9,15},{10,... | collective-permute-start | bytes 147464 | tf_op jit(solution)/shard_map/ppermute | solution.py:37
  73.6 34.1 %collective-permute-start.22 = (f32[128,128]{0,1:T(8,128)S(1)}, f32[128,128]{0,1:T(8,128)S(1)}, u32[]{:S(2)}, u32[]{:S(2)}) collective-permute-start(f32[128,128]{0,1:T(8,128)S(1)} %broadcast_in_dim.46), channel_id=1, source_target_pairs={{0,1},{1,0},{2,3},{3,2},{4,5},{5,4},{6,7},{7,6},{8,9},{9,8},{10,11... | collective-permute-start | bytes 196616 | tf_op jit(solution)/shard_map/ppermute | solution.py:32
  74.8 8.8 %collective-permute-start.20 = (bf16[2,96,768]{2,1,0:T(8,128)(2,1)}, bf16[2,96,768]{2,1,0:T(8,128)(2,1)S(1)}, u32[]{:S(2)}, u32[]{:S(2)}) collective-permute-start(bf16[2,96,768]{2,1,0:T(8,128)(2,1)} %copy-done.44), channel_id=1, source_target_pairs={{0,16},{8,24},{16,0},{24,8},{1,17},{9,25},{17,1},{25,9},{2,18},{10... | collective-permute-start | bytes 884744 | tf_op jit(solution)/shard_map/ppermute | solution.py:27
  86.6 6.0 %collective-permute-start.21 = (bf16[2,4,96,768]{3,2,1,0:T(8,128)(2,1)}, bf16[2,4,96,768]{3,2,1,0:T(8,128)(2,1)S(1)}, u32[]{:S(2)}, u32[]{:S(2)}) collective-permute-start(bf16[2,4,96,768]{3,2,1,0:T(8,128)(2,1)} %stack_pieces.3.mine_ref), channel_id=1, source_target_pairs={{0,1},{1,0},{2,3},{3,2},{4,5},{5,4},{6,7},{7,6},{8,9},{9,8},{10,11... | collective-permute-start | bytes 3538952 | tf_op jit(solution)/shard_map/ppermute | solution.py:32
  107.6 1.8 collective-permute-start.23
  109.8 10.2 %collective-permute-start.26 = (bf16[1,40,1536]{2,1,0:T(8,128)(2,1)S(1)}, bf16[1,40,1536]{2,1,0:T(8,128)(2,1)S(1)}, u32[]{:S(2)}, u32[]{:S(2)}) collective-permute-start(bf16[1,40,1536]{2,1,0:T(8,128)(2,1)S(1)} %get-tuple-element.299), channel_id=1, source_target_pairs={{0,6},{1,7},{2,4},{3,5},{4,2},{5,3},{6,0},{7,1},{8,14},{9,15},{10,... | collective-permute-start | bytes 368648 | tf_op jit(solution)/shard_map/ppermute | solution.py:37
  110.7 10.9 %collective-permute-start.25 = (bf16[1,40,1536]{2,1,0:T(8,128)(2,1)S(1)}, bf16[1,40,1536]{2,1,0:T(8,128)(2,1)S(1)}, u32[]{:S(2)}, u32[]{:S(2)}) collective-permute-start(bf16[1,40,1536]{2,1,0:T(8,128)(2,1)S(1)} %get-tuple-element.300), channel_id=1, source_target_pairs={{0,4},{1,5},{2,6},{3,7},{4,0},{5,1},{6,2},{7,3},{8,12},{9,13},{10,... | collective-permute-start | bytes 368648 | tf_op jit(solution)/shard_map/ppermute | solution.py:37
  111.8 9.8 %collective-permute-start.24 = (bf16[1,40,1536]{2,1,0:T(8,128)(2,1)S(1)}, bf16[1,40,1536]{2,1,0:T(8,128)(2,1)S(1)}, u32[]{:S(2)}, u32[]{:S(2)}) collective-permute-start(bf16[1,40,1536]{2,1,0:T(8,128)(2,1)S(1)} %get-tuple-element.301), channel_id=1, source_target_pairs={{0,2},{1,3},{2,0},{3,1},{4,6},{5,7},{6,4},{7,5},{8,10},{9,11},{10,... | collective-permute-start | bytes 368648 | tf_op jit(solution)/shard_map/ppermute | solution.py:37
  121.7 12.4 %collective-permute-start.27 = (bf16[160,1536]{1,0:T(8,128)(2,1)S(1)}, bf16[160,1536]{1,0:T(8,128)(2,1)S(1)}, u32[]{:S(2)}, u32[]{:S(2)}) collective-permute-start(bf16[160,1536]{1,0:T(8,128)(2,1)S(1)} %maximum_bitcast_fusion.refs_0_), channel_id=1, source_target_pairs={{0,8},{8,0},{16,24},{24,16},{1,9},{9,1},{17,25},{25,17},{2,10},{10... | collective-permute-start | bytes 1474568 | tf_op jit(solution)/shard_map/ppermute | solution.py:27
  121.8 12.3 %collective-permute-start.28 = (bf16[160,1536]{1,0:T(8,128)(2,1)S(1)}, bf16[160,1536]{1,0:T(8,128)(2,1)S(1)}, u32[]{:S(2)}, u32[]{:S(2)}) collective-permute-start(bf16[160,1536]{1,0:T(8,128)(2,1)S(1)} %maximum_bitcast_fusion.refs_0_), channel_id=1, source_target_pairs={{0,16},{8,24},{16,0},{24,8},{1,17},{9,25},{17,1},{25,9},{2,18},{10... | collective-permute-start | bytes 1474568 | tf_op jit(solution)/shard_map/ppermute | solution.py:27
  123.1 22.4 %collective-permute-start.29 = (bf16[160,1536]{1,0:T(8,128)(2,1)S(1)}, bf16[160,1536]{1,0:T(8,128)(2,1)S(1)}, u32[]{:S(2)}, u32[]{:S(2)}) collective-permute-start(bf16[160,1536]{1,0:T(8,128)(2,1)S(1)} %maximum_bitcast_fusion.refs_0_), channel_id=1, source_target_pairs={{0,24},{8,16},{16,8},{24,0},{1,25},{9,17},{17,9},{25,1},{2,26},{10... | collective-permute-start | bytes 1474568 | tf_op jit(solution)/shard_map/ppermute | solution.py:27
  154.5 11.6 %collective-permute-start.30 = (bf16[160,1536]{1,0:T(8,128)(2,1)}, bf16[160,1536]{1,0:T(8,128)(2,1)S(1)}, u32[]{:S(2)}, u32[]{:S(2)}) collective-permute-start(bf16[160,1536]{1,0:T(8,128)(2,1)} %get-tuple-element.205), channel_id=1, source_target_pairs={{0,8},{8,0},{16,24},{24,16},{1,9},{9,1},{17,25},{25,17},{2,10},{10... | collective-permute-start | bytes 1474568 | tf_op jit(solution)/shard_map/ppermute | solution.py:27
  154.5 11.6 %collective-permute-start.31 = (bf16[160,1536]{1,0:T(8,128)(2,1)}, bf16[160,1536]{1,0:T(8,128)(2,1)S(1)}, u32[]{:S(2)}, u32[]{:S(2)}) collective-permute-start(bf16[160,1536]{1,0:T(8,128)(2,1)} %get-tuple-element.206), channel_id=1, source_target_pairs={{0,16},{8,24},{16,0},{24,8},{1,17},{9,25},{17,1},{25,9},{2,18},{10... | collective-permute-start | bytes 1474568 | tf_op jit(solution)/shard_map/ppermute | solution.py:27
  156.1 20.4 %collective-permute-start.32 = (bf16[160,1536]{1,0:T(8,128)(2,1)}, bf16[160,1536]{1,0:T(8,128)(2,1)S(1)}, u32[]{:S(2)}, u32[]{:S(2)}) collective-permute-start(bf16[160,1536]{1,0:T(8,128)(2,1)} %get-tuple-element.207), channel_id=1, source_target_pairs={{0,24},{8,16},{16,8},{24,0},{1,25},{9,17},{17,9},{25,1},{2,26},{10... | collective-permute-start | bytes 1474568 | tf_op jit(solution)/shard_map/ppermute | solution.py:27
  179.6 4.3 %collective-permute-start.35 = (bf16[40,1536]{1,0:T(8,128)(2,1)}, bf16[40,1536]{1,0:T(8,128)(2,1)S(1)}, u32[]{:S(2)}, u32[]{:S(2)}) collective-permute-start(bf16[40,1536]{1,0:T(8,128)(2,1)} %get-tuple-element.215), channel_id=1, source_target_pairs={{0,6},{1,7},{2,4},{3,5},{4,2},{5,3},{6,0},{7,1},{8,14},{9,15},{10,... | collective-permute-start | bytes 368648 | tf_op jit(solution)/shard_map/ppermute | solution.py:37
  179.6 11.9 %collective-permute-start.34 = (bf16[40,1536]{1,0:T(8,128)(2,1)}, bf16[40,1536]{1,0:T(8,128)(2,1)S(1)}, u32[]{:S(2)}, u32[]{:S(2)}) collective-permute-start(bf16[40,1536]{1,0:T(8,128)(2,1)} %get-tuple-element.214), channel_id=1, source_target_pairs={{0,4},{1,5},{2,6},{3,7},{4,0},{5,1},{6,2},{7,3},{8,12},{9,13},{10,... | collective-permute-start | bytes 368648 | tf_op jit(solution)/shard_map/ppermute | solution.py:37
  182.9 8.6 %collective-permute-start.33 = (bf16[40,1536]{1,0:T(8,128)(2,1)}, bf16[40,1536]{1,0:T(8,128)(2,1)S(1)}, u32[]{:S(2)}, u32[]{:S(2)}) collective-permute-start(bf16[40,1536]{1,0:T(8,128)(2,1)} %get-tuple-element.213), channel_id=1, source_target_pairs={{0,2},{1,3},{2,0},{3,1},{4,6},{5,7},{6,4},{7,5},{8,10},{9,11},{10,... | collective-permute-start | bytes 368648 | tf_op jit(solution)/shard_map/ppermute | solution.py:37
  192.9 3.6 collective-permute-start.36
  219.2 10.6 %collective-permute-start.40 = (bf16[4,1024,384]{2,1,0:T(8,128)(2,1)}, bf16[4,1024,384]{2,1,0:T(8,128)(2,1)}, u32[]{:S(2)}, u32[]{:S(2)}) collective-permute-start(bf16[4,1024,384]{2,1,0:T(8,128)(2,1)} %get-tuple-element.222), channel_id=1, source_target_pairs={{0,1},{1,0},{2,3},{3,2},{4,5},{5,4},{6,7},{7,6},{8,9},{9,8},{10,11... | collective-permute-start | bytes 9437192 | tf_op jit(solution)/shard_map/ppermute | solution.py:32
  220.4 3.6 collective-permute-start.37
  222.0 4.1 %collective-permute-start.38 = (bf16[128,192]{1,0:T(8,128)(2,1)S(1)}, bf16[128,192]{1,0:T(8,128)(2,1)S(1)}, u32[]{:S(2)}, u32[]{:S(2)}) collective-permute-start(bf16[128,192]{1,0:T(8,128)(2,1)S(1)} %get-tuple-element.303), channel_id=1, source_target_pairs={{0,4},{1,5},{2,6},{3,7},{4,0},{5,1},{6,2},{7,3},{8,12},{9,13},{10,... | collective-permute-start | bytes 147464 | tf_op jit(solution)/shard_map/ppermute | solution.py:37
  223.0 6.8 %collective-permute-start.39 = (bf16[128,192]{1,0:T(8,128)(2,1)S(1)}, bf16[128,192]{1,0:T(8,128)(2,1)S(1)}, u32[]{:S(2)}, u32[]{:S(2)}) collective-permute-start(bf16[128,192]{1,0:T(8,128)(2,1)S(1)} %get-tuple-element.302), channel_id=1, source_target_pairs={{0,6},{1,7},{2,4},{3,5},{4,2},{5,3},{6,0},{7,1},{8,14},{9,15},{10,... | collective-permute-start | bytes 147464 | tf_op jit(solution)/shard_map/ppermute | solution.py:37
  235.0 18.3 %collective-permute-start.41 = (bf16[1024,384]{1,0:T(8,128)(2,1)S(1)}, bf16[1024,384]{1,0:T(8,128)(2,1)S(1)}, u32[]{:S(2)}, u32[]{:S(2)}) collective-permute-start(bf16[1024,384]{1,0:T(8,128)(2,1)S(1)} %get-tuple-element.235), channel_id=1, source_target_pairs={{0,8},{8,0},{16,24},{24,16},{1,9},{9,1},{17,25},{25,17},{2,10},{10... | collective-permute-start | bytes 2359304 | tf_op jit(solution)/shard_map/ppermute | solution.py:27
  236.1 17.9 %collective-permute-start.42 = (bf16[1024,384]{1,0:T(8,128)(2,1)S(1)}, bf16[1024,384]{1,0:T(8,128)(2,1)S(1)}, u32[]{:S(2)}, u32[]{:S(2)}) collective-permute-start(bf16[1024,384]{1,0:T(8,128)(2,1)S(1)} %get-tuple-element.236), channel_id=1, source_target_pairs={{0,16},{8,24},{16,0},{24,8},{1,17},{9,25},{17,1},{25,9},{2,18},{10... | collective-permute-start | bytes 2359304 | tf_op jit(solution)/shard_map/ppermute | solution.py:27
  236.3 64.1 %collective-permute-start.48 = (bf16[1024,384]{1,0:T(8,128)(2,1)S(1)}, bf16[1024,384]{1,0:T(8,128)(2,1)}, u32[]{:S(2)}, u32[]{:S(2)}) collective-permute-start(bf16[1024,384]{1,0:T(8,128)(2,1)S(1)} %get-tuple-element.247), channel_id=1, source_target_pairs={{0,24},{8,16},{16,8},{24,0},{1,25},{9,17},{17,9},{25,1},{2,26},{10... | collective-permute-start | bytes 2359304 | tf_op jit(solution)/shard_map/ppermute | solution.py:27
  253.9 6.4 %collective-permute-start.43 = (bf16[512,384]{1,0:T(8,128)(2,1)}, bf16[512,384]{1,0:T(8,128)(2,1)S(1)}, u32[]{:S(2)}, u32[]{:S(2)}) collective-permute-start(bf16[512,384]{1,0:T(8,128)(2,1)} %get-tuple-element.239), channel_id=1, source_target_pairs={{0,1},{1,0},{2,3},{3,2},{4,5},{5,4},{6,7},{7,6},{8,9},{9,8},{10,11... | collective-permute-start | bytes 1179656 | tf_op jit(solution)/shard_map/ppermute | solution.py:32
  264.8 35.6 %collective-permute-start.47 = (bf16[4,112,576]{2,1,0:T(8,128)(2,1)}, bf16[4,112,576]{2,1,0:T(8,128)(2,1)S(1)}, u32[]{:S(2)}, u32[]{:S(2)}) collective-permute-start(bf16[4,112,576]{2,1,0:T(8,128)(2,1)} %get-tuple-element.246), channel_id=1, source_target_pairs={{0,1},{1,0},{2,3},{3,2},{4,5},{5,4},{6,7},{7,6},{8,9},{9,8},{10,11... | collective-permute-start | bytes 1548296 | tf_op jit(solution)/shard_map/ppermute | solution.py:32
  266.0 23.6 %collective-permute-start.44 = (bf16[128,768]{1,0:T(8,128)(2,1)S(1)}, bf16[128,768]{1,0:T(8,128)(2,1)S(1)}, u32[]{:S(2)}, u32[]{:S(2)}) collective-permute-start(bf16[128,768]{1,0:T(8,128)(2,1)S(1)} %get-tuple-element.294), channel_id=1, source_target_pairs={{0,2},{1,3},{2,0},{3,1},{4,6},{5,7},{6,4},{7,5},{8,10},{9,11},{10,... | collective-permute-start | bytes 589832 | tf_op jit(solution)/shard_map/ppermute | solution.py:37
  281.2 14.8 %collective-permute-start.45 = (bf16[128,768]{1,0:T(8,128)(2,1)S(1)}, bf16[128,768]{1,0:T(8,128)(2,1)S(1)}, u32[]{:S(2)}, u32[]{:S(2)}) collective-permute-start(bf16[128,768]{1,0:T(8,128)(2,1)S(1)} %get-tuple-element.293), channel_id=1, source_target_pairs={{0,4},{1,5},{2,6},{3,7},{4,0},{5,1},{6,2},{7,3},{8,12},{9,13},{10,... | collective-permute-start | bytes 589832 | tf_op jit(solution)/shard_map/ppermute | solution.py:37
  283.8 16.6 %collective-permute-start.46 = (bf16[128,768]{1,0:T(8,128)(2,1)S(1)}, bf16[128,768]{1,0:T(8,128)(2,1)S(1)}, u32[]{:S(2)}, u32[]{:S(2)}) collective-permute-start(bf16[128,768]{1,0:T(8,128)(2,1)S(1)} %get-tuple-element.292), channel_id=1, source_target_pairs={{0,6},{1,7},{2,4},{3,5},{4,2},{5,3},{6,0},{7,1},{8,14},{9,15},{10,... | collective-permute-start | bytes 589832 | tf_op jit(solution)/shard_map/ppermute | solution.py:37
  303.3 7.6 %collective-permute-start.51 = (bf16[112,576]{1,0:T(8,128)(2,1)}, bf16[112,576]{1,0:T(8,128)(2,1)S(1)}, u32[]{:S(2)}, u32[]{:S(2)}) collective-permute-start(bf16[112,576]{1,0:T(8,128)(2,1)} %get-tuple-element.252), channel_id=1, source_target_pairs={{0,24},{8,16},{16,8},{24,0},{1,25},{9,17},{17,9},{25,1},{2,26},{10... | collective-permute-start | bytes 387080 | tf_op jit(solution)/shard_map/ppermute | solution.py:27
  305.7 7.0 %collective-permute-start.50 = (bf16[112,576]{1,0:T(8,128)(2,1)}, bf16[112,576]{1,0:T(8,128)(2,1)S(1)}, u32[]{:S(2)}, u32[]{:S(2)}) collective-permute-start(bf16[112,576]{1,0:T(8,128)(2,1)} %get-tuple-element.251), channel_id=1, source_target_pairs={{0,16},{8,24},{16,0},{24,8},{1,17},{9,25},{17,1},{25,9},{2,18},{10... | collective-permute-start | bytes 387080 | tf_op jit(solution)/shard_map/ppermute | solution.py:27
  305.8 6.9 %collective-permute-start.49 = (bf16[112,576]{1,0:T(8,128)(2,1)}, bf16[112,576]{1,0:T(8,128)(2,1)S(1)}, u32[]{:S(2)}, u32[]{:S(2)}) collective-permute-start(bf16[112,576]{1,0:T(8,128)(2,1)} %get-tuple-element.250), channel_id=1, source_target_pairs={{0,8},{8,0},{16,24},{24,16},{1,9},{9,1},{17,25},{25,17},{2,10},{10... | collective-permute-start | bytes 387080 | tf_op jit(solution)/shard_map/ppermute | solution.py:27
  309.0 13.4 %collective-permute-start.58 = (bf16[256,384]{1,0:T(8,128)(2,1)}, bf16[256,384]{1,0:T(8,128)(2,1)S(1)}, u32[]{:S(2)}, u32[]{:S(2)}) collective-permute-start(bf16[256,384]{1,0:T(8,128)(2,1)} %get-tuple-element.261), channel_id=1, source_target_pairs={{0,6},{1,7},{2,4},{3,5},{4,2},{5,3},{6,0},{7,1},{8,14},{9,15},{10,... | collective-permute-start | bytes 589832 | tf_op jit(solution)/shard_map/ppermute | solution.py:37
  310.9 15.5 %collective-permute-start.57 = (bf16[256,384]{1,0:T(8,128)(2,1)}, bf16[256,384]{1,0:T(8,128)(2,1)S(1)}, u32[]{:S(2)}, u32[]{:S(2)}) collective-permute-start(bf16[256,384]{1,0:T(8,128)(2,1)} %get-tuple-element.260), channel_id=1, source_target_pairs={{0,4},{1,5},{2,6},{3,7},{4,0},{5,1},{6,2},{7,3},{8,12},{9,13},{10,... | collective-permute-start | bytes 589832 | tf_op jit(solution)/shard_map/ppermute | solution.py:37
  310.9 15.5 %collective-permute-start.56 = (bf16[256,384]{1,0:T(8,128)(2,1)}, bf16[256,384]{1,0:T(8,128)(2,1)S(1)}, u32[]{:S(2)}, u32[]{:S(2)}) collective-permute-start(bf16[256,384]{1,0:T(8,128)(2,1)} %get-tuple-element.259), channel_id=1, source_target_pairs={{0,2},{1,3},{2,0},{3,1},{4,6},{5,7},{6,4},{7,5},{8,10},{9,11},{10,... | collective-permute-start | bytes 589832 | tf_op jit(solution)/shard_map/ppermute | solution.py:37
  312.9 25.8 %copy-start.15 = (bf16[112,576]{1,0:T(8,128)(2,1)}, bf16[112,576]{1,0:T(8,128)(2,1)S(1)}, u32[]{:S(2)}) copy-start(bf16[112,576]{1,0:T(8,128)(2,1)S(1)} %add_convert_fusion.7.refs_0_) | copy-start | bytes 387076
  312.9 18.7 %collective-permute-start.52 = (bf16[112,576]{1,0:T(8,128)(2,1)S(1)}, bf16[112,576]{1,0:T(8,128)(2,1)S(1)}, u32[]{:S(2)}, u32[]{:S(2)}) collective-permute-start(bf16[112,576]{1,0:T(8,128)(2,1)S(1)} %add_convert_fusion.7.refs_0_), channel_id=1, source_target_pairs={{0,2},{1,3},{2,0},{3,1},{4,6},{5,7},{6,4},{7,5},{8,10},{9,11},{10,... | collective-permute-start | bytes 387080 | tf_op jit(solution)/shard_map/ppermute | solution.py:37
  313.0 25.7 %collective-permute-start.53 = (bf16[112,576]{1,0:T(8,128)(2,1)S(1)}, bf16[112,576]{1,0:T(8,128)(2,1)S(1)}, u32[]{:S(2)}, u32[]{:S(2)}) collective-permute-start(bf16[112,576]{1,0:T(8,128)(2,1)S(1)} %add_convert_fusion.7.refs_0_), channel_id=1, source_target_pairs={{0,4},{1,5},{2,6},{3,7},{4,0},{5,1},{6,2},{7,3},{8,12},{9,13},{10,... | collective-permute-start | bytes 387080 | tf_op jit(solution)/shard_map/ppermute | solution.py:37
  322.3 25.0 %collective-permute-start.54 = (bf16[112,576]{1,0:T(8,128)(2,1)S(1)}, bf16[112,576]{1,0:T(8,128)(2,1)S(1)}, u32[]{:S(2)}, u32[]{:S(2)}) collective-permute-start(bf16[112,576]{1,0:T(8,128)(2,1)S(1)} %add_convert_fusion.7.refs_0_), channel_id=1, source_target_pairs={{0,6},{1,7},{2,4},{3,5},{4,2},{5,3},{6,0},{7,1},{8,14},{9,15},{10,... | collective-permute-start | bytes 387080 | tf_op jit(solution)/shard_map/ppermute | solution.py:37
  327.5 24.0 %collective-permute-start.59 = (bf16[256,384]{1,0:T(8,128)(2,1)S(1)}, bf16[256,384]{1,0:T(8,128)(2,1)S(1)}, u32[]{:S(2)}, u32[]{:S(2)}) collective-permute-start(bf16[256,384]{1,0:T(8,128)(2,1)S(1)} %add_convert_fusion.5.refs_0_), channel_id=1, source_target_pairs={{0,2},{1,3},{2,0},{3,1},{4,6},{5,7},{6,4},{7,5},{8,10},{9,11},{10,... | collective-permute-start | bytes 589832 | tf_op jit(solution)/shard_map/ppermute | solution.py:37
  331.6 19.9 %collective-permute-start.60 = (bf16[256,384]{1,0:T(8,128)(2,1)S(1)}, bf16[256,384]{1,0:T(8,128)(2,1)S(1)}, u32[]{:S(2)}, u32[]{:S(2)}) collective-permute-start(bf16[256,384]{1,0:T(8,128)(2,1)S(1)} %add_convert_fusion.5.refs_0_), channel_id=1, source_target_pairs={{0,4},{1,5},{2,6},{3,7},{4,0},{5,1},{6,2},{7,3},{8,12},{9,13},{10,... | collective-permute-start | bytes 589832 | tf_op jit(solution)/shard_map/ppermute | solution.py:37
  331.6 24.1 %collective-permute-start.61 = (bf16[256,384]{1,0:T(8,128)(2,1)S(1)}, bf16[256,384]{1,0:T(8,128)(2,1)S(1)}, u32[]{:S(2)}, u32[]{:S(2)}) collective-permute-start(bf16[256,384]{1,0:T(8,128)(2,1)S(1)} %add_convert_fusion.5.refs_0_), channel_id=1, source_target_pairs={{0,6},{1,7},{2,4},{3,5},{4,2},{5,3},{6,0},{7,1},{8,14},{9,15},{10,... | collective-permute-start | bytes 589832 | tf_op jit(solution)/shard_map/ppermute | solution.py:37
  349.9 10.9 %collective-permute-start.55 = (bf16[4,112,576]{2,1,0:T(8,128)(2,1)}, bf16[4,112,576]{2,1,0:T(8,128)(2,1)S(1)}, u32[]{:S(2)}, u32[]{:S(2)}) collective-permute-start(bf16[4,112,576]{2,1,0:T(8,128)(2,1)} %collect.2.mine_ref), channel_id=1, source_target_pairs={{0,1},{1,0},{2,3},{3,2},{4,5},{5,4},{6,7},{7,6},{8,9},{9,8},{10,11... | collective-permute-start | bytes 1548296 | tf_op jit(solution)/shard_map/ppermute | solution.py:32
  358.6 5.9 %collective-permute-start.62 = (bf16[1024,384]{1,0:T(8,128)(2,1)}, bf16[1024,384]{1,0:T(8,128)(2,1)S(1)}, u32[]{:S(2)}, u32[]{:S(2)}) collective-permute-start(bf16[1024,384]{1,0:T(8,128)(2,1)} %bitcast.138), channel_id=1, source_target_pairs={{0,1},{1,0},{2,3},{3,2},{4,5},{5,4},{6,7},{7,6},{8,9},{9,8},{10,11... | collective-permute-start | bytes 2359304 | tf_op jit(solution)/shard_map/ppermute | solution.py:32
  (63 other events, 345.5 us)
where the time goes:
time: 371 us; the launch traced here: 369 us
  waiting for transfers between devices  130 us (35%)
  Pallas kernels  98.7 us (27%)
  starting transfers between devices  83.1 us (22%)
  other arithmetic  19.1 us (5%)
  local copies, waits for them, and re-layouts  19 us (5%)
  matrix products  17.9 us (5%)
    ppermute x30, waiting for transfers between devices, swap_group(): return lax.ppermute(rows, 'ctx', [(i, i ^ 2 * k) for i in range(size)])  76.2 us
    ppermute x21, waiting for transfers between devices, swap_fsdp(): return lax.ppermute(rows, 'fsdp', [(i, i ^ k) for i in range(size)])  51.1 us
    ppermute x30, starting transfers between devices, swap_group(): return lax.ppermute(rows, 'ctx', [(i, i ^ 2 * k) for i in range(size)])  46.8 us
    ppermute x21, starting transfers between devices, swap_fsdp(): return lax.ppermute(rows, 'fsdp', [(i, i ^ k) for i in range(size)])  19.2 us
    ppermute x12, starting transfers between devices, swap_core(): return lax.ppermute(rows, 'ctx', [(i, i ^ 1) for i in range(size)])  17.1 us
    pallas_call x1, Pallas kernels, self_backward(): pl.pallas_call(partial(self_backward_kernel, first, done), grid_spec=pltp...  12.6 us
    dot_general x10, matrix products, dot(): return jnp.dot(left, right, preferred_element_type=WIDE)  12.4 us
    unnamed x132, local copies, waits for them, and re-layouts  11.5 us
  transfers between devices with their start and end apart: 63, of which 29 were waited for; matrix products, arithmetic and copies ran while one was open for 8% of the time, Pallas kernels for 17%

commit v1 on v0

--- a/solution.py
+++ b/solution.py
@@ -356,37 +356,25 @@
     return total.astype(LOW)
 
 
-def add_kernel(keep_ref, received_ref, *outs):
-    for k, out in enumerate(outs):
-        out[...] = add_low(keep_ref[k], received_ref[k])
-
-
-def add_pieces(keep, received):
-    size = keep.shape[0]
-    return pl.pallas_call(
-        add_kernel,
-        out_shape=[jax.ShapeDtypeStruct(keep.shape[1:], LOW)] * size,
-        in_specs=vmem(2),
-        out_specs=vmem(size),
-        compiler_params=pltpu.CompilerParams(vmem_limit_bytes=VMEM_LIMIT),
-        cost_estimate=takes(4),
-        name="add_pieces",
-    )(keep, received)
-
-
 def quarter_kernel(index_ref, *refs):
-    pieces, outs = refs[: len(refs) - GROUP], refs[len(refs) - GROUP :]
-    rows = outs[0].shape[0]
+    outs = refs[len(refs) - GROUP :]
+    count = (len(refs) - GROUP) // 2
+    rows = outs[0].shape[0] // 2
     for k, out in enumerate(outs):
         here = pl.ds(pl.multiple_of(index_ref[k] * rows, 16), rows)
-        out[...] = sum_low(pieces[0][here], [piece[here] for piece in pieces[1:]])
-
-
-def sum_quarters(pieces, group):
-    rows, width = pieces[0].shape
+        for half in range(2):
+            pieces = refs[half * count : (half + 1) * count]
+            out[half * rows : (half + 1) * rows] = sum_low(
+                pieces[0][here], [piece[here] for piece in pieces[1:]]
+            )
+
+
+def sum_quarters(top, bottom, group):
+    rows, width = top[0].shape
+    pieces = list(top) + list(bottom)
     return pl.pallas_call(
         quarter_kernel,
-        out_shape=[jax.ShapeDtypeStruct((rows // GROUP, width), LOW)] * GROUP,
+        out_shape=[jax.ShapeDtypeStruct((2 * rows // GROUP, width), LOW)] * GROUP,
         in_specs=[smem()] + vmem(len(pieces)),
         out_specs=vmem(GROUP),
         compiler_params=pltpu.CompilerParams(vmem_limit_bytes=VMEM_LIMIT),
@@ -397,15 +385,17 @@
 
 def collect_kernel(index_ref, *refs):
     pieces, out = refs[:-1], refs[-1]
+    rows = out.shape[2]
     for k in range(len(pieces)):
-        out[index_ref[k]] = pieces[k][...]
-
-
-def collect(pieces, spots):
-    rows = pieces[0]
+        for half in range(out.shape[0]):
+            out[half, index_ref[k]] = pieces[k][half * rows : (half + 1) * rows]
+
+
+def collect(pieces, spots, halves):
+    rows, width = pieces[0].shape
     return pl.pallas_call(
         collect_kernel,
-        out_shape=jax.ShapeDtypeStruct((GROUP,) + rows.shape, rows.dtype),
+        out_shape=jax.ShapeDtypeStruct((halves, GROUP, rows // halves, width), LOW),
         in_specs=[smem()] + vmem(GROUP),
         out_specs=vmem(1)[0],
         cost_estimate=takes(2),
@@ -455,24 +445,64 @@
     return list(results[:5]) + [results[5].T] + [one[0] for one in results[6:]]
 
 
-def qkv_grads_kernel(index_ref, rows_ref, grad_ref, table_ref, keep, send):
+def key_grads_kernel(index_ref, rows_ref, query_ref, own_ref, rest_ref, weight_ref, *outs):
     f_index, core = index_ref[0], index_ref[1]
-    size = keep.shape[0]
-    extra = 16
-    rows = keep.shape[1] - extra
-    product = dot_tn(rows_ref[...], grad_ref[...])
-    buckets = table_ref.shape[0] // size
+    ones, (keep, send) = outs[:-2], outs[-2:]
+    grads = jnp.concatenate([query_ref[...], add_low(own_ref[...], rest_ref[...])], axis=1)
+    count = grads.shape[0] // len(ones)
+    for k, one in enumerate(ones):
+        one[...] = dot_nt(grads[k * count : (k + 1) * count], weight_ref[...]).astype(LOW)
+    size, rows, _ = keep.shape
+    product = dot_tn(rows_ref[...], grads)
     for block in range(size):
         spot = block ^ f_index
         top = product[2 * block * rows : (2 * block + 1) * rows].astype(LOW)
         bottom = product[(2 * block + 1) * rows : (2 * block + 2) * rows].astype(LOW)
-        keep[spot, :rows] = jnp.where(core == 0, top, bottom)
-        send[spot, :rows] = jnp.where(core == 0, bottom, top)
-        keep[spot, rows:] = jnp.zeros((extra, keep.shape[2]), LOW)
-        send[spot, rows:] = jnp.zeros((extra, keep.shape[2]), LOW)
-        keep[spot, rows : rows + buckets, : table_ref.shape[1]] = table_ref[
-            block * buckets : (block + 1) * buckets
-        ].astype(LOW)
+        keep[spot] = jnp.where(core == 0, top, bottom)
+        send[spot] = jnp.where(core == 0, bottom, top)
+
+
+def key_grads(rows, query, own, rest, weight, f_index, core, size):
+    count, width = rows.shape
+    shape = jax.ShapeDtypeStruct((size, width // size // 2, weight.shape[1]), LOW)
+    results = pl.pallas_call(
+        key_grads_kernel,
+        out_shape=[jax.ShapeDtypeStruct((count // GROUP, width), LOW)] * GROUP + [shape] * 2,
+        in_specs=[smem()] + vmem(5),
+        out_specs=vmem(GROUP + 2),
+        compiler_params=pltpu.CompilerParams(vmem_limit_bytes=VMEM_LIMIT),
+        cost_estimate=takes(0.1),
+        name="key_grads",
+    )(jnp.stack([f_index, core]).astype(jnp.int32), rows, query, own, rest, weight)
+    return list(results[:GROUP]), results[GROUP], results[GROUP + 1]
+
+
+def add_qkv_kernel(index_ref, keep_ref, received_ref, table_ref, *outs):
+    rows = keep_ref.shape[1]
+    buckets = table_ref.shape[0] // len(outs)
+    for k, out in enumerate(outs):
+        out[:rows] = add_low(keep_ref[k], received_ref[k])
+        here = pl.ds(pl.multiple_of((index_ref[0] ^ k) * buckets, 8), buckets)
+        table = table_ref[here]
+        spare = out.shape[1] - table.shape[1]
+        table = jnp.concatenate([table, jnp.zeros((buckets, spare), WIDE)], axis=1)
+        below = jnp.zeros((out.shape[0] - rows - buckets, out.shape[1]), WIDE)
+        out[rows:] = jnp.concatenate([table, below]).astype(LOW)
+
+
+def add_qkv(keep, received, table, f_index):
+    size, rows, width = keep.shape
+    return list(
+        pl.pallas_call(
+            add_qkv_kernel,
+            out_shape=[jax.ShapeDtypeStruct((rows + 16, width), LOW)] * size,
+            in_specs=[smem()] + vmem(3),
+            out_specs=vmem(size),
+            compiler_params=pltpu.CompilerParams(vmem_limit_bytes=VMEM_LIMIT),
+            cost_estimate=takes(2),
+            name="add_qkv",
+        )(f_index.reshape(1).astype(jnp.int32), keep, received, table)
+    )
 
 
 def qkv_finish_kernel(index_ref, mine_ref, theirs_ref, *refs):
@@ -498,22 +528,6 @@
     for g in range(GROUP):
         table = mine_ref[g, rows:, :128].astype(WIDE) + theirs_ref[g, rows:, :128].astype(WIDE)
         bias_ref[:, g * OWN_HEADS : (g + 1) * OWN_HEADS] = table[:buckets, :OWN_HEADS]
-
-
-def qkv_weight_grads(rows, grads, table, f_index, core, size):
-    width = rows.shape[1]
-    half_shard = width // size // 2
-    extra = 16
-    shape = jax.ShapeDtypeStruct((size, half_shard + extra, grads.shape[1]), LOW)
-    return pl.pallas_call(
-        qkv_grads_kernel,
-        out_shape=[shape, shape],
-        in_specs=[smem()] + vmem(3),
-        out_specs=vmem(2),
-        compiler_params=pltpu.CompilerParams(vmem_limit_bytes=VMEM_LIMIT),
-        cost_estimate=takes(3.1),
-        name="qkv_grads",
-    )(jnp.stack([f_index, core]).astype(jnp.int32), rows, grads, table)
 
 
 def finish_qkv(mine, theirs, weights, gain, core, bias_shape):
@@ -1095,9 +1109,7 @@
     pairs_own = dot(normed_own, own_qkv[:, own_width:]).astype(LOW)
     pairs_rest = swap_core(pairs_own)
     encoder_pieces = gather_group(after(encoder, early).reshape(-1, width))
-    pairs_own, pairs_rest, early_x, early_y, *encoder_pieces = tie(
-        pairs_own, pairs_rest, early_x, early_y, *encoder_pieces
-    )
+    pairs_own, pairs_rest, early_x, early_y = tie(pairs_own, pairs_rest, early_x, early_y)
     early_xy = swap_fsdp(early_x, 2)
     late_x, late_y = swap_fsdp(late, 1), swap_fsdp(late, 2)
     if rests > 1:
@@ -1106,16 +1118,16 @@
             [pairs_rest] + [shift_rest(near, r) for r in range(1, rests)]
         )
     *attended_own, self_logs = self_forward(kinds, tiles, queries, pairs_own, pairs_rest)
-    *attended_own, early_xy, late_x = tie(*attended_own, early_xy, late_x)
+    attended_own, early_xy, late_x, encoder_pieces = tie(
+        attended_own, early_xy, late_x, encoder_pieces
+    )
     attended = [attended_own[0]] + [swap_group(attended_own[k], k) for k in range(1, GROUP)]
     late_xy = swap_fsdp(late_x, 2)
     early_mine = stack_pieces((early, early_x, early_y, early_xy), 1, f_index, group)
     early_theirs = swap_core(early_mine)
     encoder_own = jnp.concatenate(encoder_pieces)
     encoder_other = swap_core(encoder_own)
-    *attended, early_theirs, encoder_other, late_y = tie(
-        *attended, early_theirs, encoder_other, late_y
-    )
+    *attended, early_theirs, encoder_other = tie(*attended, early_theirs, encoder_other)
     out_full, cross_k_full, cross_v_full = weave_halves(early_mine, early_theirs, core)
     encoder_all = jnp.concatenate([encoder_own, encoder_other])
     if rests > 1:
@@ -1127,7 +1139,7 @@
     first_sum = hidden + dot(attended, out_full)
     inv_two = rms_of(first_sum)
     normed_two = (first_sum * inv_two * gain_two).astype(LOW)
-    normed_two, late_xy = tie(normed_two, late_xy)
+    normed_two, late_xy, late_y = tie(normed_two, late_xy, late_y)
     late_mine = stack_pieces((late, late_x, late_y, late_xy), 0, f_index, group)
     late_theirs = swap_core(late_mine)
 
@@ -1212,15 +1224,18 @@
     )
     *up_pieces, received = tie(*up_pieces, swap_core(send))
     up_own = jnp.concatenate(up_pieces)
-    parts = [add_low(keep[k], received[k]) for k in range(fsdp_size)]
-    up_own, *parts[1:] = tie(up_own, *parts[1:])
-    parts = [parts[0]] + [swap_fsdp(parts[k], k) for k in range(1, fsdp_size)]
+    middle = keep.shape[1] // 2
+    top = [add_low(keep[k, :middle], received[k, :middle]) for k in range(fsdp_size)]
+    bottom = [add_low(keep[k, middle:], received[k, middle:]) for k in range(fsdp_size)]
+    up_own, top[1:], bottom[1:] = tie(up_own, top[1:], bottom[1:])
+    top = [top[0]] + [swap_fsdp(top[k], k) for k in range(1, fsdp_size)]
     query_low, pair_own, pair_rest, bias_parts = self_backward(
         0, own_count // span, kinds, tiles, queries, up_own, self_logs, pairs_own, pairs_rest
     )
-    query_low, pair_own, pair_rest, bias_parts, parts[1], parts[2] = tie(
-        query_low, pair_own, pair_rest, bias_parts, parts[1], parts[2]
-    )
+    query_low, pair_own, pair_rest, bias_parts, top, bottom = tie(
+        query_low, pair_own, pair_rest, bias_parts, top, bottom
+    )
+    bottom = [bottom[0]] + [swap_fsdp(bottom[k], k) for k in range(1, fsdp_size)]
     if rests > 1:
         near = jnp.concatenate([pair_own, pair_rest[:own_count]]).astype(WIDE)
         for r in range(1, rests):
@@ -1228,27 +1243,27 @@
             piece = pair_rest[first : first + 2 * own_count]
             near = near + shift_rest(piece, -r).astype(WIDE)
         pair_own, pair_rest = near[:own_count].astype(LOW), near[own_count:].astype(LOW)
-    pair_low = add_low(pair_own, swap_core(pair_rest))
-    qkv_low = jnp.concatenate([query_low, pair_low], axis=1)
-    one_part = dot_nt(qkv_low, own_qkv).astype(LOW)
-    one_parts = one_part.reshape(GROUP, span, width)
+    one_parts, qkv_keep, qkv_send = key_grads(
+        normed_own, query_low, pair_own, swap_core(pair_rest), own_qkv, f_index, core, fsdp_size
+    )
     one_parts = [one_parts[0]] + [swap_group(one_parts[k], k) for k in range(1, GROUP)]
+    qkv_send, bottom, bias_parts, one_parts[1] = tie(
+        swap_core(qkv_send), bottom, bias_parts, one_parts[1]
+    )
+    quarters = sum_quarters(top, bottom, group)
+    quarters = [quarters[0]] + [swap_group(quarters[k], k) for k in range(1, GROUP)]
 
     table = jnp.pad(bucket_sums(bias_parts, lower_bounds).T, ((0, 0), (0, 128 - OWN_HEADS)))
-    qkv_keep, qkv_send = qkv_weight_grads(normed_own, qkv_low, table, f_index, core, fsdp_size)
-    qkv_send, parts[3:] = tie(swap_core(qkv_send), parts[3:])
-    qkv_parts = add_pieces(qkv_keep, qkv_send)
+    qkv_parts = add_qkv(qkv_keep, qkv_send, table, f_index)
     qkv_parts = [qkv_parts[0]] + [swap_fsdp(qkv_parts[k], k) for k in range(1, fsdp_size)]
-    qkv_shard = sum_rest(sum_low(qkv_parts[0], qkv_parts[1:])).astype(LOW)
-    *one_parts, parts[0] = tie(*one_parts, parts[0])
+    qkv_parts, one_parts, quarters = tie(qkv_parts, one_parts, quarters)
+    dense_shard = sum_rest(sum_low(quarters[0], quarters[1:])).astype(LOW)
     one_grad = sum(one.astype(WIDE) for one in one_parts)
     tokens_grad = first_grad + norm_grad(hidden, rms_of(hidden), gain_one, one_grad)
     tokens_grad = tokens_grad.reshape(tokens.shape)
-    quarters = sum_quarters(parts, group)
-    quarters = [quarters[0]] + [swap_group(quarters[k], k) for k in range(1, GROUP)]
-    dense_shard = sum_rest(sum_low(quarters[0], quarters[1:])).astype(LOW)
+    qkv_shard = sum_rest(sum_low(qkv_parts[0], qkv_parts[1:])).astype(LOW)
     spots = [group ^ k for k in range(GROUP)]
-    qkv_mine = collect(gather_group(qkv_shard), spots)
+    qkv_mine = collect(gather_group(qkv_shard), spots, 1)[0]
     query_total, key_total, value_total, bias_total, grad_gain_one = finish_qkv(
         qkv_mine,
         swap_core(qkv_mine),
@@ -1257,7 +1272,7 @@
         core,
         position_bias.shape,
     )
-    dense_mine = collect(gather_group(dense_shard), spots).reshape(-1, half_width)
+    dense_mine = collect(gather_group(dense_shard), spots, 2).reshape(-1, half_width)
     (
         cross_o_total,
         cross_q_total,

time: 371 us -> 347 us (0.935)
  waiting for transfers between devices: 130 us -> 110 us
  starting transfers between devices: 83.1 us -> 78.8 us
    ppermute x30, waiting for transfers between devices: 76.2 us -> 48.5 us  [swap_group(): return lax.ppermute(rows, 'ctx', [(i, i ^ 2 * k) for i in range(size)])]
    ppermute x30, starting transfers between devices: 46.8 us -> 29.6 us  [swap_group(): return lax.ppermute(rows, 'ctx', [(i, i ^ 2 * k) for i in range(size)])]
    ppermute x12, starting transfers between devices: 17.1 us -> 27.1 us  [swap_core(): return lax.ppermute(rows, 'ctx', [(i, i ^ 1) for i in range(size)])]
    ppermute x21 -> x24, waiting for transfers between devices: 51.1 us -> 59.8 us  [swap_fsdp(): return lax.ppermute(rows, 'fsdp', [(i, i ^ k) for i in range(size)])]
    ppermute x21 -> x24, starting transfers between devices: 19.2 us -> 22 us  [swap_fsdp(): return lax.ppermute(rows, 'fsdp', [(i, i ^ k) for i in range(size)])]
    unnamed x132 -> x130, local copies, waits for them, and re-layouts: 11.5 us -> 12.6 us
  transfers between devices with their start and end apart: 63 -> 66, of which waited for: 29 -> 30; matrix products, arithmetic and copies ran while one was open for 8% -> 8% of each run, Pallas kernels for 17% -> 19%
where the time goes in v1:
time: 347 us; the launch traced here: 345 us
  waiting for transfers between devices  110 us (32%)
  Pallas kernels  100 us (29%)
  starting transfers between devices  78.8 us (23%)
  local copies, waits for them, and re-layouts  20.7 us (6%)
  matrix products  17 us (5%)
  other arithmetic  16.8 us (5%)
    ppermute x24, waiting for transfers between devices, swap_fsdp(): return lax.ppermute(rows, 'fsdp', [(i, i ^ k) for i in range(size)])  59.8 us
    ppermute x30, waiting for transfers between devices, swap_group(): return lax.ppermute(rows, 'ctx', [(i, i ^ 2 * k) for i in range(size)])  48.5 us
    ppermute x30, starting transfers between devices, swap_group(): return lax.ppermute(rows, 'ctx', [(i, i ^ 2 * k) for i in range(size)])  29.6 us
    ppermute x12, starting transfers between devices, swap_core(): return lax.ppermute(rows, 'ctx', [(i, i ^ 1) for i in range(size)])  27.1 us
    ppermute x24, starting transfers between devices, swap_fsdp(): return lax.ppermute(rows, 'fsdp', [(i, i ^ k) for i in range(size)])  22 us
    unnamed x130, local copies, waits for them, and re-layouts  12.6 us
    pallas_call x1, Pallas kernels, self_backward(): pl.pallas_call(partial(self_backward_kernel, first, done), grid_spec=pltp...  12.6 us
    dot_general x10, matrix products, dot(): return jnp.dot(left, right, preferred_element_type=WIDE)  12.4 us
  transfers between devices with their start and end apart: 66, of which 30 were waited for; matrix products, arithmetic and copies ran while one was open for 8% of the time, Pallas kernels for 19%

profile of v1, /device:TPU:13, one launch (start us, length us, event | category | flops | bytes accessed | tf_op | source)
XLA Modules:
  0.0 345.0 jit_solution(7214883999745780714)
XLA Ops:
  0.9 2.3 collective-permute-start.1
  8.0 2.8 pack_weights.1
  16.8 7.3 %collective-permute-done.2 = bf16[128,768]{1,0:T(8,128)(2,1)S(1)} collective-permute-done((bf16[128,768]{1,0:T(8,128)(2,1)S(1)}, bf16[128,768]{1,0:T(8,128)(2,1)S(1)}, u32[]{:S(2)}, u32[]{:S(2)}) %collective-permute-start.2) | collective-permute-done | bytes 196640 | tf_op jit(solution)/shard_map/ppermute | solution.py:37
  25.0 2.3 place_qkv.1
  31.9 2.0 collective-permute-start.12
  35.2 2.6 collective-permute-start.6
  38.5 2.8 bias_tiles.1.tile_ref
  45.2 8.6 %self_forward.1 = (bf16[128,192]{1,0:T(8,128)(2,1)}, bf16[128,192]{1,0:T(8,128)(2,1)}, bf16[128,192]{1,0:T(8,128)(2,1)}, bf16[128,192]{1,0:T(8,128)(2,1)}, f32[512,128]{1,0:T(8,128)}) custom-call(s32[8,16]{1,0:T(8,128)} %clamp_add_fusion.kind_ref, f32[2,3,5,64,128]{4,3,2,1,0:T(8,128)} %bias_tiles.1.tile_ref, ...), custom_call_target="tpu_custom_call" | custom-call | flops 8499999744 | bytes 29750000 | tf_op jit(solution)/shard_map/self_forward/pallas_call | solution.py:801
  53.8 1.5 collective-permute-done.9.refs_3_
  56.1 2.8 stack_pieces.2.mine_ref
  63.7 2.3 collective-permute-start.22
  71.3 4.0 %weave_halves.2 = (bf16[4,2,96,768]{3,2,1,0:T(8,128)(2,1)}, bf16[4,2,96,768]{3,2,1,0:T(8,128)(2,1)}, bf16[4,2,96,768]{3,2,1,0:T(8,128)(2,1)}) custom-call(s32[1]{0:T(128)} %bitcast.2.index_ref, bf16[3,4,96,768]{3,2,1,0:T(8,128)(2,1)} %stack_pieces.2.mine_ref, bf16[3,4,96,768]{3,2,1,0:T(8,128)(2,1)} %copy-done.27), custom_call_target="tpu_custom_call" | custom-call | flops 4000000000 | bytes 14000000 | tf_op jit(solution)/shard_map/weave_halves/pallas_call | solution.py:207
  75.4 1.8 multiply_reduce_fusion.4
  77.4 1.8 collective-permute-done.19.refs_3_
  79.9 2.3 stack_pieces.3.mine_ref
  82.2 3.0 collective-permute-start.21
  85.6 1.4 copy-done.62
  87.0 1.7 convolution_convert_fusion.2.value_ref
  88.7 1.7 convolution_convert_fusion.3.key_ref
  91.4 3.2 weave_halves.3
  94.6 2.3 convolution_convert_fusion.8.query_ref
  96.9 6.6 %cross_forward.1 = (bf16[128,768]{1,0:T(8,128)(2,1)}, f32[128,768]{1,0:T(8,128)}) custom-call(bf16[128,768]{1,0:T(8,128)(2,1)} %convolution_convert_fusion.8.query_ref, bf16[512,768]{1,0:T(8,128)(2,1)} %convolution_convert_fusion.3.key_ref, bf16[512,768]{1,0:T(8,128)(2,1)} %convolution_convert_fusion.2.value_ref), custom_call_target="tpu_custom_call" | custom-call | flops 6600000000 | bytes 23100000 | tf_op jit(solution)/shard_map/cross_forward/pallas_call | solution.py:869
  107.8 3.2 collective-permute-start.25
  111.1 6.4 %collective-permute-done.26 = bf16[1,40,1536]{2,1,0:T(8,128)(2,1)S(1)} collective-permute-done((bf16[1,40,1536]{2,1,0:T(8,128)(2,1)S(1)}, bf16[1,40,1536]{2,1,0:T(8,128)(2,1)S(1)}, u32[]{:S(2)}, u32[]{:S(2)}) %collective-permute-start.26) | collective-permute-done | bytes 122912 | tf_op jit(solution)/shard_map/ppermute | solution.py:37
  118.4 2.0 collective-permute-start.27
  120.3 1.5 collective-permute-start.28
  121.8 9.3 %collective-permute-done.27.refs_1_ = bf16[160,1536]{1,0:T(8,128)(2,1)S(1)} collective-permute-done((bf16[160,1536]{1,0:T(8,128)(2,1)S(1)}, bf16[160,1536]{1,0:T(8,128)(2,1)S(1)}, u32[]{:S(2)}, u32[]{:S(2)}) %collective-permute-start.27) | collective-permute-done | bytes 491552 | tf_op jit(solution)/shard_map/ppermute | solution.py:27
  132.0 10.9 %collective-permute-done.29.refs_3_ = bf16[160,1536]{1,0:T(8,128)(2,1)S(1)} collective-permute-done((bf16[160,1536]{1,0:T(8,128)(2,1)S(1)}, bf16[160,1536]{1,0:T(8,128)(2,1)S(1)}, u32[]{:S(2)}, u32[]{:S(2)}) %collective-permute-start.29) | collective-permute-done | bytes 491552 | tf_op jit(solution)/shard_map/ppermute | solution.py:27
  143.7 8.3 %experts.1 = (bf16[160,1536]{1,0:T(8,128)(2,1)}, bf16[160,1536]{1,0:T(8,128)(2,1)}, bf16[160,1536]{1,0:T(8,128)(2,1)}, bf16[160,1536]{1,0:T(8,128)(2,1)}, bf16[640,1536]{1,0:T(8,128)(2,1)}) custom-call(bf16[160,1536]{1,0:T(8,128)(2,1)} %copy-done.13, bf16[160,1536]{1,0:T(8,128)(2,1)} %copy-done.31, bf16[160,1536]{1,0:T(8,128)(2,1)} %copy-done.32, ...), custom_call_target="tpu_custom_call" | custom-call | flops 8200000000 | bytes 28700000 | tf_op jit(solution)/shard_map/experts/pallas_call | solution.py:246
  154.7 8.6 %collective-permute-done.30.refs_1_ = bf16[160,1536]{1,0:T(8,128)(2,1)S(1)} collective-permute-done((bf16[160,1536]{1,0:T(8,128)(2,1)}, bf16[160,1536]{1,0:T(8,128)(2,1)S(1)}, u32[]{:S(2)}, u32[]{:S(2)}) %collective-permute-start.30) | collective-permute-done | bytes 491552 | tf_op jit(solution)/shard_map/ppermute | solution.py:27
  164.3 10.2 %collective-permute-done.32.refs_3_ = bf16[160,1536]{1,0:T(8,128)(2,1)S(1)} collective-permute-done((bf16[160,1536]{1,0:T(8,128)(2,1)}, bf16[160,1536]{1,0:T(8,128)(2,1)S(1)}, u32[]{:S(2)}, u32[]{:S(2)}) %collective-permute-start.32) | collective-permute-done | bytes 491552 | tf_op jit(solution)/shard_map/ppermute | solution.py:27
  175.3 2.4 sum_home.1
  177.7 2.2 collective-permute-start.34
  180.3 4.3 %collective-permute-done.35 = bf16[40,1536]{1,0:T(8,128)(2,1)S(1)} collective-permute-done((bf16[40,1536]{1,0:T(8,128)(2,1)}, bf16[40,1536]{1,0:T(8,128)(2,1)S(1)}, u32[]{:S(2)}, u32[]{:S(2)}) %collective-permute-start.35) | collective-permute-done | bytes 122912 | tf_op jit(solution)/shard_map/ppermute | solution.py:37
  186.3 5.8 %collective-permute-start.36 = (bf16[128,1536]{1,0:T(8,128)(2,1)S(1)}, bf16[128,1536]{1,0:T(8,128)(2,1)S(1)}, u32[]{:S(2)}, u32[]{:S(2)}) collective-permute-start(bf16[128,1536]{1,0:T(8,128)(2,1)S(1)} %slice.185), channel_id=1, source_target_pairs={{0,1},{1,0},{2,3},{3,2},{4,5},{5,4},{6,7},{7,6},{8,9},{9,8},{10,11... | collective-permute-start | bytes 1179656 | tf_op jit(solution)/shard_map/ppermute | solution.py:32
  196.3 8.1 %cross_backward.1 = (bf16[128,768]{1,0:T(8,128)(2,1)}, bf16[512,768]{1,0:T(8,128)(2,1)}, bf16[512,768]{1,0:T(8,128)(2,1)}) custom-call(bf16[128,768]{1,0:T(8,128)(2,1)} %convolution_convert_fusion.8.query_ref, bf16[128,768]{1,0:T(8,128)(2,1)} %convolution_convert_fusion.7.up_ref, f32[128,768]{1,0:T(8,128)} %get-tuple-element.241.log_ref, ...), custom_call_target="tpu_custom_call" | custom-call | flops 8200000000 | bytes 28700000 | tf_op jit(solution)/shard_map/cross_backward/pallas_call | solution.py:887
  204.4 1.6 multiply_reduce_fusion.1
  208.5 7.6 %weight_grads.1 = (bf16[4,1024,384]{2,1,0:T(8,128)(2,1)}, bf16[4,1024,384]{2,1,0:T(8,128)(2,1)}) custom-call(s32[3]{0:T(128)} %pad_add_fusion.3.index_ref, bf16[128,768]{1,0:T(8,128)(2,1)} %get-tuple-element.222.refs_0_, bf16[128,768]{1,0:T(8,128)(2,1)} %copy-done.10, bf16[128,768]{1,0:T(8,128)(2,1)} %copy-done.8, ...), custom_call_target="tpu_custom_call" | custom-call | flops 7500000256 | bytes 26250000 | tf_op jit(solution)/shard_map/weight_grads/pallas_call | solution.py:337
  216.6 2.1 collective-permute-start.37
  221.0 1.8 collective-permute-done.38
  222.8 3.4 collective-permute-done.39
  226.2 3.8 %fusion.34 = (bf16[512,384]{1,0:T(8,128)(2,1)}, bf16[512,384]{1,0:T(8,128)(2,1)}, bf16[512,384]{1,0:T(8,128)(2,1)S(1)}, bf16[512,384]{1,0:T(8,128)(2,1)S(1)}, bf...) fusion(bf16[4,1024,384]{2,1,0:T(8,128)(2,1)S(1)} %collective-pe, ...), kind=kLoop, calls=%fused_computation.68 | loop fusion | flops 6291456 | bytes 9437184 | tf_op jit(solution)/shard_map/convert_element_type | solution.py:349
  230.7 1.6 collective-permute-start.41
  233.5 12.6 %self_backward.1 = (bf16[512,192]{1,0:T(8,128)(2,1)}, bf16[512,384]{1,0:T(8,128)(2,1)}, bf16[512,384]{1,0:T(8,128)(2,1)}, f32[2,3,5,64,128]{4,3,2,1,0:T(8,128)}) custom-call(s32[8,16]{1,0:T(8,128)} %clamp_add_fusion.kind_ref, f32[2,3,5,64,128]{4,3,2,1,0:T(8,128)} %bias_tiles.1.tile_ref, bf16[512,192]{1,0:T(8,128)(2,1)} %convolution_convert_fusion.5.query_ref, ...), custom_call_target="tpu_custom_call" | custom-call | flops 8999999488 | bytes 31500000 | tf_op jit(solution)/shard_map/self_backward/pallas_call | solution.py:841
  246.2 3.7 %collective-permute-done.43.refs_3_ = bf16[512,384]{1,0:T(8,128)(2,1)S(1)} collective-permute-done((bf16[512,384]{1,0:T(8,128)(2,1)S(1)}, bf16[512,384]{1,0:T(8,128)(2,1)S(1)}, u32[]{:S(2)}, u32[]{:S(2)}) %collective-permute-start.43) | collective-permute-done | bytes 393248 | tf_op jit(solution)/shard_map/ppermute | solution.py:27
  249.9 2.5 collective-permute-start.44
  254.1 1.5 collective-permute-start.48
  256.4 4.7 %key_grads.1 = (bf16[128,768]{1,0:T(8,128)(2,1)}, bf16[128,768]{1,0:T(8,128)(2,1)}, bf16[128,768]{1,0:T(8,128)(2,1)}, bf16[128,768]{1,0:T(8,128)(2,1)}, bf16[4,9...) custom-call(s32[2]{0:T(128)} %pad_add_fusion.2.index_ref, bf16[512,768]{1,0:T(8,128)(2,1)} %copy-done.4, ...), custom_call_target="tpu_custom_call" | custom-call | flops 100000000 | bytes 350000 | tf_op jit(solution)/shard_map/key_grads/pallas_call | solution.py:468
  265.8 7.1 %collective-permute-done.48.refs_7_ = bf16[512,384]{1,0:T(8,128)(2,1)} collective-permute-done((bf16[512,384]{1,0:T(8,128)(2,1)S(1)}, bf16[512,384]{1,0:T(8,128)(2,1)}, u32[]{:S(2)}, u32[]{:S(2)}) %collective-permute-start.48) | collective-permute-done | bytes 393248 | tf_op jit(solution)/shard_map/ppermute | solution.py:27
  274.8 2.0 add_qkv.1
  277.1 2.9 sum_quarters.1
  280.0 1.8 collective-permute-start.56
  285.4 2.8 collective-permute-done.51
  289.5 9.8 %collective-permute-done.57 = bf16[256,384]{1,0:T(8,128)(2,1)S(1)} collective-permute-done((bf16[256,384]{1,0:T(8,128)(2,1)}, bf16[256,384]{1,0:T(8,128)(2,1)S(1)}, u32[]{:S(2)}, u32[]{:S(2)}) %collective-permute-start.57) | collective-permute-done | bytes 196640 | tf_op jit(solution)/shard_map/ppermute | solution.py:37
  300.5 1.6 collective-permute-start.60
  304.4 1.5 collective-permute-start.64
  305.9 5.7 %expert_grads.1 = (f32[768,768]{1,0:T(8,128)}, f32[768,768]{1,0:T(8,128)}) custom-call(bf16[160,1536]{1,0:T(8,128)(2,1)} %copy-done.13, bf16[160,1536]{1,0:T(8,128)(2,1)} %copy-done.31, bf16[160,1536]{1,0:T(8,128)(2,1)} %copy-done.32, bf16[160,1536]{1,0:T(8,128)(2,1)} %copy-done.33, bf16[640,1536]{1,0:T(8,128)(2,1)} %get-tuple-element.324.refs_4_), custom_call_target="tpu_custom_call" | custom-call | flops 5699999744 | bytes 19950000 | tf_op jit(solution)/shard_map/expert_grads/pallas_call | solution.py:270
  311.7 6.4 %collective-permute-done.60.refs_3_ = bf16[112,576]{1,0:T(8,128)(2,1)S(1)} collective-permute-done((bf16[112,576]{1,0:T(8,128)(2,1)S(1)}, bf16[112,576]{1,0:T(8,128)(2,1)S(1)}, u32[]{:S(2)}, u32[]{:S(2)}) %collective-permute-start.60) | collective-permute-done | bytes 129056 | tf_op jit(solution)/shard_map/ppermute | solution.py:37
  318.7 2.0 collect.2
  320.7 7.0 %collective-permute-start.61 = (bf16[4,112,576]{2,1,0:T(8,128)(2,1)}, bf16[4,112,576]{2,1,0:T(8,128)(2,1)S(1)}, u32[]{:S(2)}, u32[]{:S(2)}) collective-permute-start(bf16[4,112,576]{2,1,0:T(8,128)(2,1)} %bitcast.151), channel_id=1, source_target_pairs={{0,1},{1,0},{2,3},{3,2},{4,5},{5,4},{6,7},{7,6},{8,9},{9,8},{10,11... | collective-permute-start | bytes 1548296 | tf_op jit(solution)/shard_map/ppermute | solution.py:32
  327.7 4.1 %collective-permute-done.64.refs_3_ = bf16[256,384]{1,0:T(8,128)(2,1)S(1)} collective-permute-done((bf16[256,384]{1,0:T(8,128)(2,1)S(1)}, bf16[256,384]{1,0:T(8,128)(2,1)S(1)}, u32[]{:S(2)}, u32[]{:S(2)}) %collective-permute-start.64) | collective-permute-done | bytes 196640 | tf_op jit(solution)/shard_map/ppermute | solution.py:37
  332.5 2.2 collect.3
  337.8 2.9 qkv_finish.1
  341.6 3.4 finish_weights.1
  (324 shorter events, 83.3 us)
Async XLA Ops:
  0.7 15.3 %collective-permute-start = (bf16[128,768]{1,0:T(8,128)(2,1)}, bf16[128,768]{1,0:T(8,128)(2,1)S(1)}, u32[]{:S(2)}, u32[]{:S(2)}) collective-permute-start(bf16[128,768]{1,0:T(8,128)(2,1)} %bitcast.121), channel_id=1, source_target_pairs={{0,2},{1,3},{2,0},{3,1},{4,6},{5,7},{6,4},{7,5},{8,10},{9,11},{10,... | collective-permute-start | bytes 589832 | tf_op jit(solution)/shard_map/ppermute | solution.py:37
  0.9 15.9 %collective-permute-start.1 = (bf16[128,768]{1,0:T(8,128)(2,1)}, bf16[128,768]{1,0:T(8,128)(2,1)S(1)}, u32[]{:S(2)}, u32[]{:S(2)}) collective-permute-start(bf16[128,768]{1,0:T(8,128)(2,1)} %bitcast.122), channel_id=1, source_target_pairs={{0,4},{1,5},{2,6},{3,7},{4,0},{5,1},{6,2},{7,3},{8,12},{9,13},{10,... | collective-permute-start | bytes 589832 | tf_op jit(solution)/shard_map/ppermute | solution.py:37
  10.8 13.3 %collective-permute-start.3 = (bf16[208,576]{1,0:T(8,128)(2,1)}, bf16[208,576]{1,0:T(8,128)(2,1)S(1)}, u32[]{:S(2)}, u32[]{:S(2)}) collective-permute-start(bf16[208,576]{1,0:T(8,128)(2,1)} %get-tuple-element.177.refs_0_), channel_id=1, source_target_pairs={{0,8},{8,0},{16,24},{24,16},{1,9},{9,1},{17,25},{25,17},{2,10},{10... | collective-permute-start | bytes 718856 | tf_op jit(solution)/shard_map/ppermute | solution.py:27
  12.1 12.0 %collective-permute-start.4 = (bf16[208,576]{1,0:T(8,128)(2,1)}, bf16[208,576]{1,0:T(8,128)(2,1)S(1)}, u32[]{:S(2)}, u32[]{:S(2)}) collective-permute-start(bf16[208,576]{1,0:T(8,128)(2,1)} %get-tuple-element.177.refs_0_), channel_id=1, source_target_pairs={{0,16},{8,24},{16,0},{24,8},{1,17},{9,25},{17,1},{25,9},{2,18},{10... | collective-permute-start | bytes 718856 | tf_op jit(solution)/shard_map/ppermute | solution.py:27
  12.3 11.8 %collective-permute-start.5 = (bf16[208,576]{1,0:T(8,128)(2,1)}, bf16[208,576]{1,0:T(8,128)(2,1)S(1)}, u32[]{:S(2)}, u32[]{:S(2)}) collective-permute-start(bf16[208,576]{1,0:T(8,128)(2,1)} %get-tuple-element.177.refs_0_), channel_id=1, source_target_pairs={{0,24},{8,16},{16,8},{24,0},{1,25},{9,17},{17,9},{25,1},{2,26},{10... | collective-permute-start | bytes 718856 | tf_op jit(solution)/shard_map/ppermute | solution.py:27
  16.0 8.1 %collective-permute-start.2 = (bf16[128,768]{1,0:T(8,128)(2,1)S(1)}, bf16[128,768]{1,0:T(8,128)(2,1)S(1)}, u32[]{:S(2)}, u32[]{:S(2)}) collective-permute-start(bf16[128,768]{1,0:T(8,128)(2,1)S(1)} %bitcast.123), channel_id=1, source_target_pairs={{0,6},{1,7},{2,4},{3,5},{4,2},{5,3},{6,0},{7,1},{8,14},{9,15},{10,... | collective-permute-start | bytes 589832 | tf_op jit(solution)/shard_map/ppermute | solution.py:37
  29.0 14.7 %collective-permute-start.7 = (bf16[3,96,768]{2,1,0:T(8,128)(2,1)S(1)}, bf16[3,96,768]{2,1,0:T(8,128)(2,1)}, u32[]{:S(2)}, u32[]{:S(2)}) collective-permute-start(bf16[3,96,768]{2,1,0:T(8,128)(2,1)S(1)} %copy-done.38), channel_id=1, source_target_pairs={{0,8},{8,0},{16,24},{24,16},{1,9},{9,1},{17,25},{25,17},{2,10},{10... | collective-permute-start | bytes 1327112 | tf_op jit(solution)/shard_map/ppermute | solution.py:27
  30.2 13.7 %collective-permute-start.8 = (bf16[3,96,768]{2,1,0:T(8,128)(2,1)S(1)}, bf16[3,96,768]{2,1,0:T(8,128)(2,1)}, u32[]{:S(2)}, u32[]{:S(2)}) collective-permute-start(bf16[3,96,768]{2,1,0:T(8,128)(2,1)S(1)} %copy-done.38), channel_id=1, source_target_pairs={{0,16},{8,24},{16,0},{24,8},{1,17},{9,25},{17,1},{25,9},{2,18},{10... | collective-permute-start | bytes 1327112 | tf_op jit(solution)/shard_map/ppermute | solution.py:27
  30.6 23.2 %collective-permute-start.11 = (bf16[64,768]{1,0:T(8,128)(2,1)S(1)}, bf16[64,768]{1,0:T(8,128)(2,1)S(1)}, u32[]{:S(2)}, u32[]{:S(2)}) collective-permute-start(bf16[64,768]{1,0:T(8,128)(2,1)S(1)} %bitcast.136), channel_id=1, source_target_pairs={{0,2},{1,3},{2,0},{3,1},{4,6},{5,7},{6,4},{7,5},{8,10},{9,11},{10,... | collective-permute-start | bytes 294920 | tf_op jit(solution)/shard_map/ppermute | solution.py:37
  31.9 21.9 %collective-permute-start.12 = (bf16[64,768]{1,0:T(8,128)(2,1)S(1)}, bf16[64,768]{1,0:T(8,128)(2,1)S(1)}, u32[]{:S(2)}, u32[]{:S(2)}) collective-permute-start(bf16[64,768]{1,0:T(8,128)(2,1)S(1)} %bitcast.137), channel_id=1, source_target_pairs={{0,4},{1,5},{2,6},{3,7},{4,0},{5,1},{6,2},{7,3},{8,12},{9,13},{10,... | collective-permute-start | bytes 294920 | tf_op jit(solution)/shard_map/ppermute | solution.py:37
  35.2 7.1 %collective-permute-start.6 = (bf16[512,384]{1,0:T(8,128)(2,1)S(1)}, bf16[512,384]{1,0:T(8,128)(2,1)}, u32[]{:S(2)}, u32[]{:S(2)}) collective-permute-start(bf16[512,384]{1,0:T(8,128)(2,1)S(1)} %convolution_convert_fusion.4.own_ref), channel_id=1, source_target_pairs={{0,1},{1,0},{2,3},{3,2},{4,5},{5,4},{6,7},{7,6},{8,9},{9,8},{10,11... | collective-permute-start | bytes 1179656 | tf_op jit(solution)/shard_map/ppermute | solution.py:32
  42.3 11.4 %collective-permute-start.13 = (bf16[64,768]{1,0:T(8,128)(2,1)S(1)}, bf16[64,768]{1,0:T(8,128)(2,1)S(1)}, u32[]{:S(2)}, u32[]{:S(2)}) collective-permute-start(bf16[64,768]{1,0:T(8,128)(2,1)S(1)} %bitcast.138), channel_id=1, source_target_pairs={{0,6},{1,7},{2,4},{3,5},{4,2},{5,3},{6,0},{7,1},{8,14},{9,15},{10,... | collective-permute-start | bytes 294920 | tf_op jit(solution)/shard_map/ppermute | solution.py:37
  43.7 10.1 %collective-permute-start.10 = (bf16[2,96,768]{2,1,0:T(8,128)(2,1)S(1)}, bf16[2,96,768]{2,1,0:T(8,128)(2,1)S(1)}, u32[]{:S(2)}, u32[]{:S(2)}) collective-permute-start(bf16[2,96,768]{2,1,0:T(8,128)(2,1)S(1)} %copy-done.44), channel_id=1, source_target_pairs={{0,8},{8,0},{16,24},{24,16},{1,9},{9,1},{17,25},{25,17},{2,10},{10... | collective-permute-start | bytes 884744 | tf_op jit(solution)/shard_map/ppermute | solution.py:27
  43.9 11.4 %collective-permute-start.9 = (bf16[3,96,768]{2,1,0:T(8,128)(2,1)}, bf16[3,96,768]{2,1,0:T(8,128)(2,1)S(1)}, u32[]{:S(2)}, u32[]{:S(2)}) collective-permute-start(bf16[3,96,768]{2,1,0:T(8,128)(2,1)} %collective-permute-done.7.refs_1_), channel_id=1, source_target_pairs={{0,16},{8,24},{16,0},{24,8},{1,17},{9,25},{17,1},{25,9},{2,18},{10... | collective-permute-start | bytes 1327112 | tf_op jit(solution)/shard_map/ppermute | solution.py:27
  58.8 11.2 %collective-permute-start.17 = (bf16[3,4,96,768]{3,2,1,0:T(8,128)(2,1)}, bf16[3,4,96,768]{3,2,1,0:T(8,128)(2,1)S(1)}, u32[]{:S(2)}, u32[]{:S(2)}) collective-permute-start(bf16[3,4,96,768]{3,2,1,0:T(8,128)(2,1)} %stack_pieces.2.mine_ref), channel_id=1, source_target_pairs={{0,1},{1,0},{2,3},{3,2},{4,5},{5,4},{6,7},{7,6},{8,9},{9,8},{10,11... | collective-permute-start | bytes 5308424 | tf_op jit(solution)/shard_map/ppermute | solution.py:32
  60.3 9.8 %collective-permute-start.18 = (bf16[256,768]{1,0:T(8,128)(2,1)S(1)}, bf16[256,768]{1,0:T(8,128)(2,1)S(1)}, u32[]{:S(2)}, u32[]{:S(2)}) collective-permute-start(bf16[256,768]{1,0:T(8,128)(2,1)S(1)} %pad_maximum_fusion.1), channel_id=1, source_target_pairs={{0,1},{1,0},{2,3},{3,2},{4,5},{5,4},{6,7},{7,6},{8,9},{9,8},{10,11... | collective-permute-start | bytes 1179656 | tf_op jit(solution)/shard_map/ppermute | solution.py:32
  61.9 4.3 %collective-permute-start.15 = (bf16[128,192]{1,0:T(8,128)(2,1)}, bf16[128,192]{1,0:T(8,128)(2,1)S(1)}, u32[]{:S(2)}, u32[]{:S(2)}) collective-permute-start(bf16[128,192]{1,0:T(8,128)(2,1)} %get-tuple-element.199), channel_id=1, source_target_pairs={{0,4},{1,5},{2,6},{3,7},{4,0},{5,1},{6,2},{7,3},{8,12},{9,13},{10,... | collective-permute-start | bytes 147464 | tf_op jit(solution)/shard_map/ppermute | solution.py:37
  61.9 6.9 %collective-permute-start.16 = (bf16[128,192]{1,0:T(8,128)(2,1)}, bf16[128,192]{1,0:T(8,128)(2,1)S(1)}, u32[]{:S(2)}, u32[]{:S(2)}) collective-permute-start(bf16[128,192]{1,0:T(8,128)(2,1)} %get-tuple-element.200), channel_id=1, source_target_pairs={{0,6},{1,7},{2,4},{3,5},{4,2},{5,3},{6,0},{7,1},{8,14},{9,15},{10,... | collective-permute-start | bytes 147464 | tf_op jit(solution)/shard_map/ppermute | solution.py:37
  63.7 41.8 %collective-permute-start.22 = (f32[128,128]{0,1:T(8,128)S(1)}, f32[128,128]{0,1:T(8,128)}, u32[]{:S(2)}, u32[]{:S(2)}) collective-permute-start(f32[128,128]{0,1:T(8,128)S(1)} %broadcast_in_dim.46), channel_id=1, source_target_pairs={{0,1},{1,0},{2,3},{3,2},{4,5},{5,4},{6,7},{7,6},{8,9},{9,8},{10,11... | collective-permute-start | bytes 196616 | tf_op jit(solution)/shard_map/ppermute | solution.py:32
  66.3 11.1 %collective-permute-start.20 = (bf16[2,96,768]{2,1,0:T(8,128)(2,1)}, bf16[2,96,768]{2,1,0:T(8,128)(2,1)S(1)}, u32[]{:S(2)}, u32[]{:S(2)}) collective-permute-start(bf16[2,96,768]{2,1,0:T(8,128)(2,1)} %get-tuple-element.195.refs_0_), channel_id=1, source_target_pairs={{0,16},{8,24},{16,0},{24,8},{1,17},{9,25},{17,1},{25,9},{2,18},{10... | collective-permute-start | bytes 884744 | tf_op jit(solution)/shard_map/ppermute | solution.py:27
  68.8 10.4 %collective-permute-start.19 = (bf16[2,96,768]{2,1,0:T(8,128)(2,1)}, bf16[2,96,768]{2,1,0:T(8,128)(2,1)S(1)}, u32[]{:S(2)}, u32[]{:S(2)}) collective-permute-start(bf16[2,96,768]{2,1,0:T(8,128)(2,1)} %copy-done.45), channel_id=1, source_target_pairs={{0,16},{8,24},{16,0},{24,8},{1,17},{9,25},{17,1},{25,9},{2,18},{10... | collective-permute-start | bytes 884744 | tf_op jit(solution)/shard_map/ppermute | solution.py:27
  82.2 8.2 %collective-permute-start.21 = (bf16[2,4,96,768]{3,2,1,0:T(8,128)(2,1)}, bf16[2,4,96,768]{3,2,1,0:T(8,128)(2,1)S(1)}, u32[]{:S(2)}, u32[]{:S(2)}) collective-permute-start(bf16[2,4,96,768]{3,2,1,0:T(8,128)(2,1)} %stack_pieces.3.mine_ref), channel_id=1, source_target_pairs={{0,1},{1,0},{2,3},{3,2},{4,5},{5,4},{6,7},{7,6},{8,9},{9,8},{10,11... | collective-permute-start | bytes 3538952 | tf_op jit(solution)/shard_map/ppermute | solution.py:32
  107.7 9.7 %collective-permute-start.26 = (bf16[1,40,1536]{2,1,0:T(8,128)(2,1)S(1)}, bf16[1,40,1536]{2,1,0:T(8,128)(2,1)S(1)}, u32[]{:S(2)}, u32[]{:S(2)}) collective-permute-start(bf16[1,40,1536]{2,1,0:T(8,128)(2,1)S(1)} %get-tuple-element.349), channel_id=1, source_target_pairs={{0,6},{1,7},{2,4},{3,5},{4,2},{5,3},{6,0},{7,1},{8,14},{9,15},{10,... | collective-permute-start | bytes 368648 | tf_op jit(solution)/shard_map/ppermute | solution.py:37
  107.8 10.5 %collective-permute-start.25 = (bf16[1,40,1536]{2,1,0:T(8,128)(2,1)S(1)}, bf16[1,40,1536]{2,1,0:T(8,128)(2,1)S(1)}, u32[]{:S(2)}, u32[]{:S(2)}) collective-permute-start(bf16[1,40,1536]{2,1,0:T(8,128)(2,1)S(1)} %get-tuple-element.350), channel_id=1, source_target_pairs={{0,4},{1,5},{2,6},{3,7},{4,0},{5,1},{6,2},{7,3},{8,12},{9,13},{10,... | collective-permute-start | bytes 368648 | tf_op jit(solution)/shard_map/ppermute | solution.py:37
  111.0 7.2 %collective-permute-start.24 = (bf16[1,40,1536]{2,1,0:T(8,128)(2,1)S(1)}, bf16[1,40,1536]{2,1,0:T(8,128)(2,1)S(1)}, u32[]{:S(2)}, u32[]{:S(2)}) collective-permute-start(bf16[1,40,1536]{2,1,0:T(8,128)(2,1)S(1)} %get-tuple-element.351), channel_id=1, source_target_pairs={{0,2},{1,3},{2,0},{3,1},{4,6},{5,7},{6,4},{7,5},{8,10},{9,11},{10,... | collective-permute-start | bytes 368648 | tf_op jit(solution)/shard_map/ppermute | solution.py:37
  118.4 12.7 %collective-permute-start.27 = (bf16[160,1536]{1,0:T(8,128)(2,1)S(1)}, bf16[160,1536]{1,0:T(8,128)(2,1)S(1)}, u32[]{:S(2)}, u32[]{:S(2)}) collective-permute-start(bf16[160,1536]{1,0:T(8,128)(2,1)S(1)} %maximum_bitcast_fusion.refs_0_), channel_id=1, source_target_pairs={{0,8},{8,0},{16,24},{24,16},{1,9},{9,1},{17,25},{25,17},{2,10},{10... | collective-permute-start | bytes 1474568 | tf_op jit(solution)/shard_map/ppermute | solution.py:27
  120.3 11.7 %collective-permute-start.28 = (bf16[160,1536]{1,0:T(8,128)(2,1)S(1)}, bf16[160,1536]{1,0:T(8,128)(2,1)S(1)}, u32[]{:S(2)}, u32[]{:S(2)}) collective-permute-start(bf16[160,1536]{1,0:T(8,128)(2,1)S(1)} %maximum_bitcast_fusion.refs_0_), channel_id=1, source_target_pairs={{0,16},{8,24},{16,0},{24,8},{1,17},{9,25},{17,1},{25,9},{2,18},{10... | collective-permute-start | bytes 1474568 | tf_op jit(solution)/shard_map/ppermute | solution.py:27
  121.8 21.2 %collective-permute-start.29 = (bf16[160,1536]{1,0:T(8,128)(2,1)S(1)}, bf16[160,1536]{1,0:T(8,128)(2,1)S(1)}, u32[]{:S(2)}, u32[]{:S(2)}) collective-permute-start(bf16[160,1536]{1,0:T(8,128)(2,1)S(1)} %maximum_bitcast_fusion.refs_0_), channel_id=1, source_target_pairs={{0,24},{8,16},{16,8},{24,0},{1,25},{9,17},{17,9},{25,1},{2,26},{10... | collective-permute-start | bytes 1474568 | tf_op jit(solution)/shard_map/ppermute | solution.py:27
  152.0 11.2 %collective-permute-start.30 = (bf16[160,1536]{1,0:T(8,128)(2,1)}, bf16[160,1536]{1,0:T(8,128)(2,1)S(1)}, u32[]{:S(2)}, u32[]{:S(2)}) collective-permute-start(bf16[160,1536]{1,0:T(8,128)(2,1)} %get-tuple-element.230), channel_id=1, source_target_pairs={{0,8},{8,0},{16,24},{24,16},{1,9},{9,1},{17,25},{25,17},{2,10},{10... | collective-permute-start | bytes 1474568 | tf_op jit(solution)/shard_map/ppermute | solution.py:27
  153.1 11.2 %collective-permute-start.31 = (bf16[160,1536]{1,0:T(8,128)(2,1)}, bf16[160,1536]{1,0:T(8,128)(2,1)S(1)}, u32[]{:S(2)}, u32[]{:S(2)}) collective-permute-start(bf16[160,1536]{1,0:T(8,128)(2,1)} %get-tuple-element.231), channel_id=1, source_target_pairs={{0,16},{8,24},{16,0},{24,8},{1,17},{9,25},{17,1},{25,9},{2,18},{10... | collective-permute-start | bytes 1474568 | tf_op jit(solution)/shard_map/ppermute | solution.py:27
  153.2 21.3 %collective-permute-start.32 = (bf16[160,1536]{1,0:T(8,128)(2,1)}, bf16[160,1536]{1,0:T(8,128)(2,1)S(1)}, u32[]{:S(2)}, u32[]{:S(2)}) collective-permute-start(bf16[160,1536]{1,0:T(8,128)(2,1)} %get-tuple-element.232), channel_id=1, source_target_pairs={{0,24},{8,16},{16,8},{24,0},{1,25},{9,17},{17,9},{25,1},{2,26},{10... | collective-permute-start | bytes 1474568 | tf_op jit(solution)/shard_map/ppermute | solution.py:27
  177.7 6.9 %collective-permute-start.35 = (bf16[40,1536]{1,0:T(8,128)(2,1)}, bf16[40,1536]{1,0:T(8,128)(2,1)S(1)}, u32[]{:S(2)}, u32[]{:S(2)}) collective-permute-start(bf16[40,1536]{1,0:T(8,128)(2,1)} %get-tuple-element.240), channel_id=1, source_target_pairs={{0,6},{1,7},{2,4},{3,5},{4,2},{5,3},{6,0},{7,1},{8,14},{9,15},{10,... | collective-permute-start | bytes 368648 | tf_op jit(solution)/shard_map/ppermute | solution.py:37
  177.7 6.9 %collective-permute-start.34 = (bf16[40,1536]{1,0:T(8,128)(2,1)}, bf16[40,1536]{1,0:T(8,128)(2,1)S(1)}, u32[]{:S(2)}, u32[]{:S(2)}) collective-permute-start(bf16[40,1536]{1,0:T(8,128)(2,1)} %get-tuple-element.239), channel_id=1, source_target_pairs={{0,4},{1,5},{2,6},{3,7},{4,0},{5,1},{6,2},{7,3},{8,12},{9,13},{10,... | collective-permute-start | bytes 368648 | tf_op jit(solution)/shard_map/ppermute | solution.py:37
  179.9 5.0 %collective-permute-start.33 = (bf16[40,1536]{1,0:T(8,128)(2,1)}, bf16[40,1536]{1,0:T(8,128)(2,1)S(1)}, u32[]{:S(2)}, u32[]{:S(2)}) collective-permute-start(bf16[40,1536]{1,0:T(8,128)(2,1)} %get-tuple-element.238), channel_id=1, source_target_pairs={{0,2},{1,3},{2,0},{3,1},{4,6},{5,7},{6,4},{7,5},{8,10},{9,11},{10,... | collective-permute-start | bytes 368648 | tf_op jit(solution)/shard_map/ppermute | solution.py:37
  186.3 7.1 %collective-permute-start.36 = (bf16[128,1536]{1,0:T(8,128)(2,1)S(1)}, bf16[128,1536]{1,0:T(8,128)(2,1)S(1)}, u32[]{:S(2)}, u32[]{:S(2)}) collective-permute-start(bf16[128,1536]{1,0:T(8,128)(2,1)S(1)} %slice.185), channel_id=1, source_target_pairs={{0,1},{1,0},{2,3},{3,2},{4,5},{5,4},{6,7},{7,6},{8,9},{9,8},{10,11... | collective-permute-start | bytes 1179656 | tf_op jit(solution)/shard_map/ppermute | solution.py:32
  216.1 10.1 %collective-permute-start.40 = (bf16[4,1024,384]{2,1,0:T(8,128)(2,1)}, bf16[4,1024,384]{2,1,0:T(8,128)(2,1)S(1)}, u32[]{:S(2)}, u32[]{:S(2)}) collective-permute-start(bf16[4,1024,384]{2,1,0:T(8,128)(2,1)} %get-tuple-element.247), channel_id=1, source_target_pairs={{0,1},{1,0},{2,3},{3,2},{4,5},{5,4},{6,7},{7,6},{8,9},{9,8},{10,11... | collective-permute-start | bytes 9437192 | tf_op jit(solution)/shard_map/ppermute | solution.py:32
  216.6 4.4 %collective-permute-start.37 = (bf16[128,192]{1,0:T(8,128)(2,1)S(1)}, bf16[128,192]{1,0:T(8,128)(2,1)S(1)}, u32[]{:S(2)}, u32[]{:S(2)}) collective-permute-start(bf16[128,192]{1,0:T(8,128)(2,1)S(1)} %get-tuple-element.354), channel_id=1, source_target_pairs={{0,2},{1,3},{2,0},{3,1},{4,6},{5,7},{6,4},{7,5},{8,10},{9,11},{10,... | collective-permute-start | bytes 147464 | tf_op jit(solution)/shard_map/ppermute | solution.py:37
  218.7 4.1 %collective-permute-start.38 = (bf16[128,192]{1,0:T(8,128)(2,1)S(1)}, bf16[128,192]{1,0:T(8,128)(2,1)S(1)}, u32[]{:S(2)}, u32[]{:S(2)}) collective-permute-start(bf16[128,192]{1,0:T(8,128)(2,1)S(1)} %get-tuple-element.353), channel_id=1, source_target_pairs={{0,4},{1,5},{2,6},{3,7},{4,0},{5,1},{6,2},{7,3},{8,12},{9,13},{10,... | collective-permute-start | bytes 147464 | tf_op jit(solution)/shard_map/ppermute | solution.py:37
  218.8 7.4 %collective-permute-start.39 = (bf16[128,192]{1,0:T(8,128)(2,1)S(1)}, bf16[128,192]{1,0:T(8,128)(2,1)S(1)}, u32[]{:S(2)}, u32[]{:S(2)}) collective-permute-start(bf16[128,192]{1,0:T(8,128)(2,1)S(1)} %get-tuple-element.352), channel_id=1, source_target_pairs={{0,6},{1,7},{2,4},{3,5},{4,2},{5,3},{6,0},{7,1},{8,14},{9,15},{10,... | collective-permute-start | bytes 147464 | tf_op jit(solution)/shard_map/ppermute | solution.py:37
  230.7 15.4 %collective-permute-start.41 = (bf16[512,384]{1,0:T(8,128)(2,1)S(1)}, bf16[512,384]{1,0:T(8,128)(2,1)S(1)}, u32[]{:S(2)}, u32[]{:S(2)}) collective-permute-start(bf16[512,384]{1,0:T(8,128)(2,1)S(1)} %get-tuple-element.260), channel_id=1, source_target_pairs={{0,8},{8,0},{16,24},{24,16},{1,9},{9,1},{17,25},{25,17},{2,10},{10... | collective-permute-start | bytes 1179656 | tf_op jit(solution)/shard_map/ppermute | solution.py:27
  232.3 13.8 %collective-permute-start.42 = (bf16[512,384]{1,0:T(8,128)(2,1)S(1)}, bf16[512,384]{1,0:T(8,128)(2,1)S(1)}, u32[]{:S(2)}, u32[]{:S(2)}) collective-permute-start(bf16[512,384]{1,0:T(8,128)(2,1)S(1)} %get-tuple-element.261), channel_id=1, source_target_pairs={{0,16},{8,24},{16,0},{24,8},{1,17},{9,25},{17,1},{25,9},{2,18},{10... | collective-permute-start | bytes 1179656 | tf_op jit(solution)/shard_map/ppermute | solution.py:27
  233.5 16.4 %collective-permute-start.43 = (bf16[512,384]{1,0:T(8,128)(2,1)S(1)}, bf16[512,384]{1,0:T(8,128)(2,1)S(1)}, u32[]{:S(2)}, u32[]{:S(2)}) collective-permute-start(bf16[512,384]{1,0:T(8,128)(2,1)S(1)} %get-tuple-element.262), channel_id=1, source_target_pairs={{0,24},{8,16},{16,8},{24,0},{1,25},{9,17},{17,9},{25,1},{2,26},{10... | collective-permute-start | bytes 1179656 | tf_op jit(solution)/shard_map/ppermute | solution.py:27
  249.9 5.7 %collective-permute-start.44 = (bf16[512,384]{1,0:T(8,128)(2,1)}, bf16[512,384]{1,0:T(8,128)(2,1)S(1)}, u32[]{:S(2)}, u32[]{:S(2)}) collective-permute-start(bf16[512,384]{1,0:T(8,128)(2,1)} %get-tuple-element.268), channel_id=1, source_target_pairs={{0,1},{1,0},{2,3},{3,2},{4,5},{5,4},{6,7},{7,6},{8,9},{9,8},{10,11... | collective-permute-start | bytes 1179656 | tf_op jit(solution)/shard_map/ppermute | solution.py:32
  253.0 10.7 %collective-permute-start.46 = (bf16[512,384]{1,0:T(8,128)(2,1)S(1)}, bf16[512,384]{1,0:T(8,128)(2,1)}, u32[]{:S(2)}, u32[]{:S(2)}) collective-permute-start(bf16[512,384]{1,0:T(8,128)(2,1)S(1)} %get-tuple-element.272), channel_id=1, source_target_pairs={{0,8},{8,0},{16,24},{24,16},{1,9},{9,1},{17,25},{25,17},{2,10},{10... | collective-permute-start | bytes 1179656 | tf_op jit(solution)/shard_map/ppermute | solution.py:27
  253.8 11.0 %collective-permute-start.47 = (bf16[512,384]{1,0:T(8,128)(2,1)S(1)}, bf16[512,384]{1,0:T(8,128)(2,1)}, u32[]{:S(2)}, u32[]{:S(2)}) collective-permute-start(bf16[512,384]{1,0:T(8,128)(2,1)S(1)} %get-tuple-element.273), channel_id=1, source_target_pairs={{0,16},{8,24},{16,0},{24,8},{1,17},{9,25},{17,1},{25,9},{2,18},{10... | collective-permute-start | bytes 1179656 | tf_op jit(solution)/shard_map/ppermute | solution.py:27
  254.1 18.8 %collective-permute-start.48 = (bf16[512,384]{1,0:T(8,128)(2,1)S(1)}, bf16[512,384]{1,0:T(8,128)(2,1)}, u32[]{:S(2)}, u32[]{:S(2)}) collective-permute-start(bf16[512,384]{1,0:T(8,128)(2,1)S(1)} %get-tuple-element.274), channel_id=1, source_target_pairs={{0,24},{8,16},{16,8},{24,0},{1,25},{9,17},{17,9},{25,1},{2,26},{10... | collective-permute-start | bytes 1179656 | tf_op jit(solution)/shard_map/ppermute | solution.py:27
  261.1 11.9 %collective-permute-start.45 = (bf16[4,96,576]{2,1,0:T(8,128)(2,1)}, bf16[4,96,576]{2,1,0:T(8,128)(2,1)S(1)}, u32[]{:S(2)}, u32[]{:S(2)}) collective-permute-start(bf16[4,96,576]{2,1,0:T(8,128)(2,1)} %get-tuple-element.270), channel_id=1, source_target_pairs={{0,1},{1,0},{2,3},{3,2},{4,5},{5,4},{6,7},{7,6},{8,9},{9,8},{10,11... | collective-permute-start | bytes 1327112 | tf_op jit(solution)/shard_map/ppermute | solution.py:32
  262.3 10.6 %collective-permute-start.49 = (bf16[128,768]{1,0:T(8,128)(2,1)}, bf16[128,768]{1,0:T(8,128)(2,1)S(1)}, u32[]{:S(2)}, u32[]{:S(2)}) collective-permute-start(bf16[128,768]{1,0:T(8,128)(2,1)} %get-tuple-element.276), channel_id=1, source_target_pairs={{0,2},{1,3},{2,0},{3,1},{4,6},{5,7},{6,4},{7,5},{8,10},{9,11},{10,... | collective-permute-start | bytes 589832 | tf_op jit(solution)/shard_map/ppermute | solution.py:37
  263.6 18.2 %collective-permute-start.53 = (bf16[128,768]{1,0:T(8,128)(2,1)}, bf16[128,768]{1,0:T(8,128)(2,1)S(1)}, u32[]{:S(2)}, u32[]{:S(2)}) collective-permute-start(bf16[128,768]{1,0:T(8,128)(2,1)} %get-tuple-element.285), channel_id=1, source_target_pairs={{0,4},{1,5},{2,6},{3,7},{4,0},{5,1},{6,2},{7,3},{8,12},{9,13},{10,... | collective-permute-start | bytes 589832 | tf_op jit(solution)/shard_map/ppermute | solution.py:37
  264.8 18.7 %collective-permute-start.54 = (bf16[128,768]{1,0:T(8,128)(2,1)}, bf16[128,768]{1,0:T(8,128)(2,1)S(1)}, u32[]{:S(2)}, u32[]{:S(2)}) collective-permute-start(bf16[128,768]{1,0:T(8,128)(2,1)} %get-tuple-element.286), channel_id=1, source_target_pairs={{0,6},{1,7},{2,4},{3,5},{4,2},{5,3},{6,0},{7,1},{8,14},{9,15},{10,... | collective-permute-start | bytes 589832 | tf_op jit(solution)/shard_map/ppermute | solution.py:37
  276.8 7.8 %collective-permute-start.50 = (bf16[112,576]{1,0:T(8,128)(2,1)}, bf16[112,576]{1,0:T(8,128)(2,1)S(1)}, u32[]{:S(2)}, u32[]{:S(2)}) collective-permute-start(bf16[112,576]{1,0:T(8,128)(2,1)} %get-tuple-element.280), channel_id=1, source_target_pairs={{0,8},{8,0},{16,24},{24,16},{1,9},{9,1},{17,25},{25,17},{2,10},{10... | collective-permute-start | bytes 387080 | tf_op jit(solution)/shard_map/ppermute | solution.py:27
  280.0 9.6 %collective-permute-start.55 = (bf16[256,384]{1,0:T(8,128)(2,1)}, bf16[256,384]{1,0:T(8,128)(2,1)S(1)}, u32[]{:S(2)}, u32[]{:S(2)}) collective-permute-start(bf16[256,384]{1,0:T(8,128)(2,1)} %get-tuple-element.296), channel_id=1, source_target_pairs={{0,2},{1,3},{2,0},{3,1},{4,6},{5,7},{6,4},{7,5},{8,10},{9,11},{10,... | collective-permute-start | bytes 589832 | tf_op jit(solution)/shard_map/ppermute | solution.py:37
  280.0 9.6 %collective-permute-start.56 = (bf16[256,384]{1,0:T(8,128)(2,1)}, bf16[256,384]{1,0:T(8,128)(2,1)S(1)}, u32[]{:S(2)}, u32[]{:S(2)}) collective-permute-start(bf16[256,384]{1,0:T(8,128)(2,1)} %get-tuple-element.297), channel_id=1, source_target_pairs={{0,4},{1,5},{2,6},{3,7},{4,0},{5,1},{6,2},{7,3},{8,12},{9,13},{10,... | collective-permute-start | bytes 589832 | tf_op jit(solution)/shard_map/ppermute | solution.py:37
  281.8 17.5 %collective-permute-start.57 = (bf16[256,384]{1,0:T(8,128)(2,1)}, bf16[256,384]{1,0:T(8,128)(2,1)S(1)}, u32[]{:S(2)}, u32[]{:S(2)}) collective-permute-start(bf16[256,384]{1,0:T(8,128)(2,1)} %get-tuple-element.298), channel_id=1, source_target_pairs={{0,6},{1,7},{2,4},{3,5},{4,2},{5,3},{6,0},{7,1},{8,14},{9,15},{10,... | collective-permute-start | bytes 589832 | tf_op jit(solution)/shard_map/ppermute | solution.py:37
  283.4 4.7 %collective-permute-start.51 = (bf16[112,576]{1,0:T(8,128)(2,1)S(1)}, bf16[112,576]{1,0:T(8,128)(2,1)S(1)}, u32[]{:S(2)}, u32[]{:S(2)}) collective-permute-start(bf16[112,576]{1,0:T(8,128)(2,1)S(1)} %copy-done.55), channel_id=1, source_target_pairs={{0,16},{8,24},{16,0},{24,8},{1,17},{9,25},{17,1},{25,9},{2,18},{10... | collective-permute-start | bytes 387080 | tf_op jit(solution)/shard_map/ppermute | solution.py:27
  284.6 4.9 %collective-permute-start.52 = (bf16[112,576]{1,0:T(8,128)(2,1)S(1)}, bf16[112,576]{1,0:T(8,128)(2,1)S(1)}, u32[]{:S(2)}, u32[]{:S(2)}) collective-permute-start(bf16[112,576]{1,0:T(8,128)(2,1)S(1)} %copy-done.54), channel_id=1, source_target_pairs={{0,24},{8,16},{16,8},{24,0},{1,25},{9,17},{17,9},{25,1},{2,26},{10... | collective-permute-start | bytes 387080 | tf_op jit(solution)/shard_map/ppermute | solution.py:27
  299.4 5.0 %collective-permute-start.58 = (bf16[112,576]{1,0:T(8,128)(2,1)S(1)}, bf16[112,576]{1,0:T(8,128)(2,1)S(1)}, u32[]{:S(2)}, u32[]{:S(2)}) collective-permute-start(bf16[112,576]{1,0:T(8,128)(2,1)S(1)} %add_convert_fusion.10.refs_0_), channel_id=1, source_target_pairs={{0,2},{1,3},{2,0},{3,1},{4,6},{5,7},{6,4},{7,5},{8,10},{9,11},{10,... | collective-permute-start | bytes 387080 | tf_op jit(solution)/shard_map/ppermute | solution.py:37
  299.5 12.2 %collective-permute-start.59 = (bf16[112,576]{1,0:T(8,128)(2,1)S(1)}, bf16[112,576]{1,0:T(8,128)(2,1)S(1)}, u32[]{:S(2)}, u32[]{:S(2)}) collective-permute-start(bf16[112,576]{1,0:T(8,128)(2,1)S(1)} %add_convert_fusion.10.refs_0_), channel_id=1, source_target_pairs={{0,4},{1,5},{2,6},{3,7},{4,0},{5,1},{6,2},{7,3},{8,12},{9,13},{10,... | collective-permute-start | bytes 387080 | tf_op jit(solution)/shard_map/ppermute | solution.py:37
  300.5 17.6 %collective-permute-start.60 = (bf16[112,576]{1,0:T(8,128)(2,1)S(1)}, bf16[112,576]{1,0:T(8,128)(2,1)S(1)}, u32[]{:S(2)}, u32[]{:S(2)}) collective-permute-start(bf16[112,576]{1,0:T(8,128)(2,1)S(1)} %add_convert_fusion.10.refs_0_), channel_id=1, source_target_pairs={{0,6},{1,7},{2,4},{3,5},{4,2},{5,3},{6,0},{7,1},{8,14},{9,15},{10,... | collective-permute-start | bytes 387080 | tf_op jit(solution)/shard_map/ppermute | solution.py:37
  303.2 24.5 %collective-permute-start.62 = (bf16[256,384]{1,0:T(8,128)(2,1)S(1)}, bf16[256,384]{1,0:T(8,128)(2,1)S(1)}, u32[]{:S(2)}, u32[]{:S(2)}) collective-permute-start(bf16[256,384]{1,0:T(8,128)(2,1)S(1)} %add_convert_fusion.8.refs_0_), channel_id=1, source_target_pairs={{0,2},{1,3},{2,0},{3,1},{4,6},{5,7},{6,4},{7,5},{8,10},{9,11},{10,... | collective-permute-start | bytes 589832 | tf_op jit(solution)/shard_map/ppermute | solution.py:37
  304.2 23.5 %collective-permute-start.63 = (bf16[256,384]{1,0:T(8,128)(2,1)S(1)}, bf16[256,384]{1,0:T(8,128)(2,1)S(1)}, u32[]{:S(2)}, u32[]{:S(2)}) collective-permute-start(bf16[256,384]{1,0:T(8,128)(2,1)S(1)} %add_convert_fusion.8.refs_0_), channel_id=1, source_target_pairs={{0,4},{1,5},{2,6},{3,7},{4,0},{5,1},{6,2},{7,3},{8,12},{9,13},{10,... | collective-permute-start | bytes 589832 | tf_op jit(solution)/shard_map/ppermute | solution.py:37
  304.4 27.4 %collective-permute-start.64 = (bf16[256,384]{1,0:T(8,128)(2,1)S(1)}, bf16[256,384]{1,0:T(8,128)(2,1)S(1)}, u32[]{:S(2)}, u32[]{:S(2)}) collective-permute-start(bf16[256,384]{1,0:T(8,128)(2,1)S(1)} %add_convert_fusion.8.refs_0_), channel_id=1, source_target_pairs={{0,6},{1,7},{2,4},{3,5},{4,2},{5,3},{6,0},{7,1},{8,14},{9,15},{10,... | collective-permute-start | bytes 589832 | tf_op jit(solution)/shard_map/ppermute | solution.py:37
  320.7 16.2 %collective-permute-start.61 = (bf16[4,112,576]{2,1,0:T(8,128)(2,1)}, bf16[4,112,576]{2,1,0:T(8,128)(2,1)S(1)}, u32[]{:S(2)}, u32[]{:S(2)}) collective-permute-start(bf16[4,112,576]{2,1,0:T(8,128)(2,1)} %bitcast.151), channel_id=1, source_target_pairs={{0,1},{1,0},{2,3},{3,2},{4,5},{5,4},{6,7},{7,6},{8,9},{9,8},{10,11... | collective-permute-start | bytes 1548296 | tf_op jit(solution)/shard_map/ppermute | solution.py:32
  334.7 6.0 %collective-permute-start.65 = (bf16[1024,384]{1,0:T(8,128)(2,1)}, bf16[1024,384]{1,0:T(8,128)(2,1)S(1)}, u32[]{:S(2)}, u32[]{:S(2)}) collective-permute-start(bf16[1024,384]{1,0:T(8,128)(2,1)} %bitcast.149), channel_id=1, source_target_pairs={{0,1},{1,0},{2,3},{3,2},{4,5},{5,4},{6,7},{7,6},{8,9},{9,8},{10,11... | collective-permute-start | bytes 2359304 | tf_op jit(solution)/shard_map/ppermute | solution.py:32
  (65 other events, 429.1 us)

commit v2 on v1

--- a/solution.py
+++ b/solution.py
@@ -98,7 +98,11 @@
     return pl.BlockSpec(memory_space=pltpu.SMEM)
 
 
-def pack_kernel(index_ref, small_ref, *refs):
+def small_rows(small):
+    return -(-(8 + small[1].shape[0] + small[2].shape[0]) // 16) * 16
+
+
+def pack_kernel(index_ref, gain_ref, router_ref, bias_ref, *refs):
     group, core = index_ref[0], index_ref[1]
     ins, (qkv_ref, early_ref, late_ref) = refs[:-3], refs[-3:]
     rows = early_ref.shape[1]
@@ -113,8 +117,26 @@
                     :, choice * own : (choice + 1) * own
                 ]
 
-    qkv_ref[shard:] = jnp.zeros((small_ref.shape[0], 3 * own), LOW)
-    qkv_ref[shard:, :shard] = small_ref[...]
+    def widened(rows, count):
+        rows = rows.astype(WIDE)
+        if rows.shape[1] < shard:
+            spare = jnp.zeros((rows.shape[0], shard - rows.shape[1]), WIDE)
+            rows = jnp.concatenate([rows, spare], axis=1)
+        if rows.shape[0] < count:
+            rows = jnp.concatenate([rows, jnp.zeros((count - rows.shape[0], shard), WIDE)])
+        return rows
+
+    experts = router_ref.shape[0]
+    extra = qkv_ref.shape[0] - shard
+    small = jnp.concatenate(
+        [
+            widened(gain_ref[...], 8),
+            router_ref[...].astype(WIDE),
+            widened(bias_ref[...], extra - 8 - experts),
+        ]
+    )
+    qkv_ref[shard:] = jnp.zeros((extra, 3 * own), LOW)
+    qkv_ref[shard:, :shard] = small.astype(LOW)
     here = pl.ds(pl.multiple_of(core * rows, 16), rows)
     early = early_ref.shape[0]
     for i in range(early):
@@ -130,16 +152,16 @@
     return pl.pallas_call(
         pack_kernel,
         out_shape=[
-            jax.ShapeDtypeStruct((shard + small.shape[0], 3 * own), LOW),
+            jax.ShapeDtypeStruct((shard + small_rows(small), 3 * own), LOW),
             jax.ShapeDtypeStruct((early, shard // 2, width), LOW),
             jax.ShapeDtypeStruct((late, shard // 2, width), LOW),
         ],
-        in_specs=[smem()] + vmem(1 + len(weights)),
+        in_specs=[smem()] + vmem(3 + len(weights)),
         out_specs=vmem(3),
         compiler_params=pltpu.CompilerParams(vmem_limit_bytes=VMEM_LIMIT),
         cost_estimate=takes(3),
         name="pack_weights",
-    )(jnp.stack([group, core]).astype(jnp.int32), small, *weights)
+    )(jnp.stack([group, core]).astype(jnp.int32), *small, *weights)
 
 
 def place_qkv_kernel(index_ref, *refs):
@@ -250,35 +272,36 @@
         in_specs=vmem(count + 2),
         out_specs=vmem(count + 1),
         compiler_params=pltpu.CompilerParams(vmem_limit_bytes=VMEM_LIMIT),
-        cost_estimate=takes(8.2),
+        cost_estimate=takes(4.1),
         name="experts",
     )(*pieces, expert_in, expert_out)
     return list(results[:count]), results[count]
 
 
-def expert_grads_kernel(*refs):
-    pieces, (middle, in_ref, out_ref) = refs[:-3], refs[-3:]
+def expert_grads_kernel(count, *refs):
+    pieces, middles, (in_ref, out_ref) = refs[:count], refs[count:-2], refs[-2:]
     width, hidden = in_ref.shape
     rows = jnp.concatenate([piece[...] for piece in pieces])
+    middle = jnp.concatenate([one[...] for one in middles])
     in_ref[...] = dot_tn(rows[:, :width], middle[:, hidden:])
     out_ref[...] = dot_tn(middle[:, :hidden], rows[:, width:])
 
 
-def expert_grads(pieces, middle):
+def expert_grads(pieces, middles):
     width = pieces[0].shape[1] // 2
-    hidden = middle.shape[1] // 2
+    hidden = middles[0].shape[1] // 2
     return pl.pallas_call(
-        expert_grads_kernel,
+        partial(expert_grads_kernel, len(pieces)),
         out_shape=[
             jax.ShapeDtypeStruct((width, hidden), WIDE),
             jax.ShapeDtypeStruct((hidden, width), WIDE),
         ],
-        in_specs=vmem(1 + len(pieces)),
+        in_specs=vmem(len(pieces) + len(middles)),
         out_specs=vmem(2),
         compiler_params=pltpu.CompilerParams(vmem_limit_bytes=VMEM_LIMIT),
         cost_estimate=takes(5.7),
         name="expert_grads",
-    )(*pieces, middle)
+    )(*pieces, *middles)
 
 
 def home_kernel(rests, *refs):
@@ -385,17 +408,14 @@
 
 def collect_kernel(index_ref, *refs):
     pieces, out = refs[:-1], refs[-1]
-    rows = out.shape[2]
     for k in range(len(pieces)):
-        for half in range(out.shape[0]):
-            out[half, index_ref[k]] = pieces[k][half * rows : (half + 1) * rows]
-
-
-def collect(pieces, spots, halves):
-    rows, width = pieces[0].shape
+        out[index_ref[k]] = pieces[k][...]
+
+
+def collect(pieces, spots):
     return pl.pallas_call(
         collect_kernel,
-        out_shape=jax.ShapeDtypeStruct((halves, GROUP, rows // halves, width), LOW),
+        out_shape=jax.ShapeDtypeStruct((GROUP,) + pieces[0].shape, LOW),
         in_specs=[smem()] + vmem(GROUP),
         out_specs=vmem(1)[0],
         cost_estimate=takes(2),
@@ -411,8 +431,18 @@
     return sums[:1]
 
 
-def finish_kernel(index_ref, mine_ref, theirs_ref, weight_ref, gain_ref, *outs):
-    core = index_ref[0]
+def finish_kernel(index_ref, *refs):
+    mine_pieces, their_pieces = refs[:GROUP], refs[GROUP : 2 * GROUP]
+    weight_ref, gain_ref, *outs, mine_ref, theirs_ref = refs[2 * GROUP :]
+    core = index_ref[GROUP]
+    quarter = mine_pieces[0].shape[0] // 2
+    for out, pieces in ((mine_ref, mine_pieces), (theirs_ref, their_pieces)):
+        for k in range(GROUP):
+            for part in range(2):
+                first = (part * GROUP + index_ref[k]) * quarter
+                out[pl.ds(pl.multiple_of(first, 16), quarter)] = pieces[k][
+                    part * quarter : (part + 1) * quarter
+                ]
     half = mine_ref.shape[1]
     shard = outs[0].shape[0]
     wholes, (router_ref, third_ref, second_ref) = outs[:-3], outs[-3:]
@@ -430,18 +460,26 @@
     third_ref[...] = spread[experts : experts + 1, :shard]
 
 
-def finish_weights(mine, theirs, weight, gain, core, experts):
+def finish_weights(mine, theirs, weight, gain, group, core, experts):
     shard, width = weight.shape
+    rows, half = mine[0].shape
     shapes = [(shard, width)] * 5 + [(experts, shard)] + [(1, shard)] * 2
     results = pl.pallas_call(
         finish_kernel,
         out_shape=[jax.ShapeDtypeStruct(shape, WIDE) for shape in shapes],
-        in_specs=[smem()] + vmem(4),
+        in_specs=[smem()] + vmem(2 * GROUP + 2),
         out_specs=vmem(len(shapes)),
+        scratch_shapes=[pltpu.VMEM((GROUP * rows, half), LOW)] * 2,
         compiler_params=pltpu.CompilerParams(vmem_limit_bytes=VMEM_LIMIT),
         cost_estimate=takes(3),
         name="finish_weights",
-    )(core.reshape(1).astype(jnp.int32), mine, theirs, weight, gain[None])
+    )(
+        jnp.stack([group ^ k for k in range(GROUP)] + [core]).astype(jnp.int32),
+        *mine,
+        *theirs,
+        weight,
+        gain[None],
+    )
     return list(results[:5]) + [results[5].T] + [one[0] for one in results[6:]]
 
 
@@ -595,11 +633,16 @@
             scores = chunk_scores(
                 query_head, key_ref, lanes, first, chunk, head, step, kind_ref, tile_ref
             )
+            values = value_ref[pl.ds(first, chunk), lanes[0] : lanes[1]]
+            if key_count == chunk:
+                top = jnp.max(scores, axis=1, keepdims=True)
+                weights = jnp.exp(scores - top)
+                total = jnp.sum(weights, axis=1, keepdims=True)
+                return top, total, jnp.dot(weights.astype(LOW), values, preferred_element_type=WIDE)
             new_top = jnp.maximum(top, jnp.max(scores, axis=1, keepdims=True))
             weights = jnp.exp(scores - new_top)
             shrink = jnp.exp(top - new_top)
             total = total * shrink + jnp.sum(weights, axis=1, keepdims=True)
-            values = value_ref[pl.ds(first, chunk), lanes[0] : lanes[1]]
             mixed = mixed * shrink + jnp.dot(
                 weights.astype(LOW), values, preferred_element_type=WIDE
             )
@@ -703,7 +746,7 @@
     value_ref[own:] = rest_ref[:, width:]
 
 
-def self_forward_kernel(kind_ref, tile_ref, query_ref, own_ref, rest_ref, *refs):
+def self_forward_kernel(first, kind_ref, tile_ref, query_ref, own_ref, rest_ref, *refs):
     outs, log_ref, out_ref, key_ref, value_ref = refs[:-4], refs[-4], refs[-3], refs[-2], refs[-1]
 
     @pl.when(pl.program_id(0) == 0)
@@ -711,7 +754,7 @@
         load_keys(own_ref, rest_ref, key_ref, value_ref)
 
     forward_body(
-        pl.program_id(0), kind_ref, tile_ref, query_ref, key_ref, value_ref, out_ref, log_ref
+        first + pl.program_id(0), kind_ref, tile_ref, query_ref, key_ref, value_ref, out_ref, log_ref
     )
     for k in range(len(outs)):
 
@@ -794,32 +837,33 @@
     return pl.BlockSpec((rows, 128), lambda i, *rest: (0, i))
 
 
-def self_forward(kinds, tiles, queries, own, rest):
-    count, width = queries.shape
+def self_forward(first, last, kinds, tiles, queries, own, rest):
+    width = queries.shape[1]
     rows = 2 * HEAD_DIM
     keys = own.shape[0] + rest.shape[0]
+    blocks = last - first
     return pl.pallas_call(
-        self_forward_kernel,
+        partial(self_forward_kernel, first),
         grid_spec=pltpu.PrefetchScalarGridSpec(
             num_scalar_prefetch=1,
-            grid=(count // rows,),
+            grid=(blocks,),
             in_specs=[
                 whole_block(tiles.shape),
-                row_block(rows, width),
+                pl.BlockSpec((rows, width), lambda i, *refs: (first + i, 0)),
                 whole_block(own.shape),
                 whole_block(rest.shape),
             ],
-            out_specs=[whole_block((rows, width))] * (count // rows) + [row_block(rows, 128)],
+            out_specs=[whole_block((rows, width))] * blocks + [row_block(rows, 128)],
             scratch_shapes=[
                 pltpu.VMEM((rows, width), LOW),
                 pltpu.VMEM((keys, width), LOW),
                 pltpu.VMEM((keys, width), LOW),
             ],
         ),
-        out_shape=[jax.ShapeDtypeStruct((rows, width), LOW)] * (count // rows)
-        + [jax.ShapeDtypeStruct((count, 128), WIDE)],
-        compiler_params=pltpu.CompilerParams(vmem_limit_bytes=VMEM_LIMIT),
-        cost_estimate=takes(8.5),
+        out_shape=[jax.ShapeDtypeStruct((rows, width), LOW)] * blocks
+        + [jax.ShapeDtypeStruct((blocks * rows, 128), WIDE)],
+        compiler_params=pltpu.CompilerParams(vmem_limit_bytes=VMEM_LIMIT),
+        cost_estimate=takes(2.2 * blocks),
         name="self_forward",
     )(kinds, tiles, queries, own, rest)
 
@@ -868,12 +912,11 @@
     key_count = keys.shape[0]
     return pl.pallas_call(
         cross_forward_kernel,
-        grid=(width // 128,),
-        in_specs=[lane_block(count), lane_block(key_count), lane_block(key_count)],
-        out_specs=[lane_block(count), lane_block(count)],
+        in_specs=vmem(3),
+        out_specs=vmem(2),
         out_shape=[
             jax.ShapeDtypeStruct((count, width), LOW),
-            jax.ShapeDtypeStruct((count, width), WIDE),
+            jax.ShapeDtypeStruct((count, 128), WIDE),
         ],
         compiler_params=pltpu.CompilerParams(vmem_limit_bytes=VMEM_LIMIT),
         cost_estimate=takes(6.6),
@@ -886,10 +929,9 @@
     key_count = keys.shape[0]
     return pl.pallas_call(
         cross_backward_kernel,
-        grid=(width // 128,),
-        in_specs=[lane_block(count)] * 3 + [lane_block(key_count)] * 2,
-        out_specs=[lane_block(count), lane_block(key_count), lane_block(key_count)],
-        scratch_shapes=[pltpu.VMEM((key_count, 128), WIDE), pltpu.VMEM((key_count, 128), WIDE)],
+        in_specs=vmem(5),
+        out_specs=vmem(3),
+        scratch_shapes=[pltpu.VMEM(keys.shape, WIDE), pltpu.VMEM(keys.shape, WIDE)],
         out_shape=[
             jax.ShapeDtypeStruct((count, width), LOW),
             jax.ShapeDtypeStruct(keys.shape, LOW),
@@ -1017,17 +1059,9 @@
     hidden_low = tokens.reshape(span, width)
     upstream = cotangent.reshape(span, width).astype(WIDE)
 
-    small = jnp.concatenate(
-        [
-            first_gain[None],
-            second_gain[None],
-            third_gain[None],
-            router_weight.T,
-            jnp.pad(position_bias.reshape(1, -1), ((0, 0), (0, shard - position_bias.size))),
-        ]
-    )
-    small = jnp.pad(small, ((0, -small.shape[0] % 16), (0, 0)))
-    extra = small.shape[0]
+    gains = jnp.concatenate([first_gain, second_gain, third_gain]).reshape(3, shard)
+    small = (gains, router_weight.T, position_bias)
+    extra = small_rows(small)
     qkv_payload, early, late = pack_weights(
         small,
         (
@@ -1055,8 +1089,9 @@
     gain_one = small_full[:, 0].reshape(width).astype(WIDE)
     gain_two = small_full[:, 1].reshape(width).astype(WIDE)
     gain_three = small_full[:, 2].reshape(width).astype(WIDE)
-    router_full = small_full[:, 3 : 3 + experts].transpose(1, 0, 2).reshape(experts, width)
-    bias_full = small_full[:, 3 + experts, : position_bias.size].reshape(BUCKETS, HEADS)
+    router_full = small_full[:, 8 : 8 + experts].transpose(1, 0, 2).reshape(experts, width)
+    bias_full = small_full[:, 8 + experts : 8 + experts + position_bias.shape[0], :HEADS]
+    bias_full = bias_full.reshape(BUCKETS, HEADS)
 
     slots = jnp.arange(GROUP, dtype=jnp.int32)
     key_devices = (
@@ -1117,11 +1152,20 @@
         pairs_rest = jnp.concatenate(
             [pairs_rest] + [shift_rest(near, r) for r in range(1, rests)]
         )
-    *attended_own, self_logs = self_forward(kinds, tiles, queries, pairs_own, pairs_rest)
-    attended_own, early_xy, late_x, encoder_pieces = tie(
-        attended_own, early_xy, late_x, encoder_pieces
-    )
-    attended = [attended_own[0]] + [swap_group(attended_own[k], k) for k in range(1, GROUP)]
+    half_group = GROUP // 2
+    *far, far_logs = self_forward(
+        half_group, GROUP, kinds, tiles, queries, pairs_own, pairs_rest
+    )
+    pairs_own, *far = tie(pairs_own, *far)
+    far = [swap_group(piece, half_group + k) for k, piece in enumerate(far)]
+    *attended, near_logs = self_forward(
+        0, half_group, kinds, tiles, queries, pairs_own, pairs_rest
+    )
+    attended, far, early_xy, late_x, encoder_pieces = tie(
+        attended, far, early_xy, late_x, encoder_pieces
+    )
+    self_logs = jnp.concatenate([near_logs, far_logs])
+    attended = [attended[0]] + [swap_group(attended[k], k) for k in range(1, half_group)] + far
     late_xy = swap_fsdp(late_x, 2)
     early_mine = stack_pieces((early, early_x, early_y, early_xy), 1, f_index, group)
     early_theirs = swap_core(early_mine)
@@ -1166,8 +1210,12 @@
     arrived = jnp.concatenate(
         [near[:, 0]] + [swap_group(near[:, k], k) for k in range(1, GROUP)], axis=1
     ).reshape(slot_rows, 2 * width)
-    arrivals = tie(*gather_fsdp(arrived))
-    answers, middle = run_experts(arrivals, expert_in[0], expert_out[0])
+    arrivals = list(gather_fsdp(arrived))
+    near_count = fsdp_size // 2
+    answers, middle = run_experts(arrivals[:near_count], expert_in[0], expert_out[0])
+    answers, middle, arrivals[near_count:] = tie(answers, middle, arrivals[near_count:])
+    more_answers, more_middle = run_experts(arrivals[near_count:], expert_in[0], expert_out[0])
+    answers = answers + more_answers
     answers = tie(answers[0], *[swap_fsdp(answers[k], k) for k in range(1, fsdp_size)])
     answers = sum_home(answers, rests)
     near = [answers[0]] + [swap_group(answers[k], k) for k in range(1, GROUP)]
@@ -1178,7 +1226,7 @@
     both = dot(placing, home).astype(LOW)
     both = both[:span].astype(WIDE) + swap_core(both[span:]).astype(WIDE)
     moe_rows, dispatch_grad = both[:, :width], both[:, width:]
-    grad_expert_in, grad_expert_out = expert_grads(arrivals, middle)
+    grad_expert_in, grad_expert_out = expert_grads(arrivals, (middle, more_middle))
     grad_expert_in, grad_expert_out = grad_expert_in[None], grad_expert_out[None]
 
     mixed_out = (second_sum + gate_value * moe_rows).astype(LOW).reshape(tokens.shape)
@@ -1226,15 +1274,15 @@
     up_own = jnp.concatenate(up_pieces)
     middle = keep.shape[1] // 2
     top = [add_low(keep[k, :middle], received[k, :middle]) for k in range(fsdp_size)]
-    bottom = [add_low(keep[k, middle:], received[k, middle:]) for k in range(fsdp_size)]
-    up_own, top[1:], bottom[1:] = tie(up_own, top[1:], bottom[1:])
+    up_own, top[1:] = tie(up_own, top[1:])
     top = [top[0]] + [swap_fsdp(top[k], k) for k in range(1, fsdp_size)]
     query_low, pair_own, pair_rest, bias_parts = self_backward(
         0, own_count // span, kinds, tiles, queries, up_own, self_logs, pairs_own, pairs_rest
     )
-    query_low, pair_own, pair_rest, bias_parts, top, bottom = tie(
-        query_low, pair_own, pair_rest, bias_parts, top, bottom
-    )
+    query_low, pair_own, pair_rest, bias_parts, top, keep, received = tie(
+        query_low, pair_own, pair_rest, bias_parts, top, keep, received
+    )
+    bottom = [add_low(keep[k, middle:], received[k, middle:]) for k in range(fsdp_size)]
     bottom = [bottom[0]] + [swap_fsdp(bottom[k], k) for k in range(1, fsdp_size)]
     if rests > 1:
         near = jnp.concatenate([pair_own, pair_rest[:own_count]]).astype(WIDE)
@@ -1250,20 +1298,22 @@
     qkv_send, bottom, bias_parts, one_parts[1] = tie(
         swap_core(qkv_send), bottom, bias_parts, one_parts[1]
     )
-    quarters = sum_quarters(top, bottom, group)
+    qkv_send, *quarters = tie(qkv_send, *sum_quarters(top, bottom, group))
     quarters = [quarters[0]] + [swap_group(quarters[k], k) for k in range(1, GROUP)]
 
     table = jnp.pad(bucket_sums(bias_parts, lower_bounds).T, ((0, 0), (0, 128 - OWN_HEADS)))
     qkv_parts = add_qkv(qkv_keep, qkv_send, table, f_index)
     qkv_parts = [qkv_parts[0]] + [swap_fsdp(qkv_parts[k], k) for k in range(1, fsdp_size)]
-    qkv_parts, one_parts, quarters = tie(qkv_parts, one_parts, quarters)
+    qkv_parts, one_parts, quarters, grad_expert_in, grad_expert_out = tie(
+        qkv_parts, one_parts, quarters, grad_expert_in, grad_expert_out
+    )
     dense_shard = sum_rest(sum_low(quarters[0], quarters[1:])).astype(LOW)
     one_grad = sum(one.astype(WIDE) for one in one_parts)
     tokens_grad = first_grad + norm_grad(hidden, rms_of(hidden), gain_one, one_grad)
     tokens_grad = tokens_grad.reshape(tokens.shape)
     qkv_shard = sum_rest(sum_low(qkv_parts[0], qkv_parts[1:])).astype(LOW)
     spots = [group ^ k for k in range(GROUP)]
-    qkv_mine = collect(gather_group(qkv_shard), spots, 1)[0]
+    qkv_mine = collect(gather_group(qkv_shard), spots)
     query_total, key_total, value_total, bias_total, grad_gain_one = finish_qkv(
         qkv_mine,
         swap_core(qkv_mine),
@@ -1272,7 +1322,9 @@
         core,
         position_bias.shape,
     )
-    dense_mine = collect(gather_group(dense_shard), spots, 2).reshape(-1, half_width)
+    dense_pieces, query_total, tokens_grad = tie(
+        gather_group(dense_shard), query_total, tokens_grad
+    )
     (
         cross_o_total,
         cross_q_total,
@@ -1282,7 +1334,15 @@
         grad_router,
         grad_gain_three,
         grad_gain_two,
-    ) = finish_weights(dense_mine, swap_core(dense_mine), cross_query, second_gain, core, experts)
+    ) = finish_weights(
+        dense_pieces,
+        [swap_core(piece) for piece in dense_pieces],
+        cross_query,
+        second_gain,
+        group,
+        core,
+        experts,
+    )
 
     return (
         mixed_out,

time: 347 us -> 344 us (level); the launches traced: 345 us -> 338 us
  local copies, waits for them, and re-layouts: 20.7 us -> 15.2 us
  starting transfers between devices: 78.8 us -> 74.4 us
    ppermute x24, waiting for transfers between devices: 59.8 us -> 53.2 us  [swap_fsdp(): return lax.ppermute(rows, 'fsdp', [(i, i ^ k) for i in range(size)])]
    ppermute x12 -> x15, starting transfers between devices: 27.1 us -> 23.1 us  [swap_core(): return lax.ppermute(rows, 'ctx', [(i, i ^ 1) for i in range(size)])]
    unnamed x130 -> x133, local copies, waits for them, and re-layouts: 12.6 us -> 9.67 us
    pallas_call x1 -> x2, Pallas kernels: 8.31 us -> 11 us  [run_experts(): pl.pallas_call(expert_kernel, out_shape=[jax.ShapeDtypeStruct((rows, 2 *...]
  transfers between devices with their start and end apart: 66 -> 69, of which waited for: 30 -> 28; matrix products, arithmetic and copies ran while one was open for 8% -> 9% of each run, Pallas kernels for 19% -> 23%
where the time goes in v2:
time: 344 us; the launch traced here: 338 us
  waiting for transfers between devices  108 us (31%)
  Pallas kernels  103 us (30%)
  starting transfers between devices  74.4 us (22%)
  matrix products  18.7 us (5%)
  other arithmetic  17.1 us (5%)
  local copies, waits for them, and re-layouts  15.2 us (4%)
    ppermute x24, waiting for transfers between devices, swap_fsdp(): return lax.ppermute(rows, 'fsdp', [(i, i ^ k) for i in range(size)])  53.2 us
    ppermute x30, waiting for transfers between devices, swap_group(): return lax.ppermute(rows, 'ctx', [(i, i ^ 2 * k) for i in range(size)])  50.9 us
    ppermute x30, starting transfers between devices, swap_group(): return lax.ppermute(rows, 'ctx', [(i, i ^ 2 * k) for i in range(size)])  31 us
    ppermute x15, starting transfers between devices, swap_core(): return lax.ppermute(rows, 'ctx', [(i, i ^ 1) for i in range(size)])  23.1 us
    ppermute x24, starting transfers between devices, swap_fsdp(): return lax.ppermute(rows, 'fsdp', [(i, i ^ k) for i in range(size)])  20.2 us
    dot_general x10, matrix products, dot(): return jnp.dot(left, right, preferred_element_type=WIDE)  14.2 us
    pallas_call x1, Pallas kernels, self_backward(): pl.pallas_call(partial(self_backward_kernel, first, done), grid_spec=pltp...  12.6 us
    pallas_call x2, Pallas kernels, self_forward(): pl.pallas_call(partial(self_forward_kernel, first), grid_spec=pltpu.Prefe...  11.5 us
  transfers between devices with their start and end apart: 69, of which 28 were waited for; matrix products, arithmetic and copies ran while one was open for 9% of the time, Pallas kernels for 23%

profile of v2, /device:TPU:13, one launch (start us, length us, event | category | flops | bytes accessed | tf_op | source)
XLA Modules:
  0.0 338.0 jit_solution(17176319430323325526)
XLA Ops:
  0.9 2.3 collective-permute-start.1
  5.2 2.8 pack_weights.1
  13.9 7.3 %collective-permute-done.2 = bf16[128,768]{1,0:T(8,128)(2,1)S(1)} collective-permute-done((bf16[128,768]{1,0:T(8,128)(2,1)S(1)}, bf16[128,768]{1,0:T(8,128)(2,1)S(1)}, u32[]{:S(2)}, u32[]{:S(2)}) %collective-permute-start.2) | collective-permute-done | bytes 196640 | tf_op jit(solution)/shard_map/ppermute | solution.py:37
  22.1 2.4 place_qkv.1
  32.3 2.6 collective-permute-start.6
  35.6 2.8 bias_tiles.1.tile_ref
  42.4 5.7 %self_forward.2 = (bf16[128,192]{1,0:T(8,128)(2,1)}, bf16[128,192]{1,0:T(8,128)(2,1)}, f32[256,128]{1,0:T(8,128)}) custom-call(s32[8,16]{1,0:T(8,128)} %clamp_add_fusion.kind_ref, f32[2,3,5,64,128]{4,3,2,1,0:T(8,128)} %bias_tiles.1.tile_ref, bf16[512,192]{1,0:T(8,128)(2,1)} %convolution_convert_fusion.5.query_ref, bf16[512,384]{1,0:T(8,128)(2,1)} %copy-done.37, ...), custom_call_target="tpu_custom_call" | custom-call | flops 4400000000 | bytes 15400000 | tf_op jit(solution)/shard_map/self_forward/pallas_call | solution.py:845
  49.2 2.3 collective-permute-start.10
  51.5 5.8 %self_forward.3 = (bf16[128,192]{1,0:T(8,128)(2,1)}, bf16[128,192]{1,0:T(8,128)(2,1)}, f32[256,128]{1,0:T(8,128)}) custom-call(s32[8,16]{1,0:T(8,128)} %clamp_add_fusion.kind_ref, f32[2,3,5,64,128]{4,3,2,1,0:T(8,128)} %bias_tiles.1.tile_ref, bf16[512,192]{1,0:T(8,128)(2,1)} %convolution_convert_fusion.5.query_ref, bf16[512,384]{1,0:T(8,128)(2,1)} %copy-done.37, ...), custom_call_target="tpu_custom_call" | custom-call | flops 4400000000 | bytes 15400000 | tf_op jit(solution)/shard_map/self_forward/pallas_call | solution.py:845
  58.2 2.8 stack_pieces.2.mine_ref
  61.0 1.4 collective-permute-start.17
  64.1 1.7 collective-permute-done.16
  66.7 4.0 %weave_halves.2 = (bf16[4,2,96,768]{3,2,1,0:T(8,128)(2,1)}, bf16[4,2,96,768]{3,2,1,0:T(8,128)(2,1)}, bf16[4,2,96,768]{3,2,1,0:T(8,128)(2,1)}) custom-call(s32[1]{0:T(128)} %bitcast.2.index_ref, bf16[3,4,96,768]{3,2,1,0:T(8,128)(2,1)} %stack_pieces.2.mine_ref, bf16[3,4,96,768]{3,2,1,0:T(8,128)(2,1)} %collective-permute-done.17.theirs_ref), custom_call_target="tpu_custom_call" | custom-call | flops 4000000000 | bytes 14000000 | tf_op jit(solution)/shard_map/weave_halves/pallas_call | solution.py:229
  70.9 1.8 multiply_reduce_fusion.4
  72.8 5.8 %collective-permute-done.19.refs_3_ = bf16[2,96,768]{2,1,0:T(8,128)(2,1)S(1)} collective-permute-done((bf16[2,96,768]{2,1,0:T(8,128)(2,1)S(1)}, bf16[2,96,768]{2,1,0:T(8,128)(2,1)S(1)}, u32[]{:S(2)}, u32[]{:S(2)}) %collective-permute-start.19) | collective-permute-done | bytes 294944 | tf_op jit(solution)/shard_map/ppermute | solution.py:27
  79.4 2.3 stack_pieces.3.mine_ref
  83.6 3.2 convolution_convert_fusion.2.value_ref
  86.8 1.7 convolution_convert_fusion.3.key_ref
  88.5 3.2 weave_halves.3
  91.7 2.3 convolution_convert_fusion.8.query_ref
  94.0 5.5 %cross_forward.1 = (bf16[128,768]{1,0:T(8,128)(2,1)}, f32[128,128]{1,0:T(8,128)}) custom-call(bf16[128,768]{1,0:T(8,128)(2,1)} %convolution_convert_fusion.8.query_ref, bf16[512,768]{1,0:T(8,128)(2,1)} %convolution_convert_fusion.3.key_ref, bf16[512,768]{1,0:T(8,128)(2,1)} %convolution_convert_fusion.2.value_ref), custom_call_target="tpu_custom_call" | custom-call | flops 6600000000 | bytes 23100000 | tf_op jit(solution)/shard_map/cross_forward/pallas_call | solution.py:913
  99.5 1.4 multiply_reduce_fusion.3
  101.5 1.7 collective-permute-done.23
  104.5 2.6 collective-permute-start.25
  107.1 6.2 %collective-permute-done.26 = bf16[1,40,1536]{2,1,0:T(8,128)(2,1)S(1)} collective-permute-done((bf16[1,40,1536]{2,1,0:T(8,128)(2,1)S(1)}, bf16[1,40,1536]{2,1,0:T(8,128)(2,1)S(1)}, u32[]{:S(2)}, u32[]{:S(2)}) %collective-permute-start.26) | collective-permute-done | bytes 122912 | tf_op jit(solution)/shard_map/ppermute | solution.py:37
  113.3 1.7 collective-permute-done.25
  116.2 1.6 collective-permute-start.29
  117.8 9.1 %collective-permute-done.27.refs_1_ = bf16[160,1536]{1,0:T(8,128)(2,1)S(1)} collective-permute-done((bf16[160,1536]{1,0:T(8,128)(2,1)S(1)}, bf16[160,1536]{1,0:T(8,128)(2,1)S(1)}, u32[]{:S(2)}, u32[]{:S(2)}) %collective-permute-start.27) | collective-permute-done | bytes 491552 | tf_op jit(solution)/shard_map/ppermute | solution.py:27
  127.7 5.5 %experts.2 = (bf16[160,1536]{1,0:T(8,128)(2,1)}, bf16[160,1536]{1,0:T(8,128)(2,1)}, bf16[320,1536]{1,0:T(8,128)(2,1)}) custom-call(bf16[160,1536]{1,0:T(8,128)(2,1)} %copy-done.14, bf16[160,1536]{1,0:T(8,128)(2,1)} %copy-done.30, bf16[768,768]{1,0:T(8,128)(2,1)} %bitcast.147, bf16[768,768]{1,0:T(8,128)(2,1)} %bitcast.149), custom_call_target="tpu_custom_call" | custom-call | flops 4100000000 | bytes 14349999 | tf_op jit(solution)/shard_map/experts/pallas_call | solution.py:268
  133.2 4.6 %collective-permute-done.29.refs_1_.refs_3_ = bf16[160,1536]{1,0:T(8,128)(2,1)S(1)} collective-permute-done((bf16[160,1536]{1,0:T(8,128)(2,1)S(1)}, bf16[160,1536]{1,0:T(8,128)(2,1)S(1)}, u32[]{:S(2)}, u32[]{:S(2)}) %collective-permute-start.29) | collective-permute-done | bytes 491552 | tf_op jit(solution)/shard_map/ppermute | solution.py:27
  138.5 5.5 %experts.3 = (bf16[160,1536]{1,0:T(8,128)(2,1)}, bf16[160,1536]{1,0:T(8,128)(2,1)}, bf16[320,1536]{1,0:T(8,128)(2,1)}) custom-call(bf16[160,1536]{1,0:T(8,128)(2,1)} %copy-done.31, bf16[160,1536]{1,0:T(8,128)(2,1)} %copy-done.32, bf16[768,768]{1,0:T(8,128)(2,1)} %bitcast.148, bf16[768,768]{1,0:T(8,128)(2,1)} %bitcast.150), custom_call_target="tpu_custom_call" | custom-call | flops 4100000000 | bytes 14349999 | tf_op jit(solution)/shard_map/experts/pallas_call | solution.py:268
  145.9 2.7 collective-permute-done.30.refs_1_
  148.5 16.6 %collective-permute-done.31.refs_2_ = bf16[160,1536]{1,0:T(8,128)(2,1)S(1)} collective-permute-done((bf16[160,1536]{1,0:T(8,128)(2,1)}, bf16[160,1536]{1,0:T(8,128)(2,1)S(1)}, u32[]{:S(2)}, u32[]{:S(2)}) %collective-permute-start.31) | collective-permute-done | bytes 491552 | tf_op jit(solution)/shard_map/ppermute | solution.py:27
  166.7 2.4 sum_home.1
  169.7 4.1 %collective-permute-start.34 = (bf16[40,1536]{1,0:T(8,128)(2,1)}, bf16[40,1536]{1,0:T(8,128)(2,1)S(1)}, u32[]{:S(2)}, u32[]{:S(2)}) collective-permute-start(bf16[40,1536]{1,0:T(8,128)(2,1)} %get-tuple-element.257), channel_id=1, source_target_pairs={{0,4},{1,5},{2,6},{3,7},{4,0},{5,1},{6,2},{7,3},{8,12},{9,13},{10,... | collective-permute-start | bytes 368648 | tf_op jit(solution)/shard_map/ppermute | solution.py:37
  173.8 8.0 %collective-permute-done.34 = bf16[40,1536]{1,0:T(8,128)(2,1)S(1)} collective-permute-done((bf16[40,1536]{1,0:T(8,128)(2,1)}, bf16[40,1536]{1,0:T(8,128)(2,1)S(1)}, u32[]{:S(2)}, u32[]{:S(2)}) %collective-permute-start.34) | collective-permute-done | bytes 122912 | tf_op jit(solution)/shard_map/ppermute | solution.py:37
  181.9 1.5 convolution_convert_fusion
  183.4 1.8 collective-permute-start.36
  189.4 7.9 %cross_backward.1 = (bf16[128,768]{1,0:T(8,128)(2,1)}, bf16[512,768]{1,0:T(8,128)(2,1)}, bf16[512,768]{1,0:T(8,128)(2,1)}) custom-call(bf16[128,768]{1,0:T(8,128)(2,1)} %convolution_convert_fusion.8.query_ref, bf16[128,768]{1,0:T(8,128)(2,1)} %convolution_convert_fusion.7.up_ref, f32[128,128]{1,0:T(8,128)} %get-tuple-element.259.log_ref, ...), custom_call_target="tpu_custom_call" | custom-call | flops 8200000000 | bytes 28700000 | tf_op jit(solution)/shard_map/cross_backward/pallas_call | solution.py:930
  197.3 1.6 multiply_reduce_fusion.1
  201.4 7.6 %weight_grads.1 = (bf16[4,1024,384]{2,1,0:T(8,128)(2,1)}, bf16[4,1024,384]{2,1,0:T(8,128)(2,1)}) custom-call(s32[3]{0:T(128)} %pad_add_fusion.3.index_ref, bf16[128,768]{1,0:T(8,128)(2,1)} %get-tuple-element.239.refs_0_, bf16[128,768]{1,0:T(8,128)(2,1)} %copy-done.11, bf16[128,768]{1,0:T(8,128)(2,1)} %copy-done.9, ...), custom_call_target="tpu_custom_call" | custom-call | flops 7500000256 | bytes 26250000 | tf_op jit(solution)/shard_map/weight_grads/pallas_call | solution.py:360
  210.1 2.6 collective-permute-start.37
  215.0 1.8 collective-permute-done.38
  216.8 3.4 %collective-permute-done.39 = bf16[128,192]{1,0:T(8,128)(2,1)S(1)} collective-permute-done((bf16[128,192]{1,0:T(8,128)(2,1)S(1)}, bf16[128,192]{1,0:T(8,128)(2,1)S(1)}, u32[]{:S(2)}, u32[]{:S(2)}) %collective-permute-start.39) | collective-permute-done | bytes 49184 | tf_op jit(solution)/shard_map/ppermute | solution.py:37
  220.3 2.5 fusion.30
  226.1 12.6 %self_backward.1 = (bf16[512,192]{1,0:T(8,128)(2,1)}, bf16[512,384]{1,0:T(8,128)(2,1)}, bf16[512,384]{1,0:T(8,128)(2,1)}, f32[2,3,5,64,128]{4,3,2,1,0:T(8,128)}) custom-call(s32[8,16]{1,0:T(8,128)} %clamp_add_fusion.kind_ref, f32[2,3,5,64,128]{4,3,2,1,0:T(8,128)} %bias_tiles.1.tile_ref, bf16[512,192]{1,0:T(8,128)(2,1)} %convolution_convert_fusion.5.query_ref, ...), custom_call_target="tpu_custom_call" | custom-call | flops 8999999488 | bytes 31500000 | tf_op jit(solution)/shard_map/self_backward/pallas_call | solution.py:885
  238.8 3.9 %collective-permute-done.43.refs_3_ = bf16[512,384]{1,0:T(8,128)(2,1)} collective-permute-done((bf16[512,384]{1,0:T(8,128)(2,1)S(1)}, bf16[512,384]{1,0:T(8,128)(2,1)}, u32[]{:S(2)}, u32[]{:S(2)}) %collective-permute-start.43) | collective-permute-done | bytes 393248 | tf_op jit(solution)/shard_map/ppermute | solution.py:27
  242.7 1.9 collective-permute-start.44
  248.5 4.7 %key_grads.1 = (bf16[128,768]{1,0:T(8,128)(2,1)}, bf16[128,768]{1,0:T(8,128)(2,1)}, bf16[128,768]{1,0:T(8,128)(2,1)}, bf16[128,768]{1,0:T(8,128)(2,1)}, bf16[4,9...) custom-call(s32[2]{0:T(128)} %pad_add_fusion.2.index_ref, bf16[512,768]{1,0:T(8,128)(2,1)} %copy-done.4, ...), custom_call_target="tpu_custom_call" | custom-call | flops 100000000 | bytes 350000 | tf_op jit(solution)/shard_map/key_grads/pallas_call | solution.py:506
  255.1 1.9 collective-permute-done.46.refs_5_
  258.3 7.9 %collective-permute-done.48.refs_7_ = bf16[512,384]{1,0:T(8,128)(2,1)} collective-permute-done((bf16[512,384]{1,0:T(8,128)(2,1)S(1)}, bf16[512,384]{1,0:T(8,128)(2,1)}, u32[]{:S(2)}, u32[]{:S(2)}) %collective-permute-start.48) | collective-permute-done | bytes 393248 | tf_op jit(solution)/shard_map/ppermute | solution.py:27
  266.5 2.9 sum_quarters.1
  270.9 2.1 add_qkv.1
  274.8 1.4 collective-permute-start.52
  276.2 2.0 collective-permute-start.56
  278.9 5.7 %expert_grads.1 = (f32[768,768]{1,0:T(8,128)}, f32[768,768]{1,0:T(8,128)}) custom-call(bf16[160,1536]{1,0:T(8,128)(2,1)} %copy-done.14, bf16[160,1536]{1,0:T(8,128)(2,1)} %copy-done.30, bf16[160,1536]{1,0:T(8,128)(2,1)} %copy-done.31, bf16[160,1536]{1,0:T(8,128)(2,1)} %copy-done.32, bf16[320,1536]{1,0:T(8,128)(2,1)} %get-tuple-element.318.refs_4_, ...), custom_call_target="tpu_custom_call" | custom-call | flops 5699999744 | bytes 19950000 | tf_op jit(solution)/shard_map/expert_grads/pallas_call | solution.py:293
  285.4 9.6 %collective-permute-done.57 = bf16[256,384]{1,0:T(8,128)(2,1)S(1)} collective-permute-done((bf16[256,384]{1,0:T(8,128)(2,1)S(1)}, bf16[256,384]{1,0:T(8,128)(2,1)S(1)}, u32[]{:S(2)}, u32[]{:S(2)}) %collective-permute-start.57) | collective-permute-done | bytes 196640 | tf_op jit(solution)/shard_map/ppermute | solution.py:37
  295.1 2.3 collective-permute-start.62
  300.6 1.9 collective-permute-done.62.refs_2_
  302.5 8.1 %collective-permute-done.63.refs_3_ = bf16[112,576]{1,0:T(8,128)(2,1)S(1)} collective-permute-done((bf16[112,576]{1,0:T(8,128)(2,1)S(1)}, bf16[112,576]{1,0:T(8,128)(2,1)S(1)}, u32[]{:S(2)}, u32[]{:S(2)}) %collective-permute-start.63) | collective-permute-done | bytes 129056 | tf_op jit(solution)/shard_map/ppermute | solution.py:37
  311.2 2.0 collect.1.mine_ref
  313.2 11.3 %collective-permute-start.64 = (bf16[4,112,576]{2,1,0:T(8,128)(2,1)}, bf16[4,112,576]{2,1,0:T(8,128)(2,1)S(1)}, u32[]{:S(2)}, u32[]{:S(2)}) collective-permute-start(bf16[4,112,576]{2,1,0:T(8,128)(2,1)} %collect.1.mine_ref), channel_id=1, source_target_pairs={{0,1},{1,0},{2,3},{3,2},{4,5},{5,4},{6,7},{7,6},{8,9},{9,8},{10,11... | collective-permute-start | bytes 1548296 | tf_op jit(solution)/shard_map/ppermute | solution.py:32
  327.1 2.9 qkv_finish.1
  333.9 3.6 %finish_weights.1 = (f32[192,768]{1,0:T(8,128)}, f32[192,768]{1,0:T(8,128)}, f32[192,768]{1,0:T(8,128)}, f32[192,768]{1,0:T(8,128)}, f32[192,768]{1,0:T(8,128)},...) custom-call(s32[5]{0:T(128)} %stack.108.index_ref, bf16[256,384]{1,0:T(8,128)(2,1)} %copy-done.17, ...), custom_call_target="tpu_custom_call" | custom-call | flops 3000000000 | bytes 10500000 | tf_op jit(solution)/shard_map/finish_weights/pallas_call | solution.py:467
  (332 shorter events, 73.6 us)
Async XLA Ops:
  0.7 12.5 %collective-permute-start = (bf16[128,768]{1,0:T(8,128)(2,1)}, bf16[128,768]{1,0:T(8,128)(2,1)S(1)}, u32[]{:S(2)}, u32[]{:S(2)}) collective-permute-start(bf16[128,768]{1,0:T(8,128)(2,1)} %bitcast.122), channel_id=1, source_target_pairs={{0,2},{1,3},{2,0},{3,1},{4,6},{5,7},{6,4},{7,5},{8,10},{9,11},{10,... | collective-permute-start | bytes 589832 | tf_op jit(solution)/shard_map/ppermute | solution.py:37
  0.9 13.0 %collective-permute-start.1 = (bf16[128,768]{1,0:T(8,128)(2,1)}, bf16[128,768]{1,0:T(8,128)(2,1)S(1)}, u32[]{:S(2)}, u32[]{:S(2)}) collective-permute-start(bf16[128,768]{1,0:T(8,128)(2,1)} %bitcast.123), channel_id=1, source_target_pairs={{0,4},{1,5},{2,6},{3,7},{4,0},{5,1},{6,2},{7,3},{8,12},{9,13},{10,... | collective-permute-start | bytes 589832 | tf_op jit(solution)/shard_map/ppermute | solution.py:37
  8.0 13.2 %collective-permute-start.3 = (bf16[224,576]{1,0:T(8,128)(2,1)}, bf16[224,576]{1,0:T(8,128)(2,1)S(1)}, u32[]{:S(2)}, u32[]{:S(2)}) collective-permute-start(bf16[224,576]{1,0:T(8,128)(2,1)} %get-tuple-element.191.refs_0_), channel_id=1, source_target_pairs={{0,8},{8,0},{16,24},{24,16},{1,9},{9,1},{17,25},{25,17},{2,10},{10... | collective-permute-start | bytes 774152 | tf_op jit(solution)/shard_map/ppermute | solution.py:27
  9.2 12.0 %collective-permute-start.4 = (bf16[224,576]{1,0:T(8,128)(2,1)}, bf16[224,576]{1,0:T(8,128)(2,1)S(1)}, u32[]{:S(2)}, u32[]{:S(2)}) collective-permute-start(bf16[224,576]{1,0:T(8,128)(2,1)} %get-tuple-element.191.refs_0_), channel_id=1, source_target_pairs={{0,16},{8,24},{16,0},{24,8},{1,17},{9,25},{17,1},{25,9},{2,18},{10... | collective-permute-start | bytes 774152 | tf_op jit(solution)/shard_map/ppermute | solution.py:27
  9.4 12.0 %collective-permute-start.5 = (bf16[224,576]{1,0:T(8,128)(2,1)}, bf16[224,576]{1,0:T(8,128)(2,1)S(1)}, u32[]{:S(2)}, u32[]{:S(2)}) collective-permute-start(bf16[224,576]{1,0:T(8,128)(2,1)} %get-tuple-element.191.refs_0_), channel_id=1, source_target_pairs={{0,24},{8,16},{16,8},{24,0},{1,25},{9,17},{17,9},{25,1},{2,26},{10... | collective-permute-start | bytes 774152 | tf_op jit(solution)/shard_map/ppermute | solution.py:27
  13.1 8.1 %collective-permute-start.2 = (bf16[128,768]{1,0:T(8,128)(2,1)S(1)}, bf16[128,768]{1,0:T(8,128)(2,1)S(1)}, u32[]{:S(2)}, u32[]{:S(2)}) collective-permute-start(bf16[128,768]{1,0:T(8,128)(2,1)S(1)} %bitcast.124), channel_id=1, source_target_pairs={{0,6},{1,7},{2,4},{3,5},{4,2},{5,3},{6,0},{7,1},{8,14},{9,15},{10,... | collective-permute-start | bytes 589832 | tf_op jit(solution)/shard_map/ppermute | solution.py:37
  26.2 14.6 %collective-permute-start.7 = (bf16[3,96,768]{2,1,0:T(8,128)(2,1)}, bf16[3,96,768]{2,1,0:T(8,128)(2,1)}, u32[]{:S(2)}, u32[]{:S(2)}) collective-permute-start(bf16[3,96,768]{2,1,0:T(8,128)(2,1)} %get-tuple-element.201.refs_0_), channel_id=1, source_target_pairs={{0,8},{8,0},{16,24},{24,16},{1,9},{9,1},{17,25},{25,17},{2,10},{10... | collective-permute-start | bytes 1327112 | tf_op jit(solution)/shard_map/ppermute | solution.py:27
  27.5 13.7 %collective-permute-start.8 = (bf16[3,96,768]{2,1,0:T(8,128)(2,1)}, bf16[3,96,768]{2,1,0:T(8,128)(2,1)}, u32[]{:S(2)}, u32[]{:S(2)}) collective-permute-start(bf16[3,96,768]{2,1,0:T(8,128)(2,1)} %get-tuple-element.201.refs_0_), channel_id=1, source_target_pairs={{0,16},{8,24},{16,0},{24,8},{1,17},{9,25},{17,1},{25,9},{2,18},{10... | collective-permute-start | bytes 1327112 | tf_op jit(solution)/shard_map/ppermute | solution.py:27
  28.7 19.4 %collective-permute-start.13 = (bf16[64,768]{1,0:T(8,128)(2,1)S(1)}, bf16[64,768]{1,0:T(8,128)(2,1)S(1)}, u32[]{:S(2)}, u32[]{:S(2)}) collective-permute-start(bf16[64,768]{1,0:T(8,128)(2,1)S(1)} %bitcast.137), channel_id=1, source_target_pairs={{0,2},{1,3},{2,0},{3,1},{4,6},{5,7},{6,4},{7,5},{8,10},{9,11},{10,... | collective-permute-start | bytes 294920 | tf_op jit(solution)/shard_map/ppermute | solution.py:37
  29.9 19.3 %collective-permute-start.14 = (bf16[64,768]{1,0:T(8,128)(2,1)S(1)}, bf16[64,768]{1,0:T(8,128)(2,1)S(1)}, u32[]{:S(2)}, u32[]{:S(2)}) collective-permute-start(bf16[64,768]{1,0:T(8,128)(2,1)S(1)} %bitcast.138), channel_id=1, source_target_pairs={{0,4},{1,5},{2,6},{3,7},{4,0},{5,1},{6,2},{7,3},{8,12},{9,13},{10,... | collective-permute-start | bytes 294920 | tf_op jit(solution)/shard_map/ppermute | solution.py:37
  32.3 7.2 %collective-permute-start.6 = (bf16[512,384]{1,0:T(8,128)(2,1)S(1)}, bf16[512,384]{1,0:T(8,128)(2,1)S(1)}, u32[]{:S(2)}, u32[]{:S(2)}) collective-permute-start(bf16[512,384]{1,0:T(8,128)(2,1)S(1)} %convolution_convert_fusion.4.own_ref), channel_id=1, source_target_pairs={{0,1},{1,0},{2,3},{3,2},{4,5},{5,4},{6,7},{7,6},{8,9},{9,8},{10,11... | collective-permute-start | bytes 1179656 | tf_op jit(solution)/shard_map/ppermute | solution.py:32
  39.5 17.8 %collective-permute-start.15 = (bf16[64,768]{1,0:T(8,128)(2,1)S(1)}, bf16[64,768]{1,0:T(8,128)(2,1)S(1)}, u32[]{:S(2)}, u32[]{:S(2)}) collective-permute-start(bf16[64,768]{1,0:T(8,128)(2,1)S(1)} %bitcast.139), channel_id=1, source_target_pairs={{0,6},{1,7},{2,4},{3,5},{4,2},{5,3},{6,0},{7,1},{8,14},{9,15},{10,... | collective-permute-start | bytes 294920 | tf_op jit(solution)/shard_map/ppermute | solution.py:37
  40.8 16.5 %collective-permute-start.12 = (bf16[2,96,768]{2,1,0:T(8,128)(2,1)S(1)}, bf16[2,96,768]{2,1,0:T(8,128)(2,1)S(1)}, u32[]{:S(2)}, u32[]{:S(2)}) collective-permute-start(bf16[2,96,768]{2,1,0:T(8,128)(2,1)S(1)} %copy-done.40), channel_id=1, source_target_pairs={{0,8},{8,0},{16,24},{24,16},{1,9},{9,1},{17,25},{25,17},{2,10},{10... | collective-permute-start | bytes 884744 | tf_op jit(solution)/shard_map/ppermute | solution.py:27
  41.1 16.2 %collective-permute-start.11 = (bf16[3,96,768]{2,1,0:T(8,128)(2,1)}, bf16[3,96,768]{2,1,0:T(8,128)(2,1)S(1)}, u32[]{:S(2)}, u32[]{:S(2)}) collective-permute-start(bf16[3,96,768]{2,1,0:T(8,128)(2,1)} %collective-permute-done.7.refs_1_), channel_id=1, source_target_pairs={{0,16},{8,24},{16,0},{24,8},{1,17},{9,25},{17,1},{25,9},{2,18},{10... | collective-permute-start | bytes 1327112 | tf_op jit(solution)/shard_map/ppermute | solution.py:27
  48.1 9.3 %collective-permute-start.9 = (bf16[128,192]{1,0:T(8,128)(2,1)}, bf16[128,192]{1,0:T(8,128)(2,1)S(1)}, u32[]{:S(2)}, u32[]{:S(2)}) collective-permute-start(bf16[128,192]{1,0:T(8,128)(2,1)} %get-tuple-element.209), channel_id=1, source_target_pairs={{0,4},{1,5},{2,6},{3,7},{4,0},{5,1},{6,2},{7,3},{8,12},{9,13},{10,... | collective-permute-start | bytes 147464 | tf_op jit(solution)/shard_map/ppermute | solution.py:37
  49.2 8.2 %collective-permute-start.10 = (bf16[128,192]{1,0:T(8,128)(2,1)}, bf16[128,192]{1,0:T(8,128)(2,1)S(1)}, u32[]{:S(2)}, u32[]{:S(2)}) collective-permute-start(bf16[128,192]{1,0:T(8,128)(2,1)} %get-tuple-element.210), channel_id=1, source_target_pairs={{0,6},{1,7},{2,4},{3,5},{4,2},{5,3},{6,0},{7,1},{8,14},{9,15},{10,... | collective-permute-start | bytes 147464 | tf_op jit(solution)/shard_map/ppermute | solution.py:37
  61.0 5.7 %collective-permute-start.17 = (bf16[3,4,96,768]{3,2,1,0:T(8,128)(2,1)}, bf16[3,4,96,768]{3,2,1,0:T(8,128)(2,1)}, u32[]{:S(2)}, u32[]{:S(2)}) collective-permute-start(bf16[3,4,96,768]{3,2,1,0:T(8,128)(2,1)} %stack_pieces.2.mine_ref), channel_id=1, source_target_pairs={{0,1},{1,0},{2,3},{3,2},{4,5},{5,4},{6,7},{7,6},{8,9},{9,8},{10,11... | collective-permute-start | bytes 5308424 | tf_op jit(solution)/shard_map/ppermute | solution.py:32
  62.4 3.7 %collective-permute-start.18 = (bf16[256,768]{1,0:T(8,128)(2,1)S(1)}, bf16[256,768]{1,0:T(8,128)(2,1)S(1)}, u32[]{:S(2)}, u32[]{:S(2)}) collective-permute-start(bf16[256,768]{1,0:T(8,128)(2,1)S(1)} %pad_maximum_fusion.1), channel_id=1, source_target_pairs={{0,1},{1,0},{2,3},{3,2},{4,5},{5,4},{6,7},{7,6},{8,9},{9,8},{10,11... | collective-permute-start | bytes 1179656 | tf_op jit(solution)/shard_map/ppermute | solution.py:32
  62.7 3.2 collective-permute-start.16
  62.9 38.6 %collective-permute-start.22 = (f32[128,128]{0,1:T(8,128)S(1)}, f32[128,128]{0,1:T(8,128)S(1)}, u32[]{:S(2)}, u32[]{:S(2)}) collective-permute-start(f32[128,128]{0,1:T(8,128)S(1)} %broadcast_in_dim.41), channel_id=1, source_target_pairs={{0,1},{1,0},{2,3},{3,2},{4,5},{5,4},{6,7},{7,6},{8,9},{9,8},{10,11... | collective-permute-start | bytes 196616 | tf_op jit(solution)/shard_map/ppermute | solution.py:32
  63.8 9.0 %collective-permute-start.20 = (bf16[2,96,768]{2,1,0:T(8,128)(2,1)S(1)}, bf16[2,96,768]{2,1,0:T(8,128)(2,1)S(1)}, u32[]{:S(2)}, u32[]{:S(2)}) collective-permute-start(bf16[2,96,768]{2,1,0:T(8,128)(2,1)S(1)} %copy-done.41), channel_id=1, source_target_pairs={{0,16},{8,24},{16,0},{24,8},{1,17},{9,25},{17,1},{25,9},{2,18},{10... | collective-permute-start | bytes 884744 | tf_op jit(solution)/shard_map/ppermute | solution.py:27
  65.8 12.8 %collective-permute-start.19 = (bf16[2,96,768]{2,1,0:T(8,128)(2,1)S(1)}, bf16[2,96,768]{2,1,0:T(8,128)(2,1)S(1)}, u32[]{:S(2)}, u32[]{:S(2)}) collective-permute-start(bf16[2,96,768]{2,1,0:T(8,128)(2,1)S(1)} %collective-permute-done.12.refs_1_), channel_id=1, source_target_pairs={{0,16},{8,24},{16,0},{24,8},{1,17},{9,25},{17,1},{25,9},{2,18},{10... | collective-permute-start | bytes 884744 | tf_op jit(solution)/shard_map/ppermute | solution.py:27
  81.7 6.8 %collective-permute-start.21 = (bf16[2,4,96,768]{3,2,1,0:T(8,128)(2,1)}, bf16[2,4,96,768]{3,2,1,0:T(8,128)(2,1)}, u32[]{:S(2)}, u32[]{:S(2)}) collective-permute-start(bf16[2,4,96,768]{3,2,1,0:T(8,128)(2,1)} %stack_pieces.3.mine_ref), channel_id=1, source_target_pairs={{0,1},{1,0},{2,3},{3,2},{4,5},{5,4},{6,7},{7,6},{8,9},{9,8},{10,11... | collective-permute-start | bytes 3538952 | tf_op jit(solution)/shard_map/ppermute | solution.py:32
  103.7 9.6 %collective-permute-start.26 = (bf16[1,40,1536]{2,1,0:T(8,128)(2,1)S(1)}, bf16[1,40,1536]{2,1,0:T(8,128)(2,1)S(1)}, u32[]{:S(2)}, u32[]{:S(2)}) collective-permute-start(bf16[1,40,1536]{2,1,0:T(8,128)(2,1)S(1)} %get-tuple-element.377), channel_id=1, source_target_pairs={{0,6},{1,7},{2,4},{3,5},{4,2},{5,3},{6,0},{7,1},{8,14},{9,15},{10,... | collective-permute-start | bytes 368648 | tf_op jit(solution)/shard_map/ppermute | solution.py:37
  104.5 10.5 %collective-permute-start.25 = (bf16[1,40,1536]{2,1,0:T(8,128)(2,1)S(1)}, bf16[1,40,1536]{2,1,0:T(8,128)(2,1)S(1)}, u32[]{:S(2)}, u32[]{:S(2)}) collective-permute-start(bf16[1,40,1536]{2,1,0:T(8,128)(2,1)S(1)} %get-tuple-element.378), channel_id=1, source_target_pairs={{0,4},{1,5},{2,6},{3,7},{4,0},{5,1},{6,2},{7,3},{8,12},{9,13},{10,... | collective-permute-start | bytes 368648 | tf_op jit(solution)/shard_map/ppermute | solution.py:37
  107.1 7.9 %collective-permute-start.24 = (bf16[1,40,1536]{2,1,0:T(8,128)(2,1)S(1)}, bf16[1,40,1536]{2,1,0:T(8,128)(2,1)S(1)}, u32[]{:S(2)}, u32[]{:S(2)}) collective-permute-start(bf16[1,40,1536]{2,1,0:T(8,128)(2,1)S(1)} %get-tuple-element.379), channel_id=1, source_target_pairs={{0,2},{1,3},{2,0},{3,1},{4,6},{5,7},{6,4},{7,5},{8,10},{9,11},{10,... | collective-permute-start | bytes 368648 | tf_op jit(solution)/shard_map/ppermute | solution.py:37
  115.1 11.8 %collective-permute-start.27 = (bf16[160,1536]{1,0:T(8,128)(2,1)S(1)}, bf16[160,1536]{1,0:T(8,128)(2,1)S(1)}, u32[]{:S(2)}, u32[]{:S(2)}) collective-permute-start(bf16[160,1536]{1,0:T(8,128)(2,1)S(1)} %maximum_bitcast_fusion.refs_0_), channel_id=1, source_target_pairs={{0,8},{8,0},{16,24},{24,16},{1,9},{9,1},{17,25},{25,17},{2,10},{10... | collective-permute-start | bytes 1474568 | tf_op jit(solution)/shard_map/ppermute | solution.py:27
  115.6 17.5 %collective-permute-start.28 = (bf16[160,1536]{1,0:T(8,128)(2,1)S(1)}, bf16[160,1536]{1,0:T(8,128)(2,1)S(1)}, u32[]{:S(2)}, u32[]{:S(2)}) collective-permute-start(bf16[160,1536]{1,0:T(8,128)(2,1)S(1)} %maximum_bitcast_fusion.refs_0_), channel_id=1, source_target_pairs={{0,16},{8,24},{16,0},{24,8},{1,17},{9,25},{17,1},{25,9},{2,18},{10... | collective-permute-start | bytes 1474568 | tf_op jit(solution)/shard_map/ppermute | solution.py:27
  116.2 21.5 %collective-permute-start.29 = (bf16[160,1536]{1,0:T(8,128)(2,1)S(1)}, bf16[160,1536]{1,0:T(8,128)(2,1)S(1)}, u32[]{:S(2)}, u32[]{:S(2)}) collective-permute-start(bf16[160,1536]{1,0:T(8,128)(2,1)S(1)} %maximum_bitcast_fusion.refs_0_), channel_id=1, source_target_pairs={{0,24},{8,16},{16,8},{24,0},{1,25},{9,17},{17,9},{25,1},{2,26},{10... | collective-permute-start | bytes 1474568 | tf_op jit(solution)/shard_map/ppermute | solution.py:27
  137.7 10.8 %collective-permute-start.30 = (bf16[160,1536]{1,0:T(8,128)(2,1)}, bf16[160,1536]{1,0:T(8,128)(2,1)S(1)}, u32[]{:S(2)}, u32[]{:S(2)}) collective-permute-start(bf16[160,1536]{1,0:T(8,128)(2,1)} %get-tuple-element.246), channel_id=1, source_target_pairs={{0,8},{8,0},{16,24},{24,16},{1,9},{9,1},{17,25},{25,17},{2,10},{10... | collective-permute-start | bytes 1474568 | tf_op jit(solution)/shard_map/ppermute | solution.py:27
  144.0 21.1 %collective-permute-start.31 = (bf16[160,1536]{1,0:T(8,128)(2,1)}, bf16[160,1536]{1,0:T(8,128)(2,1)S(1)}, u32[]{:S(2)}, u32[]{:S(2)}) collective-permute-start(bf16[160,1536]{1,0:T(8,128)(2,1)} %get-tuple-element.249), channel_id=1, source_target_pairs={{0,16},{8,24},{16,0},{24,8},{1,17},{9,25},{17,1},{25,9},{2,18},{10... | collective-permute-start | bytes 1474568 | tf_op jit(solution)/shard_map/ppermute | solution.py:27
  144.9 20.3 %collective-permute-start.32 = (bf16[160,1536]{1,0:T(8,128)(2,1)}, bf16[160,1536]{1,0:T(8,128)(2,1)S(1)}, u32[]{:S(2)}, u32[]{:S(2)}) collective-permute-start(bf16[160,1536]{1,0:T(8,128)(2,1)} %get-tuple-element.250), channel_id=1, source_target_pairs={{0,24},{8,16},{16,8},{24,0},{1,25},{9,17},{17,9},{25,1},{2,26},{10... | collective-permute-start | bytes 1474568 | tf_op jit(solution)/shard_map/ppermute | solution.py:27
  169.1 4.7 %collective-permute-start.35 = (bf16[40,1536]{1,0:T(8,128)(2,1)}, bf16[40,1536]{1,0:T(8,128)(2,1)S(1)}, u32[]{:S(2)}, u32[]{:S(2)}) collective-permute-start(bf16[40,1536]{1,0:T(8,128)(2,1)} %get-tuple-element.258), channel_id=1, source_target_pairs={{0,6},{1,7},{2,4},{3,5},{4,2},{5,3},{6,0},{7,1},{8,14},{9,15},{10,... | collective-permute-start | bytes 368648 | tf_op jit(solution)/shard_map/ppermute | solution.py:37
  169.7 12.1 %collective-permute-start.34 = (bf16[40,1536]{1,0:T(8,128)(2,1)}, bf16[40,1536]{1,0:T(8,128)(2,1)S(1)}, u32[]{:S(2)}, u32[]{:S(2)}) collective-permute-start(bf16[40,1536]{1,0:T(8,128)(2,1)} %get-tuple-element.257), channel_id=1, source_target_pairs={{0,4},{1,5},{2,6},{3,7},{4,0},{5,1},{6,2},{7,3},{8,12},{9,13},{10,... | collective-permute-start | bytes 368648 | tf_op jit(solution)/shard_map/ppermute | solution.py:37
  173.8 8.1 %collective-permute-start.33 = (bf16[40,1536]{1,0:T(8,128)(2,1)}, bf16[40,1536]{1,0:T(8,128)(2,1)S(1)}, u32[]{:S(2)}, u32[]{:S(2)}) collective-permute-start(bf16[40,1536]{1,0:T(8,128)(2,1)} %get-tuple-element.256), channel_id=1, source_target_pairs={{0,2},{1,3},{2,0},{3,1},{4,6},{5,7},{6,4},{7,5},{8,10},{9,11},{10,... | collective-permute-start | bytes 368648 | tf_op jit(solution)/shard_map/ppermute | solution.py:37
  183.4 3.1 collective-permute-start.36
  209.0 11.3 %collective-permute-start.40 = (bf16[4,1024,384]{2,1,0:T(8,128)(2,1)}, bf16[4,1024,384]{2,1,0:T(8,128)(2,1)S(1)}, u32[]{:S(2)}, u32[]{:S(2)}) collective-permute-start(bf16[4,1024,384]{2,1,0:T(8,128)(2,1)} %get-tuple-element.265), channel_id=1, source_target_pairs={{0,1},{1,0},{2,3},{3,2},{4,5},{5,4},{6,7},{7,6},{8,9},{9,8},{10,11... | collective-permute-start | bytes 9437192 | tf_op jit(solution)/shard_map/ppermute | solution.py:32
  210.1 4.9 %collective-permute-start.37 = (bf16[128,192]{1,0:T(8,128)(2,1)S(1)}, bf16[128,192]{1,0:T(8,128)(2,1)S(1)}, u32[]{:S(2)}, u32[]{:S(2)}) collective-permute-start(bf16[128,192]{1,0:T(8,128)(2,1)S(1)} %get-tuple-element.382), channel_id=1, source_target_pairs={{0,2},{1,3},{2,0},{3,1},{4,6},{5,7},{6,4},{7,5},{8,10},{9,11},{10,... | collective-permute-start | bytes 147464 | tf_op jit(solution)/shard_map/ppermute | solution.py:37
  212.7 4.1 %collective-permute-start.38 = (bf16[128,192]{1,0:T(8,128)(2,1)S(1)}, bf16[128,192]{1,0:T(8,128)(2,1)S(1)}, u32[]{:S(2)}, u32[]{:S(2)}) collective-permute-start(bf16[128,192]{1,0:T(8,128)(2,1)S(1)} %get-tuple-element.381), channel_id=1, source_target_pairs={{0,4},{1,5},{2,6},{3,7},{4,0},{5,1},{6,2},{7,3},{8,12},{9,13},{10,... | collective-permute-start | bytes 147464 | tf_op jit(solution)/shard_map/ppermute | solution.py:37
  213.2 7.0 %collective-permute-start.39 = (bf16[128,192]{1,0:T(8,128)(2,1)S(1)}, bf16[128,192]{1,0:T(8,128)(2,1)S(1)}, u32[]{:S(2)}, u32[]{:S(2)}) collective-permute-start(bf16[128,192]{1,0:T(8,128)(2,1)S(1)} %get-tuple-element.380), channel_id=1, source_target_pairs={{0,6},{1,7},{2,4},{3,5},{4,2},{5,3},{6,0},{7,1},{8,14},{9,15},{10,... | collective-permute-start | bytes 147464 | tf_op jit(solution)/shard_map/ppermute | solution.py:37
  223.5 15.3 %collective-permute-start.41 = (bf16[512,384]{1,0:T(8,128)(2,1)S(1)}, bf16[512,384]{1,0:T(8,128)(2,1)}, u32[]{:S(2)}, u32[]{:S(2)}) collective-permute-start(bf16[512,384]{1,0:T(8,128)(2,1)S(1)} %get-tuple-element.279), channel_id=1, source_target_pairs={{0,8},{8,0},{16,24},{24,16},{1,9},{9,1},{17,25},{25,17},{2,10},{10... | collective-permute-start | bytes 1179656 | tf_op jit(solution)/shard_map/ppermute | solution.py:27
  224.3 14.5 %collective-permute-start.42 = (bf16[512,384]{1,0:T(8,128)(2,1)S(1)}, bf16[512,384]{1,0:T(8,128)(2,1)}, u32[]{:S(2)}, u32[]{:S(2)}) collective-permute-start(bf16[512,384]{1,0:T(8,128)(2,1)S(1)} %get-tuple-element.280), channel_id=1, source_target_pairs={{0,16},{8,24},{16,0},{24,8},{1,17},{9,25},{17,1},{25,9},{2,18},{10... | collective-permute-start | bytes 1179656 | tf_op jit(solution)/shard_map/ppermute | solution.py:27
  225.6 17.0 %collective-permute-start.43 = (bf16[512,384]{1,0:T(8,128)(2,1)S(1)}, bf16[512,384]{1,0:T(8,128)(2,1)}, u32[]{:S(2)}, u32[]{:S(2)}) collective-permute-start(bf16[512,384]{1,0:T(8,128)(2,1)S(1)} %get-tuple-element.281), channel_id=1, source_target_pairs={{0,24},{8,16},{16,8},{24,0},{1,25},{9,17},{17,9},{25,1},{2,26},{10... | collective-permute-start | bytes 1179656 | tf_op jit(solution)/shard_map/ppermute | solution.py:27
  242.7 5.8 %collective-permute-start.44 = (bf16[512,384]{1,0:T(8,128)(2,1)}, bf16[512,384]{1,0:T(8,128)(2,1)}, u32[]{:S(2)}, u32[]{:S(2)}) collective-permute-start(bf16[512,384]{1,0:T(8,128)(2,1)} %get-tuple-element.284), channel_id=1, source_target_pairs={{0,1},{1,0},{2,3},{3,2},{4,5},{5,4},{6,7},{7,6},{8,9},{9,8},{10,11... | collective-permute-start | bytes 1179656 | tf_op jit(solution)/shard_map/ppermute | solution.py:32
  245.9 11.1 %collective-permute-start.46 = (bf16[512,384]{1,0:T(8,128)(2,1)}, bf16[512,384]{1,0:T(8,128)(2,1)S(1)}, u32[]{:S(2)}, u32[]{:S(2)}) collective-permute-start(bf16[512,384]{1,0:T(8,128)(2,1)} %get-tuple-element.368), channel_id=1, source_target_pairs={{0,8},{8,0},{16,24},{24,16},{1,9},{9,1},{17,25},{25,17},{2,10},{10... | collective-permute-start | bytes 1179656 | tf_op jit(solution)/shard_map/ppermute | solution.py:27
  246.7 10.7 %collective-permute-start.47 = (bf16[512,384]{1,0:T(8,128)(2,1)}, bf16[512,384]{1,0:T(8,128)(2,1)}, u32[]{:S(2)}, u32[]{:S(2)}) collective-permute-start(bf16[512,384]{1,0:T(8,128)(2,1)} %get-tuple-element.367), channel_id=1, source_target_pairs={{0,16},{8,24},{16,0},{24,8},{1,17},{9,25},{17,1},{25,9},{2,18},{10... | collective-permute-start | bytes 1179656 | tf_op jit(solution)/shard_map/ppermute | solution.py:27
  247.6 18.6 %collective-permute-start.48 = (bf16[512,384]{1,0:T(8,128)(2,1)S(1)}, bf16[512,384]{1,0:T(8,128)(2,1)}, u32[]{:S(2)}, u32[]{:S(2)}) collective-permute-start(bf16[512,384]{1,0:T(8,128)(2,1)S(1)} %get-tuple-element.366), channel_id=1, source_target_pairs={{0,24},{8,16},{16,8},{24,0},{1,25},{9,17},{17,9},{25,1},{2,26},{10... | collective-permute-start | bytes 1179656 | tf_op jit(solution)/shard_map/ppermute | solution.py:27
  253.2 13.0 %collective-permute-start.45 = (bf16[4,96,576]{2,1,0:T(8,128)(2,1)}, bf16[4,96,576]{2,1,0:T(8,128)(2,1)}, u32[]{:S(2)}, u32[]{:S(2)}) collective-permute-start(bf16[4,96,576]{2,1,0:T(8,128)(2,1)} %get-tuple-element.286), channel_id=1, source_target_pairs={{0,1},{1,0},{2,3},{3,2},{4,5},{5,4},{6,7},{7,6},{8,9},{9,8},{10,11... | collective-permute-start | bytes 1327112 | tf_op jit(solution)/shard_map/ppermute | solution.py:32
  254.3 11.9 %collective-permute-start.49 = (bf16[128,768]{1,0:T(8,128)(2,1)}, bf16[128,768]{1,0:T(8,128)(2,1)S(1)}, u32[]{:S(2)}, u32[]{:S(2)}) collective-permute-start(bf16[128,768]{1,0:T(8,128)(2,1)} %get-tuple-element.290), channel_id=1, source_target_pairs={{0,2},{1,3},{2,0},{3,1},{4,6},{5,7},{6,4},{7,5},{8,10},{9,11},{10,... | collective-permute-start | bytes 589832 | tf_op jit(solution)/shard_map/ppermute | solution.py:37
  256.9 19.3 %collective-permute-start.53 = (bf16[128,768]{1,0:T(8,128)(2,1)}, bf16[128,768]{1,0:T(8,128)(2,1)S(1)}, u32[]{:S(2)}, u32[]{:S(2)}) collective-permute-start(bf16[128,768]{1,0:T(8,128)(2,1)} %get-tuple-element.312), channel_id=1, source_target_pairs={{0,4},{1,5},{2,6},{3,7},{4,0},{5,1},{6,2},{7,3},{8,12},{9,13},{10,... | collective-permute-start | bytes 589832 | tf_op jit(solution)/shard_map/ppermute | solution.py:37
  257.5 18.8 %collective-permute-start.54 = (bf16[128,768]{1,0:T(8,128)(2,1)}, bf16[128,768]{1,0:T(8,128)(2,1)S(1)}, u32[]{:S(2)}, u32[]{:S(2)}) collective-permute-start(bf16[128,768]{1,0:T(8,128)(2,1)} %get-tuple-element.313), channel_id=1, source_target_pairs={{0,6},{1,7},{2,4},{3,5},{4,2},{5,3},{6,0},{7,1},{8,14},{9,15},{10,... | collective-permute-start | bytes 589832 | tf_op jit(solution)/shard_map/ppermute | solution.py:37
  273.0 5.2 %collective-permute-start.50 = (bf16[112,576]{1,0:T(8,128)(2,1)}, bf16[112,576]{1,0:T(8,128)(2,1)S(1)}, u32[]{:S(2)}, u32[]{:S(2)}) collective-permute-start(bf16[112,576]{1,0:T(8,128)(2,1)} %get-tuple-element.307), channel_id=1, source_target_pairs={{0,8},{8,0},{16,24},{24,16},{1,9},{9,1},{17,25},{25,17},{2,10},{10... | collective-permute-start | bytes 387080 | tf_op jit(solution)/shard_map/ppermute | solution.py:27
  274.2 10.4 %collective-permute-start.51 = (bf16[112,576]{1,0:T(8,128)(2,1)}, bf16[112,576]{1,0:T(8,128)(2,1)S(1)}, u32[]{:S(2)}, u32[]{:S(2)}) collective-permute-start(bf16[112,576]{1,0:T(8,128)(2,1)} %get-tuple-element.308), channel_id=1, source_target_pairs={{0,16},{8,24},{16,0},{24,8},{1,17},{9,25},{17,1},{25,9},{2,18},{10... | collective-permute-start | bytes 387080 | tf_op jit(solution)/shard_map/ppermute | solution.py:27
  274.8 9.8 %collective-permute-start.52 = (bf16[112,576]{1,0:T(8,128)(2,1)}, bf16[112,576]{1,0:T(8,128)(2,1)S(1)}, u32[]{:S(2)}, u32[]{:S(2)}) collective-permute-start(bf16[112,576]{1,0:T(8,128)(2,1)} %get-tuple-element.309), channel_id=1, source_target_pairs={{0,24},{8,16},{16,8},{24,0},{1,25},{9,17},{17,9},{25,1},{2,26},{10... | collective-permute-start | bytes 387080 | tf_op jit(solution)/shard_map/ppermute | solution.py:27
  276.2 8.4 %collective-permute-start.55 = (bf16[256,384]{1,0:T(8,128)(2,1)S(1)}, bf16[256,384]{1,0:T(8,128)(2,1)S(1)}, u32[]{:S(2)}, u32[]{:S(2)}) collective-permute-start(bf16[256,384]{1,0:T(8,128)(2,1)S(1)} %copy-done.53), channel_id=1, source_target_pairs={{0,2},{1,3},{2,0},{3,1},{4,6},{5,7},{6,4},{7,5},{8,10},{9,11},{10,... | collective-permute-start | bytes 589832 | tf_op jit(solution)/shard_map/ppermute | solution.py:37
  276.2 9.1 %collective-permute-start.56 = (bf16[256,384]{1,0:T(8,128)(2,1)S(1)}, bf16[256,384]{1,0:T(8,128)(2,1)S(1)}, u32[]{:S(2)}, u32[]{:S(2)}) collective-permute-start(bf16[256,384]{1,0:T(8,128)(2,1)S(1)} %copy-done.52), channel_id=1, source_target_pairs={{0,4},{1,5},{2,6},{3,7},{4,0},{5,1},{6,2},{7,3},{8,12},{9,13},{10,... | collective-permute-start | bytes 589832 | tf_op jit(solution)/shard_map/ppermute | solution.py:37
  278.3 16.7 %collective-permute-start.57 = (bf16[256,384]{1,0:T(8,128)(2,1)S(1)}, bf16[256,384]{1,0:T(8,128)(2,1)S(1)}, u32[]{:S(2)}, u32[]{:S(2)}) collective-permute-start(bf16[256,384]{1,0:T(8,128)(2,1)S(1)} %copy-done.51), channel_id=1, source_target_pairs={{0,6},{1,7},{2,4},{3,5},{4,2},{5,3},{6,0},{7,1},{8,14},{9,15},{10,... | collective-permute-start | bytes 589832 | tf_op jit(solution)/shard_map/ppermute | solution.py:37
  295.1 5.2 %collective-permute-start.61 = (bf16[112,576]{1,0:T(8,128)(2,1)S(1)}, bf16[112,576]{1,0:T(8,128)(2,1)S(1)}, u32[]{:S(2)}, u32[]{:S(2)}) collective-permute-start(bf16[112,576]{1,0:T(8,128)(2,1)S(1)} %add_convert_fusion.10.refs_0_), channel_id=1, source_target_pairs={{0,2},{1,3},{2,0},{3,1},{4,6},{5,7},{6,4},{7,5},{8,10},{9,11},{10,... | collective-permute-start | bytes 387080 | tf_op jit(solution)/shard_map/ppermute | solution.py:37
  295.1 7.3 %collective-permute-start.62 = (bf16[112,576]{1,0:T(8,128)(2,1)S(1)}, bf16[112,576]{1,0:T(8,128)(2,1)S(1)}, u32[]{:S(2)}, u32[]{:S(2)}) collective-permute-start(bf16[112,576]{1,0:T(8,128)(2,1)S(1)} %add_convert_fusion.10.refs_0_), channel_id=1, source_target_pairs={{0,4},{1,5},{2,6},{3,7},{4,0},{5,1},{6,2},{7,3},{8,12},{9,13},{10,... | collective-permute-start | bytes 387080 | tf_op jit(solution)/shard_map/ppermute | solution.py:37
  297.4 13.1 %collective-permute-start.63 = (bf16[112,576]{1,0:T(8,128)(2,1)S(1)}, bf16[112,576]{1,0:T(8,128)(2,1)S(1)}, u32[]{:S(2)}, u32[]{:S(2)}) collective-permute-start(bf16[112,576]{1,0:T(8,128)(2,1)S(1)} %add_convert_fusion.10.refs_0_), channel_id=1, source_target_pairs={{0,6},{1,7},{2,4},{3,5},{4,2},{5,3},{6,0},{7,1},{8,14},{9,15},{10,... | collective-permute-start | bytes 387080 | tf_op jit(solution)/shard_map/ppermute | solution.py:37
  297.9 32.2 %collective-permute-start.58 = (bf16[256,384]{1,0:T(8,128)(2,1)S(1)}, bf16[256,384]{1,0:T(8,128)(2,1)S(1)}, u32[]{:S(2)}, u32[]{:S(2)}) collective-permute-start(bf16[256,384]{1,0:T(8,128)(2,1)S(1)} %add_convert_fusion.8.refs_0_), channel_id=1, source_target_pairs={{0,2},{1,3},{2,0},{3,1},{4,6},{5,7},{6,4},{7,5},{8,10},{9,11},{10,... | collective-permute-start | bytes 589832 | tf_op jit(solution)/shard_map/ppermute | solution.py:37
  298.9 31.1 %collective-permute-start.59 = (bf16[256,384]{1,0:T(8,128)(2,1)S(1)}, bf16[256,384]{1,0:T(8,128)(2,1)S(1)}, u32[]{:S(2)}, u32[]{:S(2)}) collective-permute-start(bf16[256,384]{1,0:T(8,128)(2,1)S(1)} %add_convert_fusion.8.refs_0_), channel_id=1, source_target_pairs={{0,4},{1,5},{2,6},{3,7},{4,0},{5,1},{6,2},{7,3},{8,12},{9,13},{10,... | collective-permute-start | bytes 589832 | tf_op jit(solution)/shard_map/ppermute | solution.py:37
  300.3 29.8 %collective-permute-start.60 = (bf16[256,384]{1,0:T(8,128)(2,1)S(1)}, bf16[256,384]{1,0:T(8,128)(2,1)S(1)}, u32[]{:S(2)}, u32[]{:S(2)}) collective-permute-start(bf16[256,384]{1,0:T(8,128)(2,1)S(1)} %add_convert_fusion.8.refs_0_), channel_id=1, source_target_pairs={{0,6},{1,7},{2,4},{3,5},{4,2},{5,3},{6,0},{7,1},{8,14},{9,15},{10,... | collective-permute-start | bytes 589832 | tf_op jit(solution)/shard_map/ppermute | solution.py:37
  313.2 13.1 %collective-permute-start.64 = (bf16[4,112,576]{2,1,0:T(8,128)(2,1)}, bf16[4,112,576]{2,1,0:T(8,128)(2,1)S(1)}, u32[]{:S(2)}, u32[]{:S(2)}) collective-permute-start(bf16[4,112,576]{2,1,0:T(8,128)(2,1)} %collect.1.mine_ref), channel_id=1, source_target_pairs={{0,1},{1,0},{2,3},{3,2},{4,5},{5,4},{6,7},{7,6},{8,9},{9,8},{10,11... | collective-permute-start | bytes 1548296 | tf_op jit(solution)/shard_map/ppermute | solution.py:32
  (69 other events, 450.9 us)

commit v3 on v2

--- a/solution.py
+++ b/solution.py
@@ -307,12 +307,14 @@
 def home_kernel(rests, *refs):
     pieces, outs = refs[: len(refs) - GROUP], refs[len(refs) - GROUP :]
     block = outs[0].shape[0] // rests
+    total = pieces[0][...].astype(WIDE)
+    for piece in pieces[1:]:
+        total = total + piece[...].astype(WIDE)
     for k, out in enumerate(outs):
-        for r in range(rests):
-            here = slice((r * GROUP + k) * block, (r * GROUP + k + 1) * block)
-            out[r * block : (r + 1) * block] = sum_low(
-                pieces[0][here], [piece[here] for piece in pieces[1:]]
-            )
+        rows = [
+            total[(r * GROUP + k) * block : (r * GROUP + k + 1) * block] for r in range(rests)
+        ]
+        out[...] = (rows[0] if rests == 1 else jnp.concatenate(rows)).astype(LOW)
 
 
 def sum_home(pieces, rests):

time: 344 us -> 344 us (level)
  no operation moved by 1% of the time
where the time goes in v3:
time: 344 us; the launch traced here: 338 us
  waiting for transfers between devices  108 us (31%)
  Pallas kernels  103 us (30%)
  starting transfers between devices  74.4 us (22%)
  matrix products  18.7 us (5%)
  other arithmetic  17.1 us (5%)
  local copies, waits for them, and re-layouts  15.2 us (4%)
    ppermute x24, waiting for transfers between devices, swap_fsdp(): return lax.ppermute(rows, 'fsdp', [(i, i ^ k) for i in range(size)])  53.2 us
    ppermute x30, waiting for transfers between devices, swap_group(): return lax.ppermute(rows, 'ctx', [(i, i ^ 2 * k) for i in range(size)])  50.9 us
    ppermute x30, starting transfers between devices, swap_group(): return lax.ppermute(rows, 'ctx', [(i, i ^ 2 * k) for i in range(size)])  31 us
    ppermute x15, starting transfers between devices, swap_core(): return lax.ppermute(rows, 'ctx', [(i, i ^ 1) for i in range(size)])  23.1 us
    ppermute x24, starting transfers between devices, swap_fsdp(): return lax.ppermute(rows, 'fsdp', [(i, i ^ k) for i in range(size)])  20.2 us
    dot_general x10, matrix products, dot(): return jnp.dot(left, right, preferred_element_type=WIDE)  14.2 us
    pallas_call x1, Pallas kernels, self_backward(): pl.pallas_call(partial(self_backward_kernel, first, done), grid_spec=pltp...  12.6 us
    pallas_call x2, Pallas kernels, self_forward(): pl.pallas_call(partial(self_forward_kernel, first), grid_spec=pltpu.Prefe...  11.5 us
  transfers between devices with their start and end apart: 69, of which 28 were waited for; matrix products, arithmetic and copies ran while one was open for 9% of the time, Pallas kernels for 23%

profile of v3, /device:TPU:13, one launch (start us, length us, event | category | flops | bytes accessed | tf_op | source)
XLA Modules:
  0.0 338.0 jit_solution(6297338433399916064)
XLA Ops:
  0.9 2.3 collective-permute-start.1
  5.2 2.8 pack_weights.1
  13.9 7.3 %collective-permute-done.2 = bf16[128,768]{1,0:T(8,128)(2,1)S(1)} collective-permute-done((bf16[128,768]{1,0:T(8,128)(2,1)S(1)}, bf16[128,768]{1,0:T(8,128)(2,1)S(1)}, u32[]{:S(2)}, u32[]{:S(2)}) %collective-permute-start.2) | collective-permute-done | bytes 196640 | tf_op jit(solution)/shard_map/ppermute | solution.py:37
  22.1 2.4 place_qkv.1
  32.3 2.6 collective-permute-start.6
  35.6 2.8 bias_tiles.1.tile_ref
  42.4 5.7 %self_forward.2 = (bf16[128,192]{1,0:T(8,128)(2,1)}, bf16[128,192]{1,0:T(8,128)(2,1)}, f32[256,128]{1,0:T(8,128)}) custom-call(s32[8,16]{1,0:T(8,128)} %clamp_add_fusion.kind_ref, f32[2,3,5,64,128]{4,3,2,1,0:T(8,128)} %bias_tiles.1.tile_ref, bf16[512,192]{1,0:T(8,128)(2,1)} %convolution_convert_fusion.5.query_ref, bf16[512,384]{1,0:T(8,128)(2,1)} %copy-done.37, ...), custom_call_target="tpu_custom_call" | custom-call | flops 4400000000 | bytes 15400000 | tf_op jit(solution)/shard_map/self_forward/pallas_call | solution.py:847
  49.2 2.3 collective-permute-start.10
  51.5 5.8 %self_forward.3 = (bf16[128,192]{1,0:T(8,128)(2,1)}, bf16[128,192]{1,0:T(8,128)(2,1)}, f32[256,128]{1,0:T(8,128)}) custom-call(s32[8,16]{1,0:T(8,128)} %clamp_add_fusion.kind_ref, f32[2,3,5,64,128]{4,3,2,1,0:T(8,128)} %bias_tiles.1.tile_ref, bf16[512,192]{1,0:T(8,128)(2,1)} %convolution_convert_fusion.5.query_ref, bf16[512,384]{1,0:T(8,128)(2,1)} %copy-done.37, ...), custom_call_target="tpu_custom_call" | custom-call | flops 4400000000 | bytes 15400000 | tf_op jit(solution)/shard_map/self_forward/pallas_call | solution.py:847
  58.2 2.8 stack_pieces.2.mine_ref
  61.0 1.4 collective-permute-start.17
  64.1 1.7 collective-permute-done.16
  66.7 4.0 %weave_halves.2 = (bf16[4,2,96,768]{3,2,1,0:T(8,128)(2,1)}, bf16[4,2,96,768]{3,2,1,0:T(8,128)(2,1)}, bf16[4,2,96,768]{3,2,1,0:T(8,128)(2,1)}) custom-call(s32[1]{0:T(128)} %bitcast.2.index_ref, bf16[3,4,96,768]{3,2,1,0:T(8,128)(2,1)} %stack_pieces.2.mine_ref, bf16[3,4,96,768]{3,2,1,0:T(8,128)(2,1)} %collective-permute-done.17.theirs_ref), custom_call_target="tpu_custom_call" | custom-call | flops 4000000000 | bytes 14000000 | tf_op jit(solution)/shard_map/weave_halves/pallas_call | solution.py:229
  70.9 1.8 multiply_reduce_fusion.4
  72.8 5.8 %collective-permute-done.19.refs_3_ = bf16[2,96,768]{2,1,0:T(8,128)(2,1)S(1)} collective-permute-done((bf16[2,96,768]{2,1,0:T(8,128)(2,1)S(1)}, bf16[2,96,768]{2,1,0:T(8,128)(2,1)S(1)}, u32[]{:S(2)}, u32[]{:S(2)}) %collective-permute-start.19) | collective-permute-done | bytes 294944 | tf_op jit(solution)/shard_map/ppermute | solution.py:27
  79.4 2.3 stack_pieces.3.mine_ref
  83.6 3.2 convolution_convert_fusion.2.value_ref
  86.8 1.7 convolution_convert_fusion.3.key_ref
  88.5 3.2 weave_halves.3
  91.7 2.3 convolution_convert_fusion.8.query_ref
  94.0 5.5 %cross_forward.1 = (bf16[128,768]{1,0:T(8,128)(2,1)}, f32[128,128]{1,0:T(8,128)}) custom-call(bf16[128,768]{1,0:T(8,128)(2,1)} %convolution_convert_fusion.8.query_ref, bf16[512,768]{1,0:T(8,128)(2,1)} %convolution_convert_fusion.3.key_ref, bf16[512,768]{1,0:T(8,128)(2,1)} %convolution_convert_fusion.2.value_ref), custom_call_target="tpu_custom_call" | custom-call | flops 6600000000 | bytes 23100000 | tf_op jit(solution)/shard_map/cross_forward/pallas_call | solution.py:915
  99.5 1.4 multiply_reduce_fusion.3
  101.5 1.7 collective-permute-done.23
  104.5 2.6 collective-permute-start.25
  107.1 6.2 %collective-permute-done.26 = bf16[1,40,1536]{2,1,0:T(8,128)(2,1)S(1)} collective-permute-done((bf16[1,40,1536]{2,1,0:T(8,128)(2,1)S(1)}, bf16[1,40,1536]{2,1,0:T(8,128)(2,1)S(1)}, u32[]{:S(2)}, u32[]{:S(2)}) %collective-permute-start.26) | collective-permute-done | bytes 122912 | tf_op jit(solution)/shard_map/ppermute | solution.py:37
  113.3 1.7 collective-permute-done.25
  116.2 1.6 collective-permute-start.29
  117.8 9.1 %collective-permute-done.27.refs_1_ = bf16[160,1536]{1,0:T(8,128)(2,1)S(1)} collective-permute-done((bf16[160,1536]{1,0:T(8,128)(2,1)S(1)}, bf16[160,1536]{1,0:T(8,128)(2,1)S(1)}, u32[]{:S(2)}, u32[]{:S(2)}) %collective-permute-start.27) | collective-permute-done | bytes 491552 | tf_op jit(solution)/shard_map/ppermute | solution.py:27
  127.7 5.5 %experts.2 = (bf16[160,1536]{1,0:T(8,128)(2,1)}, bf16[160,1536]{1,0:T(8,128)(2,1)}, bf16[320,1536]{1,0:T(8,128)(2,1)}) custom-call(bf16[160,1536]{1,0:T(8,128)(2,1)} %copy-done.14, bf16[160,1536]{1,0:T(8,128)(2,1)} %copy-done.30, bf16[768,768]{1,0:T(8,128)(2,1)} %bitcast.147, bf16[768,768]{1,0:T(8,128)(2,1)} %bitcast.149), custom_call_target="tpu_custom_call" | custom-call | flops 4100000000 | bytes 14349999 | tf_op jit(solution)/shard_map/experts/pallas_call | solution.py:268
  133.2 4.6 %collective-permute-done.29.refs_1_.refs_3_ = bf16[160,1536]{1,0:T(8,128)(2,1)S(1)} collective-permute-done((bf16[160,1536]{1,0:T(8,128)(2,1)S(1)}, bf16[160,1536]{1,0:T(8,128)(2,1)S(1)}, u32[]{:S(2)}, u32[]{:S(2)}) %collective-permute-start.29) | collective-permute-done | bytes 491552 | tf_op jit(solution)/shard_map/ppermute | solution.py:27
  138.5 5.5 %experts.3 = (bf16[160,1536]{1,0:T(8,128)(2,1)}, bf16[160,1536]{1,0:T(8,128)(2,1)}, bf16[320,1536]{1,0:T(8,128)(2,1)}) custom-call(bf16[160,1536]{1,0:T(8,128)(2,1)} %copy-done.31, bf16[160,1536]{1,0:T(8,128)(2,1)} %copy-done.32, bf16[768,768]{1,0:T(8,128)(2,1)} %bitcast.148, bf16[768,768]{1,0:T(8,128)(2,1)} %bitcast.150), custom_call_target="tpu_custom_call" | custom-call | flops 4100000000 | bytes 14349999 | tf_op jit(solution)/shard_map/experts/pallas_call | solution.py:268
  145.9 2.7 collective-permute-done.30.refs_1_
  148.5 16.6 %collective-permute-done.31.refs_2_ = bf16[160,1536]{1,0:T(8,128)(2,1)S(1)} collective-permute-done((bf16[160,1536]{1,0:T(8,128)(2,1)}, bf16[160,1536]{1,0:T(8,128)(2,1)S(1)}, u32[]{:S(2)}, u32[]{:S(2)}) %collective-permute-start.31) | collective-permute-done | bytes 491552 | tf_op jit(solution)/shard_map/ppermute | solution.py:27
  166.7 2.4 sum_home.1
  169.7 4.1 %collective-permute-start.34 = (bf16[40,1536]{1,0:T(8,128)(2,1)}, bf16[40,1536]{1,0:T(8,128)(2,1)S(1)}, u32[]{:S(2)}, u32[]{:S(2)}) collective-permute-start(bf16[40,1536]{1,0:T(8,128)(2,1)} %get-tuple-element.257), channel_id=1, source_target_pairs={{0,4},{1,5},{2,6},{3,7},{4,0},{5,1},{6,2},{7,3},{8,12},{9,13},{10,... | collective-permute-start | bytes 368648 | tf_op jit(solution)/shard_map/ppermute | solution.py:37
  173.8 8.0 %collective-permute-done.34 = bf16[40,1536]{1,0:T(8,128)(2,1)S(1)} collective-permute-done((bf16[40,1536]{1,0:T(8,128)(2,1)}, bf16[40,1536]{1,0:T(8,128)(2,1)S(1)}, u32[]{:S(2)}, u32[]{:S(2)}) %collective-permute-start.34) | collective-permute-done | bytes 122912 | tf_op jit(solution)/shard_map/ppermute | solution.py:37
  181.9 1.5 convolution_convert_fusion
  183.4 1.8 collective-permute-start.36
  189.4 7.9 %cross_backward.1 = (bf16[128,768]{1,0:T(8,128)(2,1)}, bf16[512,768]{1,0:T(8,128)(2,1)}, bf16[512,768]{1,0:T(8,128)(2,1)}) custom-call(bf16[128,768]{1,0:T(8,128)(2,1)} %convolution_convert_fusion.8.query_ref, bf16[128,768]{1,0:T(8,128)(2,1)} %convolution_convert_fusion.7.up_ref, f32[128,128]{1,0:T(8,128)} %get-tuple-element.259.log_ref, ...), custom_call_target="tpu_custom_call" | custom-call | flops 8200000000 | bytes 28700000 | tf_op jit(solution)/shard_map/cross_backward/pallas_call | solution.py:932
  197.3 1.6 multiply_reduce_fusion.1
  201.4 7.6 %weight_grads.1 = (bf16[4,1024,384]{2,1,0:T(8,128)(2,1)}, bf16[4,1024,384]{2,1,0:T(8,128)(2,1)}) custom-call(s32[3]{0:T(128)} %pad_add_fusion.3.index_ref, bf16[128,768]{1,0:T(8,128)(2,1)} %get-tuple-element.239.refs_0_, bf16[128,768]{1,0:T(8,128)(2,1)} %copy-done.11, bf16[128,768]{1,0:T(8,128)(2,1)} %copy-done.9, ...), custom_call_target="tpu_custom_call" | custom-call | flops 7500000256 | bytes 26250000 | tf_op jit(solution)/shard_map/weight_grads/pallas_call | solution.py:362
  210.1 2.6 collective-permute-start.37
  215.0 1.8 collective-permute-done.38
  216.8 3.4 %collective-permute-done.39 = bf16[128,192]{1,0:T(8,128)(2,1)S(1)} collective-permute-done((bf16[128,192]{1,0:T(8,128)(2,1)S(1)}, bf16[128,192]{1,0:T(8,128)(2,1)S(1)}, u32[]{:S(2)}, u32[]{:S(2)}) %collective-permute-start.39) | collective-permute-done | bytes 49184 | tf_op jit(solution)/shard_map/ppermute | solution.py:37
  220.3 2.5 fusion.30
  226.1 12.6 %self_backward.1 = (bf16[512,192]{1,0:T(8,128)(2,1)}, bf16[512,384]{1,0:T(8,128)(2,1)}, bf16[512,384]{1,0:T(8,128)(2,1)}, f32[2,3,5,64,128]{4,3,2,1,0:T(8,128)}) custom-call(s32[8,16]{1,0:T(8,128)} %clamp_add_fusion.kind_ref, f32[2,3,5,64,128]{4,3,2,1,0:T(8,128)} %bias_tiles.1.tile_ref, bf16[512,192]{1,0:T(8,128)(2,1)} %convolution_convert_fusion.5.query_ref, ...), custom_call_target="tpu_custom_call" | custom-call | flops 8999999488 | bytes 31500000 | tf_op jit(solution)/shard_map/self_backward/pallas_call | solution.py:887
  238.8 3.9 %collective-permute-done.43.refs_3_ = bf16[512,384]{1,0:T(8,128)(2,1)} collective-permute-done((bf16[512,384]{1,0:T(8,128)(2,1)S(1)}, bf16[512,384]{1,0:T(8,128)(2,1)}, u32[]{:S(2)}, u32[]{:S(2)}) %collective-permute-start.43) | collective-permute-done | bytes 393248 | tf_op jit(solution)/shard_map/ppermute | solution.py:27
  242.7 1.9 collective-permute-start.44
  248.5 4.7 %key_grads.1 = (bf16[128,768]{1,0:T(8,128)(2,1)}, bf16[128,768]{1,0:T(8,128)(2,1)}, bf16[128,768]{1,0:T(8,128)(2,1)}, bf16[128,768]{1,0:T(8,128)(2,1)}, bf16[4,9...) custom-call(s32[2]{0:T(128)} %pad_add_fusion.2.index_ref, bf16[512,768]{1,0:T(8,128)(2,1)} %copy-done.4, ...), custom_call_target="tpu_custom_call" | custom-call | flops 100000000 | bytes 350000 | tf_op jit(solution)/shard_map/key_grads/pallas_call | solution.py:508
  255.1 1.9 collective-permute-done.46.refs_5_
  258.3 7.9 %collective-permute-done.48.refs_7_ = bf16[512,384]{1,0:T(8,128)(2,1)} collective-permute-done((bf16[512,384]{1,0:T(8,128)(2,1)S(1)}, bf16[512,384]{1,0:T(8,128)(2,1)}, u32[]{:S(2)}, u32[]{:S(2)}) %collective-permute-start.48) | collective-permute-done | bytes 393248 | tf_op jit(solution)/shard_map/ppermute | solution.py:27
  266.5 2.9 sum_quarters.1
  270.9 2.1 add_qkv.1
  274.8 1.4 collective-permute-start.52
  276.2 2.0 collective-permute-start.56
  278.9 5.7 %expert_grads.1 = (f32[768,768]{1,0:T(8,128)}, f32[768,768]{1,0:T(8,128)}) custom-call(bf16[160,1536]{1,0:T(8,128)(2,1)} %copy-done.14, bf16[160,1536]{1,0:T(8,128)(2,1)} %copy-done.30, bf16[160,1536]{1,0:T(8,128)(2,1)} %copy-done.31, bf16[160,1536]{1,0:T(8,128)(2,1)} %copy-done.32, bf16[320,1536]{1,0:T(8,128)(2,1)} %get-tuple-element.318.refs_4_, ...), custom_call_target="tpu_custom_call" | custom-call | flops 5699999744 | bytes 19950000 | tf_op jit(solution)/shard_map/expert_grads/pallas_call | solution.py:293
  285.4 9.6 %collective-permute-done.57 = bf16[256,384]{1,0:T(8,128)(2,1)S(1)} collective-permute-done((bf16[256,384]{1,0:T(8,128)(2,1)S(1)}, bf16[256,384]{1,0:T(8,128)(2,1)S(1)}, u32[]{:S(2)}, u32[]{:S(2)}) %collective-permute-start.57) | collective-permute-done | bytes 196640 | tf_op jit(solution)/shard_map/ppermute | solution.py:37
  295.1 2.3 collective-permute-start.62
  300.6 1.9 collective-permute-done.62.refs_2_
  302.5 8.1 %collective-permute-done.63.refs_3_ = bf16[112,576]{1,0:T(8,128)(2,1)S(1)} collective-permute-done((bf16[112,576]{1,0:T(8,128)(2,1)S(1)}, bf16[112,576]{1,0:T(8,128)(2,1)S(1)}, u32[]{:S(2)}, u32[]{:S(2)}) %collective-permute-start.63) | collective-permute-done | bytes 129056 | tf_op jit(solution)/shard_map/ppermute | solution.py:37
  311.2 2.0 collect.1.mine_ref
  313.2 11.3 %collective-permute-start.64 = (bf16[4,112,576]{2,1,0:T(8,128)(2,1)}, bf16[4,112,576]{2,1,0:T(8,128)(2,1)S(1)}, u32[]{:S(2)}, u32[]{:S(2)}) collective-permute-start(bf16[4,112,576]{2,1,0:T(8,128)(2,1)} %collect.1.mine_ref), channel_id=1, source_target_pairs={{0,1},{1,0},{2,3},{3,2},{4,5},{5,4},{6,7},{7,6},{8,9},{9,8},{10,11... | collective-permute-start | bytes 1548296 | tf_op jit(solution)/shard_map/ppermute | solution.py:32
  327.1 2.9 qkv_finish.1
  333.9 3.6 %finish_weights.1 = (f32[192,768]{1,0:T(8,128)}, f32[192,768]{1,0:T(8,128)}, f32[192,768]{1,0:T(8,128)}, f32[192,768]{1,0:T(8,128)}, f32[192,768]{1,0:T(8,128)},...) custom-call(s32[5]{0:T(128)} %stack.108.index_ref, bf16[256,384]{1,0:T(8,128)(2,1)} %copy-done.17, ...), custom_call_target="tpu_custom_call" | custom-call | flops 3000000000 | bytes 10500000 | tf_op jit(solution)/shard_map/finish_weights/pallas_call | solution.py:469
  (332 shorter events, 73.6 us)
Async XLA Ops:
  0.7 12.5 %collective-permute-start = (bf16[128,768]{1,0:T(8,128)(2,1)}, bf16[128,768]{1,0:T(8,128)(2,1)S(1)}, u32[]{:S(2)}, u32[]{:S(2)}) collective-permute-start(bf16[128,768]{1,0:T(8,128)(2,1)} %bitcast.122), channel_id=1, source_target_pairs={{0,2},{1,3},{2,0},{3,1},{4,6},{5,7},{6,4},{7,5},{8,10},{9,11},{10,... | collective-permute-start | bytes 589832 | tf_op jit(solution)/shard_map/ppermute | solution.py:37
  0.9 13.0 %collective-permute-start.1 = (bf16[128,768]{1,0:T(8,128)(2,1)}, bf16[128,768]{1,0:T(8,128)(2,1)S(1)}, u32[]{:S(2)}, u32[]{:S(2)}) collective-permute-start(bf16[128,768]{1,0:T(8,128)(2,1)} %bitcast.123), channel_id=1, source_target_pairs={{0,4},{1,5},{2,6},{3,7},{4,0},{5,1},{6,2},{7,3},{8,12},{9,13},{10,... | collective-permute-start | bytes 589832 | tf_op jit(solution)/shard_map/ppermute | solution.py:37
  8.0 13.2 %collective-permute-start.3 = (bf16[224,576]{1,0:T(8,128)(2,1)}, bf16[224,576]{1,0:T(8,128)(2,1)S(1)}, u32[]{:S(2)}, u32[]{:S(2)}) collective-permute-start(bf16[224,576]{1,0:T(8,128)(2,1)} %get-tuple-element.191.refs_0_), channel_id=1, source_target_pairs={{0,8},{8,0},{16,24},{24,16},{1,9},{9,1},{17,25},{25,17},{2,10},{10... | collective-permute-start | bytes 774152 | tf_op jit(solution)/shard_map/ppermute | solution.py:27
  9.2 12.0 %collective-permute-start.4 = (bf16[224,576]{1,0:T(8,128)(2,1)}, bf16[224,576]{1,0:T(8,128)(2,1)S(1)}, u32[]{:S(2)}, u32[]{:S(2)}) collective-permute-start(bf16[224,576]{1,0:T(8,128)(2,1)} %get-tuple-element.191.refs_0_), channel_id=1, source_target_pairs={{0,16},{8,24},{16,0},{24,8},{1,17},{9,25},{17,1},{25,9},{2,18},{10... | collective-permute-start | bytes 774152 | tf_op jit(solution)/shard_map/ppermute | solution.py:27
  9.4 12.0 %collective-permute-start.5 = (bf16[224,576]{1,0:T(8,128)(2,1)}, bf16[224,576]{1,0:T(8,128)(2,1)S(1)}, u32[]{:S(2)}, u32[]{:S(2)}) collective-permute-start(bf16[224,576]{1,0:T(8,128)(2,1)} %get-tuple-element.191.refs_0_), channel_id=1, source_target_pairs={{0,24},{8,16},{16,8},{24,0},{1,25},{9,17},{17,9},{25,1},{2,26},{10... | collective-permute-start | bytes 774152 | tf_op jit(solution)/shard_map/ppermute | solution.py:27
  13.1 8.1 %collective-permute-start.2 = (bf16[128,768]{1,0:T(8,128)(2,1)S(1)}, bf16[128,768]{1,0:T(8,128)(2,1)S(1)}, u32[]{:S(2)}, u32[]{:S(2)}) collective-permute-start(bf16[128,768]{1,0:T(8,128)(2,1)S(1)} %bitcast.124), channel_id=1, source_target_pairs={{0,6},{1,7},{2,4},{3,5},{4,2},{5,3},{6,0},{7,1},{8,14},{9,15},{10,... | collective-permute-start | bytes 589832 | tf_op jit(solution)/shard_map/ppermute | solution.py:37
  26.2 14.6 %collective-permute-start.7 = (bf16[3,96,768]{2,1,0:T(8,128)(2,1)}, bf16[3,96,768]{2,1,0:T(8,128)(2,1)}, u32[]{:S(2)}, u32[]{:S(2)}) collective-permute-start(bf16[3,96,768]{2,1,0:T(8,128)(2,1)} %get-tuple-element.201.refs_0_), channel_id=1, source_target_pairs={{0,8},{8,0},{16,24},{24,16},{1,9},{9,1},{17,25},{25,17},{2,10},{10... | collective-permute-start | bytes 1327112 | tf_op jit(solution)/shard_map/ppermute | solution.py:27
  27.5 13.7 %collective-permute-start.8 = (bf16[3,96,768]{2,1,0:T(8,128)(2,1)}, bf16[3,96,768]{2,1,0:T(8,128)(2,1)}, u32[]{:S(2)}, u32[]{:S(2)}) collective-permute-start(bf16[3,96,768]{2,1,0:T(8,128)(2,1)} %get-tuple-element.201.refs_0_), channel_id=1, source_target_pairs={{0,16},{8,24},{16,0},{24,8},{1,17},{9,25},{17,1},{25,9},{2,18},{10... | collective-permute-start | bytes 1327112 | tf_op jit(solution)/shard_map/ppermute | solution.py:27
  28.7 19.4 %collective-permute-start.13 = (bf16[64,768]{1,0:T(8,128)(2,1)S(1)}, bf16[64,768]{1,0:T(8,128)(2,1)S(1)}, u32[]{:S(2)}, u32[]{:S(2)}) collective-permute-start(bf16[64,768]{1,0:T(8,128)(2,1)S(1)} %bitcast.137), channel_id=1, source_target_pairs={{0,2},{1,3},{2,0},{3,1},{4,6},{5,7},{6,4},{7,5},{8,10},{9,11},{10,... | collective-permute-start | bytes 294920 | tf_op jit(solution)/shard_map/ppermute | solution.py:37
  29.9 19.3 %collective-permute-start.14 = (bf16[64,768]{1,0:T(8,128)(2,1)S(1)}, bf16[64,768]{1,0:T(8,128)(2,1)S(1)}, u32[]{:S(2)}, u32[]{:S(2)}) collective-permute-start(bf16[64,768]{1,0:T(8,128)(2,1)S(1)} %bitcast.138), channel_id=1, source_target_pairs={{0,4},{1,5},{2,6},{3,7},{4,0},{5,1},{6,2},{7,3},{8,12},{9,13},{10,... | collective-permute-start | bytes 294920 | tf_op jit(solution)/shard_map/ppermute | solution.py:37
  32.3 7.2 %collective-permute-start.6 = (bf16[512,384]{1,0:T(8,128)(2,1)S(1)}, bf16[512,384]{1,0:T(8,128)(2,1)S(1)}, u32[]{:S(2)}, u32[]{:S(2)}) collective-permute-start(bf16[512,384]{1,0:T(8,128)(2,1)S(1)} %convolution_convert_fusion.4.own_ref), channel_id=1, source_target_pairs={{0,1},{1,0},{2,3},{3,2},{4,5},{5,4},{6,7},{7,6},{8,9},{9,8},{10,11... | collective-permute-start | bytes 1179656 | tf_op jit(solution)/shard_map/ppermute | solution.py:32
  39.5 17.8 %collective-permute-start.15 = (bf16[64,768]{1,0:T(8,128)(2,1)S(1)}, bf16[64,768]{1,0:T(8,128)(2,1)S(1)}, u32[]{:S(2)}, u32[]{:S(2)}) collective-permute-start(bf16[64,768]{1,0:T(8,128)(2,1)S(1)} %bitcast.139), channel_id=1, source_target_pairs={{0,6},{1,7},{2,4},{3,5},{4,2},{5,3},{6,0},{7,1},{8,14},{9,15},{10,... | collective-permute-start | bytes 294920 | tf_op jit(solution)/shard_map/ppermute | solution.py:37
  40.8 16.5 %collective-permute-start.12 = (bf16[2,96,768]{2,1,0:T(8,128)(2,1)S(1)}, bf16[2,96,768]{2,1,0:T(8,128)(2,1)S(1)}, u32[]{:S(2)}, u32[]{:S(2)}) collective-permute-start(bf16[2,96,768]{2,1,0:T(8,128)(2,1)S(1)} %copy-done.40), channel_id=1, source_target_pairs={{0,8},{8,0},{16,24},{24,16},{1,9},{9,1},{17,25},{25,17},{2,10},{10... | collective-permute-start | bytes 884744 | tf_op jit(solution)/shard_map/ppermute | solution.py:27
  41.1 16.2 %collective-permute-start.11 = (bf16[3,96,768]{2,1,0:T(8,128)(2,1)}, bf16[3,96,768]{2,1,0:T(8,128)(2,1)S(1)}, u32[]{:S(2)}, u32[]{:S(2)}) collective-permute-start(bf16[3,96,768]{2,1,0:T(8,128)(2,1)} %collective-permute-done.7.refs_1_), channel_id=1, source_target_pairs={{0,16},{8,24},{16,0},{24,8},{1,17},{9,25},{17,1},{25,9},{2,18},{10... | collective-permute-start | bytes 1327112 | tf_op jit(solution)/shard_map/ppermute | solution.py:27
  48.1 9.3 %collective-permute-start.9 = (bf16[128,192]{1,0:T(8,128)(2,1)}, bf16[128,192]{1,0:T(8,128)(2,1)S(1)}, u32[]{:S(2)}, u32[]{:S(2)}) collective-permute-start(bf16[128,192]{1,0:T(8,128)(2,1)} %get-tuple-element.209), channel_id=1, source_target_pairs={{0,4},{1,5},{2,6},{3,7},{4,0},{5,1},{6,2},{7,3},{8,12},{9,13},{10,... | collective-permute-start | bytes 147464 | tf_op jit(solution)/shard_map/ppermute | solution.py:37
  49.2 8.2 %collective-permute-start.10 = (bf16[128,192]{1,0:T(8,128)(2,1)}, bf16[128,192]{1,0:T(8,128)(2,1)S(1)}, u32[]{:S(2)}, u32[]{:S(2)}) collective-permute-start(bf16[128,192]{1,0:T(8,128)(2,1)} %get-tuple-element.210), channel_id=1, source_target_pairs={{0,6},{1,7},{2,4},{3,5},{4,2},{5,3},{6,0},{7,1},{8,14},{9,15},{10,... | collective-permute-start | bytes 147464 | tf_op jit(solution)/shard_map/ppermute | solution.py:37
  61.0 5.7 %collective-permute-start.17 = (bf16[3,4,96,768]{3,2,1,0:T(8,128)(2,1)}, bf16[3,4,96,768]{3,2,1,0:T(8,128)(2,1)}, u32[]{:S(2)}, u32[]{:S(2)}) collective-permute-start(bf16[3,4,96,768]{3,2,1,0:T(8,128)(2,1)} %stack_pieces.2.mine_ref), channel_id=1, source_target_pairs={{0,1},{1,0},{2,3},{3,2},{4,5},{5,4},{6,7},{7,6},{8,9},{9,8},{10,11... | collective-permute-start | bytes 5308424 | tf_op jit(solution)/shard_map/ppermute | solution.py:32
  62.4 3.7 %collective-permute-start.18 = (bf16[256,768]{1,0:T(8,128)(2,1)S(1)}, bf16[256,768]{1,0:T(8,128)(2,1)S(1)}, u32[]{:S(2)}, u32[]{:S(2)}) collective-permute-start(bf16[256,768]{1,0:T(8,128)(2,1)S(1)} %pad_maximum_fusion.1), channel_id=1, source_target_pairs={{0,1},{1,0},{2,3},{3,2},{4,5},{5,4},{6,7},{7,6},{8,9},{9,8},{10,11... | collective-permute-start | bytes 1179656 | tf_op jit(solution)/shard_map/ppermute | solution.py:32
  62.7 3.2 collective-permute-start.16
  62.9 38.6 %collective-permute-start.22 = (f32[128,128]{0,1:T(8,128)S(1)}, f32[128,128]{0,1:T(8,128)S(1)}, u32[]{:S(2)}, u32[]{:S(2)}) collective-permute-start(f32[128,128]{0,1:T(8,128)S(1)} %broadcast_in_dim.41), channel_id=1, source_target_pairs={{0,1},{1,0},{2,3},{3,2},{4,5},{5,4},{6,7},{7,6},{8,9},{9,8},{10,11... | collective-permute-start | bytes 196616 | tf_op jit(solution)/shard_map/ppermute | solution.py:32
  63.8 9.0 %collective-permute-start.20 = (bf16[2,96,768]{2,1,0:T(8,128)(2,1)S(1)}, bf16[2,96,768]{2,1,0:T(8,128)(2,1)S(1)}, u32[]{:S(2)}, u32[]{:S(2)}) collective-permute-start(bf16[2,96,768]{2,1,0:T(8,128)(2,1)S(1)} %copy-done.41), channel_id=1, source_target_pairs={{0,16},{8,24},{16,0},{24,8},{1,17},{9,25},{17,1},{25,9},{2,18},{10... | collective-permute-start | bytes 884744 | tf_op jit(solution)/shard_map/ppermute | solution.py:27
  65.8 12.8 %collective-permute-start.19 = (bf16[2,96,768]{2,1,0:T(8,128)(2,1)S(1)}, bf16[2,96,768]{2,1,0:T(8,128)(2,1)S(1)}, u32[]{:S(2)}, u32[]{:S(2)}) collective-permute-start(bf16[2,96,768]{2,1,0:T(8,128)(2,1)S(1)} %collective-permute-done.12.refs_1_), channel_id=1, source_target_pairs={{0,16},{8,24},{16,0},{24,8},{1,17},{9,25},{17,1},{25,9},{2,18},{10... | collective-permute-start | bytes 884744 | tf_op jit(solution)/shard_map/ppermute | solution.py:27
  81.7 6.8 %collective-permute-start.21 = (bf16[2,4,96,768]{3,2,1,0:T(8,128)(2,1)}, bf16[2,4,96,768]{3,2,1,0:T(8,128)(2,1)}, u32[]{:S(2)}, u32[]{:S(2)}) collective-permute-start(bf16[2,4,96,768]{3,2,1,0:T(8,128)(2,1)} %stack_pieces.3.mine_ref), channel_id=1, source_target_pairs={{0,1},{1,0},{2,3},{3,2},{4,5},{5,4},{6,7},{7,6},{8,9},{9,8},{10,11... | collective-permute-start | bytes 3538952 | tf_op jit(solution)/shard_map/ppermute | solution.py:32
  103.7 9.6 %collective-permute-start.26 = (bf16[1,40,1536]{2,1,0:T(8,128)(2,1)S(1)}, bf16[1,40,1536]{2,1,0:T(8,128)(2,1)S(1)}, u32[]{:S(2)}, u32[]{:S(2)}) collective-permute-start(bf16[1,40,1536]{2,1,0:T(8,128)(2,1)S(1)} %get-tuple-element.377), channel_id=1, source_target_pairs={{0,6},{1,7},{2,4},{3,5},{4,2},{5,3},{6,0},{7,1},{8,14},{9,15},{10,... | collective-permute-start | bytes 368648 | tf_op jit(solution)/shard_map/ppermute | solution.py:37
  104.5 10.5 %collective-permute-start.25 = (bf16[1,40,1536]{2,1,0:T(8,128)(2,1)S(1)}, bf16[1,40,1536]{2,1,0:T(8,128)(2,1)S(1)}, u32[]{:S(2)}, u32[]{:S(2)}) collective-permute-start(bf16[1,40,1536]{2,1,0:T(8,128)(2,1)S(1)} %get-tuple-element.378), channel_id=1, source_target_pairs={{0,4},{1,5},{2,6},{3,7},{4,0},{5,1},{6,2},{7,3},{8,12},{9,13},{10,... | collective-permute-start | bytes 368648 | tf_op jit(solution)/shard_map/ppermute | solution.py:37
  107.1 7.9 %collective-permute-start.24 = (bf16[1,40,1536]{2,1,0:T(8,128)(2,1)S(1)}, bf16[1,40,1536]{2,1,0:T(8,128)(2,1)S(1)}, u32[]{:S(2)}, u32[]{:S(2)}) collective-permute-start(bf16[1,40,1536]{2,1,0:T(8,128)(2,1)S(1)} %get-tuple-element.379), channel_id=1, source_target_pairs={{0,2},{1,3},{2,0},{3,1},{4,6},{5,7},{6,4},{7,5},{8,10},{9,11},{10,... | collective-permute-start | bytes 368648 | tf_op jit(solution)/shard_map/ppermute | solution.py:37
  115.1 11.8 %collective-permute-start.27 = (bf16[160,1536]{1,0:T(8,128)(2,1)S(1)}, bf16[160,1536]{1,0:T(8,128)(2,1)S(1)}, u32[]{:S(2)}, u32[]{:S(2)}) collective-permute-start(bf16[160,1536]{1,0:T(8,128)(2,1)S(1)} %maximum_bitcast_fusion.refs_0_), channel_id=1, source_target_pairs={{0,8},{8,0},{16,24},{24,16},{1,9},{9,1},{17,25},{25,17},{2,10},{10... | collective-permute-start | bytes 1474568 | tf_op jit(solution)/shard_map/ppermute | solution.py:27
  115.6 17.5 %collective-permute-start.28 = (bf16[160,1536]{1,0:T(8,128)(2,1)S(1)}, bf16[160,1536]{1,0:T(8,128)(2,1)S(1)}, u32[]{:S(2)}, u32[]{:S(2)}) collective-permute-start(bf16[160,1536]{1,0:T(8,128)(2,1)S(1)} %maximum_bitcast_fusion.refs_0_), channel_id=1, source_target_pairs={{0,16},{8,24},{16,0},{24,8},{1,17},{9,25},{17,1},{25,9},{2,18},{10... | collective-permute-start | bytes 1474568 | tf_op jit(solution)/shard_map/ppermute | solution.py:27
  116.2 21.5 %collective-permute-start.29 = (bf16[160,1536]{1,0:T(8,128)(2,1)S(1)}, bf16[160,1536]{1,0:T(8,128)(2,1)S(1)}, u32[]{:S(2)}, u32[]{:S(2)}) collective-permute-start(bf16[160,1536]{1,0:T(8,128)(2,1)S(1)} %maximum_bitcast_fusion.refs_0_), channel_id=1, source_target_pairs={{0,24},{8,16},{16,8},{24,0},{1,25},{9,17},{17,9},{25,1},{2,26},{10... | collective-permute-start | bytes 1474568 | tf_op jit(solution)/shard_map/ppermute | solution.py:27
  137.7 10.8 %collective-permute-start.30 = (bf16[160,1536]{1,0:T(8,128)(2,1)}, bf16[160,1536]{1,0:T(8,128)(2,1)S(1)}, u32[]{:S(2)}, u32[]{:S(2)}) collective-permute-start(bf16[160,1536]{1,0:T(8,128)(2,1)} %get-tuple-element.246), channel_id=1, source_target_pairs={{0,8},{8,0},{16,24},{24,16},{1,9},{9,1},{17,25},{25,17},{2,10},{10... | collective-permute-start | bytes 1474568 | tf_op jit(solution)/shard_map/ppermute | solution.py:27
  144.0 21.1 %collective-permute-start.31 = (bf16[160,1536]{1,0:T(8,128)(2,1)}, bf16[160,1536]{1,0:T(8,128)(2,1)S(1)}, u32[]{:S(2)}, u32[]{:S(2)}) collective-permute-start(bf16[160,1536]{1,0:T(8,128)(2,1)} %get-tuple-element.249), channel_id=1, source_target_pairs={{0,16},{8,24},{16,0},{24,8},{1,17},{9,25},{17,1},{25,9},{2,18},{10... | collective-permute-start | bytes 1474568 | tf_op jit(solution)/shard_map/ppermute | solution.py:27
  144.9 20.3 %collective-permute-start.32 = (bf16[160,1536]{1,0:T(8,128)(2,1)}, bf16[160,1536]{1,0:T(8,128)(2,1)S(1)}, u32[]{:S(2)}, u32[]{:S(2)}) collective-permute-start(bf16[160,1536]{1,0:T(8,128)(2,1)} %get-tuple-element.250), channel_id=1, source_target_pairs={{0,24},{8,16},{16,8},{24,0},{1,25},{9,17},{17,9},{25,1},{2,26},{10... | collective-permute-start | bytes 1474568 | tf_op jit(solution)/shard_map/ppermute | solution.py:27
  169.1 4.7 %collective-permute-start.35 = (bf16[40,1536]{1,0:T(8,128)(2,1)}, bf16[40,1536]{1,0:T(8,128)(2,1)S(1)}, u32[]{:S(2)}, u32[]{:S(2)}) collective-permute-start(bf16[40,1536]{1,0:T(8,128)(2,1)} %get-tuple-element.258), channel_id=1, source_target_pairs={{0,6},{1,7},{2,4},{3,5},{4,2},{5,3},{6,0},{7,1},{8,14},{9,15},{10,... | collective-permute-start | bytes 368648 | tf_op jit(solution)/shard_map/ppermute | solution.py:37
  169.7 12.1 %collective-permute-start.34 = (bf16[40,1536]{1,0:T(8,128)(2,1)}, bf16[40,1536]{1,0:T(8,128)(2,1)S(1)}, u32[]{:S(2)}, u32[]{:S(2)}) collective-permute-start(bf16[40,1536]{1,0:T(8,128)(2,1)} %get-tuple-element.257), channel_id=1, source_target_pairs={{0,4},{1,5},{2,6},{3,7},{4,0},{5,1},{6,2},{7,3},{8,12},{9,13},{10,... | collective-permute-start | bytes 368648 | tf_op jit(solution)/shard_map/ppermute | solution.py:37
  173.8 8.1 %collective-permute-start.33 = (bf16[40,1536]{1,0:T(8,128)(2,1)}, bf16[40,1536]{1,0:T(8,128)(2,1)S(1)}, u32[]{:S(2)}, u32[]{:S(2)}) collective-permute-start(bf16[40,1536]{1,0:T(8,128)(2,1)} %get-tuple-element.256), channel_id=1, source_target_pairs={{0,2},{1,3},{2,0},{3,1},{4,6},{5,7},{6,4},{7,5},{8,10},{9,11},{10,... | collective-permute-start | bytes 368648 | tf_op jit(solution)/shard_map/ppermute | solution.py:37
  183.4 3.1 collective-permute-start.36
  209.0 11.3 %collective-permute-start.40 = (bf16[4,1024,384]{2,1,0:T(8,128)(2,1)}, bf16[4,1024,384]{2,1,0:T(8,128)(2,1)S(1)}, u32[]{:S(2)}, u32[]{:S(2)}) collective-permute-start(bf16[4,1024,384]{2,1,0:T(8,128)(2,1)} %get-tuple-element.265), channel_id=1, source_target_pairs={{0,1},{1,0},{2,3},{3,2},{4,5},{5,4},{6,7},{7,6},{8,9},{9,8},{10,11... | collective-permute-start | bytes 9437192 | tf_op jit(solution)/shard_map/ppermute | solution.py:32
  210.1 4.9 %collective-permute-start.37 = (bf16[128,192]{1,0:T(8,128)(2,1)S(1)}, bf16[128,192]{1,0:T(8,128)(2,1)S(1)}, u32[]{:S(2)}, u32[]{:S(2)}) collective-permute-start(bf16[128,192]{1,0:T(8,128)(2,1)S(1)} %get-tuple-element.382), channel_id=1, source_target_pairs={{0,2},{1,3},{2,0},{3,1},{4,6},{5,7},{6,4},{7,5},{8,10},{9,11},{10,... | collective-permute-start | bytes 147464 | tf_op jit(solution)/shard_map/ppermute | solution.py:37
  212.7 4.1 %collective-permute-start.38 = (bf16[128,192]{1,0:T(8,128)(2,1)S(1)}, bf16[128,192]{1,0:T(8,128)(2,1)S(1)}, u32[]{:S(2)}, u32[]{:S(2)}) collective-permute-start(bf16[128,192]{1,0:T(8,128)(2,1)S(1)} %get-tuple-element.381), channel_id=1, source_target_pairs={{0,4},{1,5},{2,6},{3,7},{4,0},{5,1},{6,2},{7,3},{8,12},{9,13},{10,... | collective-permute-start | bytes 147464 | tf_op jit(solution)/shard_map/ppermute | solution.py:37
  213.2 7.0 %collective-permute-start.39 = (bf16[128,192]{1,0:T(8,128)(2,1)S(1)}, bf16[128,192]{1,0:T(8,128)(2,1)S(1)}, u32[]{:S(2)}, u32[]{:S(2)}) collective-permute-start(bf16[128,192]{1,0:T(8,128)(2,1)S(1)} %get-tuple-element.380), channel_id=1, source_target_pairs={{0,6},{1,7},{2,4},{3,5},{4,2},{5,3},{6,0},{7,1},{8,14},{9,15},{10,... | collective-permute-start | bytes 147464 | tf_op jit(solution)/shard_map/ppermute | solution.py:37
  223.5 15.3 %collective-permute-start.41 = (bf16[512,384]{1,0:T(8,128)(2,1)S(1)}, bf16[512,384]{1,0:T(8,128)(2,1)}, u32[]{:S(2)}, u32[]{:S(2)}) collective-permute-start(bf16[512,384]{1,0:T(8,128)(2,1)S(1)} %get-tuple-element.279), channel_id=1, source_target_pairs={{0,8},{8,0},{16,24},{24,16},{1,9},{9,1},{17,25},{25,17},{2,10},{10... | collective-permute-start | bytes 1179656 | tf_op jit(solution)/shard_map/ppermute | solution.py:27
  224.3 14.5 %collective-permute-start.42 = (bf16[512,384]{1,0:T(8,128)(2,1)S(1)}, bf16[512,384]{1,0:T(8,128)(2,1)}, u32[]{:S(2)}, u32[]{:S(2)}) collective-permute-start(bf16[512,384]{1,0:T(8,128)(2,1)S(1)} %get-tuple-element.280), channel_id=1, source_target_pairs={{0,16},{8,24},{16,0},{24,8},{1,17},{9,25},{17,1},{25,9},{2,18},{10... | collective-permute-start | bytes 1179656 | tf_op jit(solution)/shard_map/ppermute | solution.py:27
  225.6 17.0 %collective-permute-start.43 = (bf16[512,384]{1,0:T(8,128)(2,1)S(1)}, bf16[512,384]{1,0:T(8,128)(2,1)}, u32[]{:S(2)}, u32[]{:S(2)}) collective-permute-start(bf16[512,384]{1,0:T(8,128)(2,1)S(1)} %get-tuple-element.281), channel_id=1, source_target_pairs={{0,24},{8,16},{16,8},{24,0},{1,25},{9,17},{17,9},{25,1},{2,26},{10... | collective-permute-start | bytes 1179656 | tf_op jit(solution)/shard_map/ppermute | solution.py:27
  242.7 5.8 %collective-permute-start.44 = (bf16[512,384]{1,0:T(8,128)(2,1)}, bf16[512,384]{1,0:T(8,128)(2,1)}, u32[]{:S(2)}, u32[]{:S(2)}) collective-permute-start(bf16[512,384]{1,0:T(8,128)(2,1)} %get-tuple-element.284), channel_id=1, source_target_pairs={{0,1},{1,0},{2,3},{3,2},{4,5},{5,4},{6,7},{7,6},{8,9},{9,8},{10,11... | collective-permute-start | bytes 1179656 | tf_op jit(solution)/shard_map/ppermute | solution.py:32
  245.9 11.1 %collective-permute-start.46 = (bf16[512,384]{1,0:T(8,128)(2,1)}, bf16[512,384]{1,0:T(8,128)(2,1)S(1)}, u32[]{:S(2)}, u32[]{:S(2)}) collective-permute-start(bf16[512,384]{1,0:T(8,128)(2,1)} %get-tuple-element.368), channel_id=1, source_target_pairs={{0,8},{8,0},{16,24},{24,16},{1,9},{9,1},{17,25},{25,17},{2,10},{10... | collective-permute-start | bytes 1179656 | tf_op jit(solution)/shard_map/ppermute | solution.py:27
  246.7 10.7 %collective-permute-start.47 = (bf16[512,384]{1,0:T(8,128)(2,1)}, bf16[512,384]{1,0:T(8,128)(2,1)}, u32[]{:S(2)}, u32[]{:S(2)}) collective-permute-start(bf16[512,384]{1,0:T(8,128)(2,1)} %get-tuple-element.367), channel_id=1, source_target_pairs={{0,16},{8,24},{16,0},{24,8},{1,17},{9,25},{17,1},{25,9},{2,18},{10... | collective-permute-start | bytes 1179656 | tf_op jit(solution)/shard_map/ppermute | solution.py:27
  247.6 18.6 %collective-permute-start.48 = (bf16[512,384]{1,0:T(8,128)(2,1)S(1)}, bf16[512,384]{1,0:T(8,128)(2,1)}, u32[]{:S(2)}, u32[]{:S(2)}) collective-permute-start(bf16[512,384]{1,0:T(8,128)(2,1)S(1)} %get-tuple-element.366), channel_id=1, source_target_pairs={{0,24},{8,16},{16,8},{24,0},{1,25},{9,17},{17,9},{25,1},{2,26},{10... | collective-permute-start | bytes 1179656 | tf_op jit(solution)/shard_map/ppermute | solution.py:27
  253.2 13.0 %collective-permute-start.45 = (bf16[4,96,576]{2,1,0:T(8,128)(2,1)}, bf16[4,96,576]{2,1,0:T(8,128)(2,1)}, u32[]{:S(2)}, u32[]{:S(2)}) collective-permute-start(bf16[4,96,576]{2,1,0:T(8,128)(2,1)} %get-tuple-element.286), channel_id=1, source_target_pairs={{0,1},{1,0},{2,3},{3,2},{4,5},{5,4},{6,7},{7,6},{8,9},{9,8},{10,11... | collective-permute-start | bytes 1327112 | tf_op jit(solution)/shard_map/ppermute | solution.py:32
  254.3 11.9 %collective-permute-start.49 = (bf16[128,768]{1,0:T(8,128)(2,1)}, bf16[128,768]{1,0:T(8,128)(2,1)S(1)}, u32[]{:S(2)}, u32[]{:S(2)}) collective-permute-start(bf16[128,768]{1,0:T(8,128)(2,1)} %get-tuple-element.290), channel_id=1, source_target_pairs={{0,2},{1,3},{2,0},{3,1},{4,6},{5,7},{6,4},{7,5},{8,10},{9,11},{10,... | collective-permute-start | bytes 589832 | tf_op jit(solution)/shard_map/ppermute | solution.py:37
  256.9 19.3 %collective-permute-start.53 = (bf16[128,768]{1,0:T(8,128)(2,1)}, bf16[128,768]{1,0:T(8,128)(2,1)S(1)}, u32[]{:S(2)}, u32[]{:S(2)}) collective-permute-start(bf16[128,768]{1,0:T(8,128)(2,1)} %get-tuple-element.312), channel_id=1, source_target_pairs={{0,4},{1,5},{2,6},{3,7},{4,0},{5,1},{6,2},{7,3},{8,12},{9,13},{10,... | collective-permute-start | bytes 589832 | tf_op jit(solution)/shard_map/ppermute | solution.py:37
  257.5 18.8 %collective-permute-start.54 = (bf16[128,768]{1,0:T(8,128)(2,1)}, bf16[128,768]{1,0:T(8,128)(2,1)S(1)}, u32[]{:S(2)}, u32[]{:S(2)}) collective-permute-start(bf16[128,768]{1,0:T(8,128)(2,1)} %get-tuple-element.313), channel_id=1, source_target_pairs={{0,6},{1,7},{2,4},{3,5},{4,2},{5,3},{6,0},{7,1},{8,14},{9,15},{10,... | collective-permute-start | bytes 589832 | tf_op jit(solution)/shard_map/ppermute | solution.py:37
  273.0 5.2 %collective-permute-start.50 = (bf16[112,576]{1,0:T(8,128)(2,1)}, bf16[112,576]{1,0:T(8,128)(2,1)S(1)}, u32[]{:S(2)}, u32[]{:S(2)}) collective-permute-start(bf16[112,576]{1,0:T(8,128)(2,1)} %get-tuple-element.307), channel_id=1, source_target_pairs={{0,8},{8,0},{16,24},{24,16},{1,9},{9,1},{17,25},{25,17},{2,10},{10... | collective-permute-start | bytes 387080 | tf_op jit(solution)/shard_map/ppermute | solution.py:27
  274.2 10.4 %collective-permute-start.51 = (bf16[112,576]{1,0:T(8,128)(2,1)}, bf16[112,576]{1,0:T(8,128)(2,1)S(1)}, u32[]{:S(2)}, u32[]{:S(2)}) collective-permute-start(bf16[112,576]{1,0:T(8,128)(2,1)} %get-tuple-element.308), channel_id=1, source_target_pairs={{0,16},{8,24},{16,0},{24,8},{1,17},{9,25},{17,1},{25,9},{2,18},{10... | collective-permute-start | bytes 387080 | tf_op jit(solution)/shard_map/ppermute | solution.py:27
  274.8 9.8 %collective-permute-start.52 = (bf16[112,576]{1,0:T(8,128)(2,1)}, bf16[112,576]{1,0:T(8,128)(2,1)S(1)}, u32[]{:S(2)}, u32[]{:S(2)}) collective-permute-start(bf16[112,576]{1,0:T(8,128)(2,1)} %get-tuple-element.309), channel_id=1, source_target_pairs={{0,24},{8,16},{16,8},{24,0},{1,25},{9,17},{17,9},{25,1},{2,26},{10... | collective-permute-start | bytes 387080 | tf_op jit(solution)/shard_map/ppermute | solution.py:27
  276.2 8.4 %collective-permute-start.55 = (bf16[256,384]{1,0:T(8,128)(2,1)S(1)}, bf16[256,384]{1,0:T(8,128)(2,1)S(1)}, u32[]{:S(2)}, u32[]{:S(2)}) collective-permute-start(bf16[256,384]{1,0:T(8,128)(2,1)S(1)} %copy-done.53), channel_id=1, source_target_pairs={{0,2},{1,3},{2,0},{3,1},{4,6},{5,7},{6,4},{7,5},{8,10},{9,11},{10,... | collective-permute-start | bytes 589832 | tf_op jit(solution)/shard_map/ppermute | solution.py:37
  276.2 9.1 %collective-permute-start.56 = (bf16[256,384]{1,0:T(8,128)(2,1)S(1)}, bf16[256,384]{1,0:T(8,128)(2,1)S(1)}, u32[]{:S(2)}, u32[]{:S(2)}) collective-permute-start(bf16[256,384]{1,0:T(8,128)(2,1)S(1)} %copy-done.52), channel_id=1, source_target_pairs={{0,4},{1,5},{2,6},{3,7},{4,0},{5,1},{6,2},{7,3},{8,12},{9,13},{10,... | collective-permute-start | bytes 589832 | tf_op jit(solution)/shard_map/ppermute | solution.py:37
  278.3 16.7 %collective-permute-start.57 = (bf16[256,384]{1,0:T(8,128)(2,1)S(1)}, bf16[256,384]{1,0:T(8,128)(2,1)S(1)}, u32[]{:S(2)}, u32[]{:S(2)}) collective-permute-start(bf16[256,384]{1,0:T(8,128)(2,1)S(1)} %copy-done.51), channel_id=1, source_target_pairs={{0,6},{1,7},{2,4},{3,5},{4,2},{5,3},{6,0},{7,1},{8,14},{9,15},{10,... | collective-permute-start | bytes 589832 | tf_op jit(solution)/shard_map/ppermute | solution.py:37
  295.1 5.2 %collective-permute-start.61 = (bf16[112,576]{1,0:T(8,128)(2,1)S(1)}, bf16[112,576]{1,0:T(8,128)(2,1)S(1)}, u32[]{:S(2)}, u32[]{:S(2)}) collective-permute-start(bf16[112,576]{1,0:T(8,128)(2,1)S(1)} %add_convert_fusion.10.refs_0_), channel_id=1, source_target_pairs={{0,2},{1,3},{2,0},{3,1},{4,6},{5,7},{6,4},{7,5},{8,10},{9,11},{10,... | collective-permute-start | bytes 387080 | tf_op jit(solution)/shard_map/ppermute | solution.py:37
  295.1 7.3 %collective-permute-start.62 = (bf16[112,576]{1,0:T(8,128)(2,1)S(1)}, bf16[112,576]{1,0:T(8,128)(2,1)S(1)}, u32[]{:S(2)}, u32[]{:S(2)}) collective-permute-start(bf16[112,576]{1,0:T(8,128)(2,1)S(1)} %add_convert_fusion.10.refs_0_), channel_id=1, source_target_pairs={{0,4},{1,5},{2,6},{3,7},{4,0},{5,1},{6,2},{7,3},{8,12},{9,13},{10,... | collective-permute-start | bytes 387080 | tf_op jit(solution)/shard_map/ppermute | solution.py:37
  297.4 13.1 %collective-permute-start.63 = (bf16[112,576]{1,0:T(8,128)(2,1)S(1)}, bf16[112,576]{1,0:T(8,128)(2,1)S(1)}, u32[]{:S(2)}, u32[]{:S(2)}) collective-permute-start(bf16[112,576]{1,0:T(8,128)(2,1)S(1)} %add_convert_fusion.10.refs_0_), channel_id=1, source_target_pairs={{0,6},{1,7},{2,4},{3,5},{4,2},{5,3},{6,0},{7,1},{8,14},{9,15},{10,... | collective-permute-start | bytes 387080 | tf_op jit(solution)/shard_map/ppermute | solution.py:37
  297.9 32.2 %collective-permute-start.58 = (bf16[256,384]{1,0:T(8,128)(2,1)S(1)}, bf16[256,384]{1,0:T(8,128)(2,1)S(1)}, u32[]{:S(2)}, u32[]{:S(2)}) collective-permute-start(bf16[256,384]{1,0:T(8,128)(2,1)S(1)} %add_convert_fusion.8.refs_0_), channel_id=1, source_target_pairs={{0,2},{1,3},{2,0},{3,1},{4,6},{5,7},{6,4},{7,5},{8,10},{9,11},{10,... | collective-permute-start | bytes 589832 | tf_op jit(solution)/shard_map/ppermute | solution.py:37
  298.9 31.1 %collective-permute-start.59 = (bf16[256,384]{1,0:T(8,128)(2,1)S(1)}, bf16[256,384]{1,0:T(8,128)(2,1)S(1)}, u32[]{:S(2)}, u32[]{:S(2)}) collective-permute-start(bf16[256,384]{1,0:T(8,128)(2,1)S(1)} %add_convert_fusion.8.refs_0_), channel_id=1, source_target_pairs={{0,4},{1,5},{2,6},{3,7},{4,0},{5,1},{6,2},{7,3},{8,12},{9,13},{10,... | collective-permute-start | bytes 589832 | tf_op jit(solution)/shard_map/ppermute | solution.py:37
  300.3 29.8 %collective-permute-start.60 = (bf16[256,384]{1,0:T(8,128)(2,1)S(1)}, bf16[256,384]{1,0:T(8,128)(2,1)S(1)}, u32[]{:S(2)}, u32[]{:S(2)}) collective-permute-start(bf16[256,384]{1,0:T(8,128)(2,1)S(1)} %add_convert_fusion.8.refs_0_), channel_id=1, source_target_pairs={{0,6},{1,7},{2,4},{3,5},{4,2},{5,3},{6,0},{7,1},{8,14},{9,15},{10,... | collective-permute-start | bytes 589832 | tf_op jit(solution)/shard_map/ppermute | solution.py:37
  313.2 13.1 %collective-permute-start.64 = (bf16[4,112,576]{2,1,0:T(8,128)(2,1)}, bf16[4,112,576]{2,1,0:T(8,128)(2,1)S(1)}, u32[]{:S(2)}, u32[]{:S(2)}) collective-permute-start(bf16[4,112,576]{2,1,0:T(8,128)(2,1)} %collect.1.mine_ref), channel_id=1, source_target_pairs={{0,1},{1,0},{2,3},{3,2},{4,5},{5,4},{6,7},{7,6},{8,9},{9,8},{10,11... | collective-permute-start | bytes 1548296 | tf_op jit(solution)/shard_map/ppermute | solution.py:32
  (69 other events, 450.9 us)
